TPU v7x, 32 devices: a whole 2x2x4 slice. The times are simulated.
32 devices in a mesh: groups: 2 (over x), row: 8 (over z, y), col: 2 (over core).
Axes of the slice: x: 2, y: 2, z: 4, core: 2. Of those that a mesh axis runs over, the one named last changes fastest.
Arguments:
- users: bfloat16 [32768, 128], P(('groups', 'row', 'col')), parts along dimension 0, may hold values from -1.796875 to 1.796875
- items: bfloat16 [16384, 128], P(('groups', 'row', 'col')), parts along dimension 0, may hold values from -1.796875 to 1.796875
- ratings: bfloat16 [16, 2, 192, 128, 128], P(('groups', 'row'), 'col'), parts along dimension 0, may hold values from -6 to 6
- observed: int32 [16, 2, 192, 16, 128], P(('groups', 'row'), 'col'), parts along dimension 0, may hold values from 0 to 255
- tile_rows: int32 [16, 2, 192], P(('groups', 'row'), 'col'), parts along dimension 0, may hold values from 0 to 15
- tile_cols: int32 [16, 2, 192], P(('groups', 'row'), 'col'), parts along dimension 0, may hold values from 0 to 31
- tile_count: int32 [16, 2], P(('groups', 'row'), 'col'), parts along dimension 0, may hold values from 48 to 192, as said below
Outputs:
- users_new: bfloat16 [32768, 128], P(('groups', 'row', 'col')), parts along dimension 0
- items_new: bfloat16 [16384, 128], P(('groups', 'row', 'col')), parts along dimension 0
There are 2 independent parts, one for each index of `groups`. A program takes and returns all parts, laid end to end along the dimension named above; each array names one. Nothing has to cross between parts.
Inputs may be any that keep to these rules, and one draw needn't show every extreme that they name: `tile_count`: slots at or after a device's count are ignored; some device's count is 192. `tile_rows`: user tile within the device's row block. `tile_cols`: item tile within the device's column block. `observed`: bit b of word w, column j: user 8 w + b of the tile rated item j.
All inputs are finite; a program needn't handle non-finite values.
Results may differ from a plain program's by a relative error of at most 0.014.
Values may be sent and summed in bfloat16 or wider, within the bound.
No kernel may reach another device: no remote copies, remote signals or barrier semaphores. Data moves between devices by JAX's collectives and lax.ppermute only.
A program may use at most 128 MiB of HBM per device.

v0:
```python
import jax
import jax.numpy as jnp
from jax import lax
from jax.sharding import PartitionSpec as P


def unpack_mask(words):
    offsets = jnp.arange(8, dtype=jnp.int32)
    planes = jnp.right_shift(words[..., :, None, :], offsets[:, None]) & 1
    target_shape = words.shape[:-2] + (words.shape[-2] * 8, words.shape[-1])
    return planes.reshape(target_shape)


def update_factor(factor, gradient, rate):
    values = factor.astype(jnp.float32)
    return (values - rate * (gradient + 0.05 * values)).astype(jnp.bfloat16)


def tile_residual(user_tiles, item_tiles, tiles, weights):
    predicted = jnp.einsum(
        "tbk,tck->tbc", user_tiles, item_tiles, preferred_element_type=jnp.float32
    )
    return (weights * (predicted - tiles.astype(jnp.float32))).astype(jnp.bfloat16)


def selector_of(indices, count, dtype):
    return (indices[:, None] == jnp.arange(count, dtype=jnp.int32)[None, :]).astype(dtype)


def pick_tiles(indices, panel_tiles):
    selector = selector_of(indices, panel_tiles.shape[0], jnp.bfloat16)
    picked = jnp.einsum("tv,vbk->tbk", selector, panel_tiles, preferred_element_type=jnp.float32)
    return picked.astype(jnp.bfloat16)


def segment_total(indices, count, grads):
    selector = selector_of(indices, count, jnp.float32)
    summed = jnp.einsum("tv,tbk->vbk", selector, grads, precision=lax.Precision.HIGHEST)
    return summed.reshape(-1, grads.shape[-1])


def body(users, items, ratings, observed, tile_rows, tile_cols, tile_count):
    tiles = ratings[0, 0]
    slot_rows = tile_rows[0, 0]
    slot_cols = tile_cols[0, 0]
    block = tiles.shape[-1]
    rank = users.shape[-1]
    slots = tiles.shape[0]
    live = jnp.arange(slots, dtype=jnp.int32) < tile_count[0, 0]
    weights = jnp.where(live[:, None, None], unpack_mask(observed[0, 0]), 0).astype(jnp.bfloat16)
    item_panel = lax.all_gather(items, "row", axis=0, tiled=True)
    item_count = item_panel.shape[0] // block
    item_tiles = pick_tiles(slot_cols, item_panel.reshape(item_count, block, rank))
    user_panel = lax.all_gather(users, "col", axis=0, tiled=True)
    user_count = user_panel.shape[0] // block
    user_tiles = pick_tiles(slot_rows, user_panel.reshape(user_count, block, rank))
    residual = tile_residual(user_tiles, item_tiles, tiles, weights)
    user_terms = jnp.einsum(
        "tbc,tck->tbk", residual, item_tiles, preferred_element_type=jnp.float32
    )
    user_partial = segment_total(slot_rows, user_count, user_terms)
    user_grad = lax.psum_scatter(
        user_partial.astype(jnp.bfloat16), "col", scatter_dimension=0, tiled=True
    ).astype(jnp.float32)
    users_new = update_factor(users, user_grad, 0.02)
    fresh_panel = lax.all_gather(users_new, "col", axis=0, tiled=True)
    fresh_tiles = pick_tiles(slot_rows, fresh_panel.reshape(user_count, block, rank))
    residual_two = tile_residual(fresh_tiles, item_tiles, tiles, weights)
    item_terms = jnp.einsum(
        "tbc,tbk->tck", residual_two, fresh_tiles, preferred_element_type=jnp.float32
    )
    item_partial = segment_total(slot_cols, item_count, item_terms)
    item_grad = lax.psum_scatter(item_partial, "row", scatter_dimension=0, tiled=True)
    items_new = update_factor(items, item_grad, 0.005)
    return (users_new, items_new)


def solution(mesh):
    return jax.shard_map(
        body,
        mesh=mesh,
        in_specs=(
            P(("groups", "row", "col"), None),
            P(("groups", "row", "col"), None),
            P(("groups", "row"), "col", None, None, None),
            P(("groups", "row"), "col", None, None, None),
            P(("groups", "row"), "col", None),
            P(("groups", "row"), "col", None),
            P(("groups", "row"), "col"),
        ),
        out_specs=(P(("groups", "row", "col"), None), P(("groups", "row", "col"), None)),
        check_vma=False,
    )
```

profile of v0, /device:TPU:0, one launch (start us, length us, event | category | flops | bytes accessed | tf_op | source)
XLA Modules:
  0.0 247.4 jit_solution(17324312887068468634)
XLA Ops:
  7.2 0.0 copy-start.4
  7.2 0.0 all-gather.2.cloned.1.call-start
  7.2 0.7 all-gather.2.cloned.1.call-update
  7.9 0.0 reduce-scatter.3.cloned.1.call-start
  8.6 0.1 shift_right_arithmetic.26
  8.7 2.5 all_gather.9
  11.2 0.0 copy-start.5
  11.2 5.2 %fusion.51 = bf16[192,128,128]{2,0,1:T(8,128)(2,1)} fusion(bf16[16,128,128]{2,1,0:T(8,128)(2,1)S(1)} %bitcast.44, s32[192]{0:T(256)} %bitcast.48), kind=kOutput, calls=%fused_computation.45 | convolution fusion | flops 100666368 | bytes 6816512 | tf_op jit(solution)/shard_map/tv,vbk->tbk/dot_general | solution.py:32
  16.4 36.6 %all-gather.2.cloned.1.call-done = bf16[4096,128]{1,0:T(8,128)(2,1)} async-done(((bf16[512,128]{1,0:T(8,128)(2,1)}), bf16[4096,128]{1,0:T(8,128)(2,1)}) %all-gather.2.cloned.1.call-update) | async-done | bytes 1048592 | tf_op jit(solution)/shard_map/all_gather | solution.py:51
  53.0 0.0 copy-done.4
  53.0 5.7 %convolution_convert_fusion = bf16[192,128,128]{2,0,1:T(8,128)(2,1)} fusion(bf16[32,128,128]{2,1,0:T(8,128)(2,1)} %bitcast.47, s32[192]{0:T(256)S(1)} %bitcast.51), kind=kOutput, calls=%fused_computation.36 | convolution fusion | flops 204478464 | bytes 7340800 | tf_op jit(solution)/shard_map/tv,vbk->tbk/dot_general | solution.py:32
  58.7 0.0 copy-done.5
  58.7 0.0 copy-start.3
  58.7 31.4 %fusion.12 = f32[192,128,128]{2,1,0:T(8,128)} fusion(bf16[1,1,192,128,128]{4,3,2,1,0:T(8,128)(2,1)} %param.9, s32[128]{0:T(128)S(1)} %shift_right_arithmetic.26, s32[192,16,128]{2,1,0:T(8,128)S(1)} %bitcast.53, pred[192]{0:T(512)(128)(4,1)S(1)} %iota_compare_fusion.2, bf16[192,128,128]{2,0,1:T(8,128)(2,1)} %convolution_convert_fusion, ...), kind=kOutput, calls=%fused_computation.17 | convolution fusion | flops 1638924288 | bytes 33030848 | tf_op jit(solution)/shard_map/tbc,tck->tbk/dot_general | solution.py:58
  90.1 0.0 copy-done.3
  90.1 0.0 copy-start
  90.1 15.4 %fusion.44 = bf16[16,128,128]{2,0,1:T(8,128)(2,1)S(1)} fusion(f32[192,128,128]{2,1,0:T(8,128)} %fusion.12, s32[192]{0:T(256)S(1)} %bitcast.49), kind=kOutput, calls=%fused_computation.38 | convolution fusion | flops 604244992 | bytes 13107968 | tf_op jit(solution)/shard_map/tv,tbk->vbk/dot_general | solution.py:38
  105.5 0.9 copy.10
  106.5 0.0 reduce-scatter.3.cloned.1.call-update
  106.5 0.0 reduce-scatter.5.cloned.1.call-start
  106.6 6.8 %reduce-scatter.3.cloned.1.call-done = bf16[1024,128]{1,0:T(8,128)(2,1)} async-done(((bf16[2048,128]{1,0:T(8,128)(2,1)}), bf16[1024,128]{1,0:T(8,128)(2,1)}) %reduce-scatter.3.cloned.1.call-update) | async-done | bytes 262160 | tf_op jit(solution)/shard_map/reduce_scatter | solution.py:62
  113.3 0.0 copy-done
  113.3 1.1 fusion.50
  114.4 0.0 copy-start.1
  114.4 2.2 all_gather.11
  116.6 4.4 %convolution_convert_fusion.1 = bf16[192,128,128]{2,0,1:T(8,128)(2,1)} fusion(bf16[16,128,128]{2,1,0:T(8,128)(2,1)S(1)} %bitcast.45, s32[192]{0:T(256)S(1)} %bitcast.50), kind=kOutput, calls=%fused_computation.37 | convolution fusion | flops 103812096 | bytes 6816512 | tf_op jit(solution)/shard_map/tv,vbk->tbk/dot_general | solution.py:32
  121.1 30.5 %fusion.10 = f32[192,128,128]{2,1,0:T(8,128)} fusion(bf16[1,1,192,128,128]{4,3,2,1,0:T(8,128)(2,1)} %param.9, s32[128]{0:T(128)S(1)} %shift_right_arithmetic.26, s32[192,16,128]{2,1,0:T(8,128)S(1)} %bitcast.54, pred[192]{0:T(512)(128)(4,1)S(1)} %iota_compare_fusion.2, bf16[192,128,128]{2,0,1:T(8,128)(2,1)} %convolution_convert_fusion.1, ...), kind=kOutput, calls=%fused_computation.16 | convolution fusion | flops 1638924288 | bytes 33030848 | tf_op jit(solution)/shard_map/tbc,tbk->tck/dot_general | solution.py:69
  151.6 0.0 copy-done.1
  151.6 15.7 %fusion.5 = f32[32,128,128]{2,0,1:T(8,128)S(1)} fusion(f32[192,128,128]{2,1,0:T(8,128)} %fusion.10, s32[192]{0:T(256)S(1)} %bitcast.52), kind=kOutput, calls=%fused_computation.10 | convolution fusion | flops 1207965696 | bytes 14680832 | tf_op jit(solution)/shard_map/tv,tbk->vbk/dot_general | solution.py:38
  167.3 0.0 copy-start.2
  167.3 2.6 %copy.12 = f32[32,128,128]{2,1,0:T(8,128)} copy(f32[32,128,128]{2,0,1:T(8,128)S(1)} %fusion.5) | data formatting | bytes 4194304 | tf_op jit(solution)/shard_map/tv,tbk->vbk/dot_general | solution.py:38
  169.9 0.0 reduce-scatter.5.cloned.1.call-update
  169.9 69.1 %reduce-scatter.5.cloned.1.call-done = f32[512,128]{1,0:T(8,128)} async-done(((f32[4096,128]{1,0:T(8,128)}), f32[512,128]{1,0:T(8,128)}) %reduce-scatter.5.cloned.1.call-update) | async-done | bytes 262160 | tf_op jit(solution)/shard_map/reduce_scatter | solution.py:73
  239.0 0.0 copy-done.2
  239.0 1.7 fusion.56
  (2 shorter events, 0.0 us)
Async XLA Ops:
  7.2 45.9 %copy-start.4 = (s32[1,1,192]{2,1,0:T(1,128)S(1)}, s32[1,1,192]{2,1,0:T(1,128)}, u32[]{:S(2)}) copy-start(s32[1,1,192]{2,1,0:T(1,128)} %param.12) | copy-start | bytes 2308
  7.2 45.8 %all-gather.2.cloned.1.call-start = ((), (), s32[]{:S(2)}) async-start(), calls=%async_computation.2 | async-start | bytes 1179648 | tf_op jit(solution)/shard_map/all_gather | solution.py:51
  7.9 105.4 %reduce-scatter.3.cloned.1.call-start = ((), (), s32[]{:S(2)}) async-start(), calls=%async_computation.3 | async-start | bytes 786432 | tf_op jit(solution)/shard_map/reduce_scatter | solution.py:62
  11.2 47.5 %copy-start.5 = (s32[1,1,192,16,128]{4,3,2,1,0:T(8,128)S(1)}, s32[1,1,192,16,128]{4,3,2,1,0:T(8,128)}, u32[]{:S(2)}) copy-start(s32[1,1,192,16,128]{4,3,2,1,0:T(8,128)} %param.10) | copy-start | bytes 4718596
  58.7 31.4 %copy-start.3 = (s32[1,1,192]{2,1,0:T(1,128)S(1)}, s32[1,1,192]{2,1,0:T(1,128)}, u32[]{:S(2)}) copy-start(s32[1,1,192]{2,1,0:T(1,128)} %param.11) | copy-start | bytes 2308
  90.1 23.3 %copy-start = (bf16[1024,128]{1,0:T(8,128)(2,1)S(1)}, bf16[1024,128]{1,0:T(8,128)(2,1)}, u32[]{:S(2)}) copy-start(bf16[1024,128]{1,0:T(8,128)(2,1)} %param.7) | copy-start | bytes 786436
  106.5 132.5 %reduce-scatter.5.cloned.1.call-start = ((), (), s32[]{:S(2)}) async-start(), calls=%async_computation.4 | async-start | bytes 2359296 | tf_op jit(solution)/shard_map/reduce_scatter | solution.py:73
  114.4 37.2 %copy-start.1 = (bf16[1024,128]{1,0:T(8,128)(2,1)}, bf16[1024,128]{1,0:T(8,128)(2,1)S(1)}, u32[]{:S(2)}) copy-start(bf16[1024,128]{1,0:T(8,128)(2,1)S(1)} %fusion.50) | copy-start | bytes 786436
  167.3 71.7 %copy-start.2 = (bf16[512,128]{1,0:T(8,128)(2,1)S(1)}, bf16[512,128]{1,0:T(8,128)(2,1)}, u32[]{:S(2)}) copy-start(bf16[512,128]{1,0:T(8,128)(2,1)} %param.8) | copy-start | bytes 393220
Sparse Core Ops, SparseCore 0:
  10.1 42.8 all-gather.1
  106.6 6.6 reduce-scatter.2
  170.0 68.9 reduce-scatter.4
where the time goes:
time: 251 us; the launch traced here: 247 us
  waiting for transfers between devices  113 us (45%)
  matrix products  108 us (43%)
  between operations  14.7 us (6%)
  blocking collectives  4.65 us (2%)
  local copies, waits for them, and re-layouts  3.61 us (1%)
  other arithmetic  2.74 us (1%)
    reduce_scatter x1, waiting for transfers between devices, body(): lax.psum_scatter(item_partial, 'row', scatter_dimension=0, tiled=True)  69.1 us
    all_gather x1, waiting for transfers between devices, body(): item_panel = lax.all_gather(items, 'row', axis=0, tiled=True)  36.6 us
    dot_general x1, matrix products, body(): jnp.einsum('tbc,tck->tbk', residual, item_tiles, preferred_element_type=j...  31.4 us
    dot_general x2, matrix products, segment_total(): jnp.einsum('tv,tbk->vbk', selector, grads, precision=lax.Precision.HIGHEST)  31.2 us
    dot_general x1, matrix products, body(): jnp.einsum('tbc,tbk->tck', residual_two, fresh_tiles, preferred_element_t...  30.5 us
    dot_general x3, matrix products, pick_tiles(): jnp.einsum('tv,vbk->tbk', selector, panel_tiles, preferred_element_type=j...  15.4 us
    reduce_scatter x1, waiting for transfers between devices, body(): lax.psum_scatter(user_partial.astype(jnp.bfloat16), 'col', scatter_dimens...  6.79 us
  transfers between devices with their start and end apart: 3, of which 3 were waited for; matrix products, arithmetic and copies ran while one was open for 2% of the time, Pallas kernels for 0%

commit v1 on v0

v1 whole, which is shorter than its diff:
```python
import functools

import jax
import jax.numpy as jnp
from jax import lax
from jax.experimental import pallas as pl
from jax.experimental.pallas import tpu as pltpu
from jax.sharding import PartitionSpec as P

BLOCK = 128
UNROLL = 4
VMEM_LIMIT = 48 * 1024 * 1024

NN = (((1,), (0,)), ((), ()))
NT = (((1,), (1,)), ((), ()))

vmem = functools.partial(pl.BlockSpec, memory_space=pltpu.VMEM)
smem = functools.partial(pl.BlockSpec, memory_space=pltpu.SMEM)
anywhere = functools.partial(pl.BlockSpec, memory_space=pl.ANY)


def params():
    return pltpu.CompilerParams(vmem_limit_bytes=VMEM_LIMIT)


def dot(a, b, dims):
    return lax.dot_general(a, b, dims, preferred_element_type=jnp.float32)


def rows_of(index):
    return pl.ds(pl.multiple_of(index * BLOCK, BLOCK), BLOCK)


def plan_kernel(
    slots, pad, shard_tiles, keys, info, rows, cols, ratings, observed,
    meta, tiles_out, words_out, place, sems,
):
    copy_tiles = pltpu.make_async_copy(ratings, tiles_out, sems.at[0])
    copy_words = pltpu.make_async_copy(observed, words_out, sems.at[1])
    copy_tiles.start()
    copy_words.start()
    count = info[0]
    me = info[1]

    def clear(k, _):
        place[k] = 0
        return _

    lax.fori_loop(0, keys + 1, clear, 0)

    def key_of(t):
        return jnp.bitwise_xor(cols[t] // shard_tiles, me) if keys > 1 else 0

    def tally(t, _):
        k = key_of(t)
        place[k + 1] = place[k + 1] + 1
        return _

    lax.fori_loop(0, count, tally, 0)

    def sums(k, total):
        total = total + place[k]
        place[k] = total
        meta[3 * pad + k] = total
        return total

    lax.fori_loop(0, keys + 1, sums, 0)

    def put(t, _):
        k = key_of(t)
        at = place[k]
        place[k] = at + 1
        meta[at] = t
        meta[pad + at] = rows[t]
        meta[2 * pad + at] = cols[t] % shard_tiles if keys > 1 else cols[t]
        return _

    lax.fori_loop(0, count, put, 0)

    def fill(at, _):
        meta[at] = 0
        meta[pad + at] = 0
        meta[2 * pad + at] = 0
        return _

    lax.fori_loop(count, pad, fill, 0)
    copy_tiles.wait()
    copy_words.wait()


def stage_loop(pad, key, meta, group):
    low = meta[3 * pad + key]
    high = meta[3 * pad + key + 1]

    def step(i, _):
        group([
            (meta[at], meta[pad + at], meta[2 * pad + at], at < high)
            for at in [low + i * UNROLL + j for j in range(UNROLL)]
        ])
        return _

    lax.fori_loop(0, (high - low + UNROLL - 1) // UNROLL, step, 0)


def masked_residual(predicted, tiles, words, slot, live):
    bit = jnp.left_shift(1, lax.broadcasted_iota(jnp.int32, (8, BLOCK), 0))
    bit = jnp.where(live, bit, 0)
    parts = []
    for w in range(BLOCK // 8):
        seen = jnp.broadcast_to(words[slot, pl.ds(w, 1), :], (8, BLOCK)) & bit
        gap = predicted[8 * w : 8 * w + 8] - tiles[slot, pl.ds(8 * w, 8), :].astype(jnp.float32)
        parts.append(jnp.where(seen != 0, gap, 0.0))
    return jnp.concatenate(parts, axis=0).astype(jnp.bfloat16)


def user_kernel(pad, key, last, meta, tiles, words, users, shard, *rest):
    if key:
        prior, total = rest[0], rest[1]
    else:
        total = rest[0]
        total[...] = jnp.zeros_like(total)
    flipped = rest[-1]
    for v in range(shard.shape[0] // BLOCK):
        flipped[v * BLOCK : (v + 1) * BLOCK] = shard[v * BLOCK : (v + 1) * BLOCK].T

    def group(entries):
        terms = []
        for slot, u, v, live in entries:
            predicted = dot(users[rows_of(u), :], flipped[rows_of(v), :], NN)
            residual = masked_residual(predicted, tiles, words, slot, live)
            terms.append(dot(residual, shard[rows_of(v), :], NN))
        for (slot, u, v, live), term in zip(entries, terms):
            total[rows_of(u), :] += term

    stage_loop(pad, key, meta, group)
    if last:
        rest[-2][...] = total[...].astype(jnp.bfloat16)


def fresh_kernel(mine, theirs, users, fresh, turned):
    for u in range(users.shape[0] // BLOCK):
        at = slice(u * BLOCK, (u + 1) * BLOCK)
        values = users[at].astype(jnp.float32)
        gradient = mine[at].astype(jnp.float32) + theirs[at].astype(jnp.float32)
        new = (values - 0.02 * (gradient + 0.05 * values)).astype(jnp.bfloat16)
        fresh[at] = new
        turned[at] = new.T


def item_kernel(pad, key, meta, tiles, words, fresh, turned, shard, out, total, flipped):
    total[...] = jnp.zeros_like(total)
    for v in range(shard.shape[0] // BLOCK):
        flipped[v * BLOCK : (v + 1) * BLOCK] = shard[v * BLOCK : (v + 1) * BLOCK].T

    def group(entries):
        terms = []
        for slot, u, v, live in entries:
            predicted = dot(fresh[rows_of(u), :], flipped[rows_of(v), :], NN)
            residual = masked_residual(predicted, tiles, words, slot, live)
            terms.append(dot(turned[rows_of(u), :], residual, NN))
        for (slot, u, v, live), term in zip(entries, terms):
            total[rows_of(v), :] += term

    stage_loop(pad, key, meta, group)
    for v in range(shard.shape[0] // BLOCK):
        at = slice(v * BLOCK, (v + 1) * BLOCK)
        out[at] = total[at].T.astype(out.dtype)


def body(n_row, n_col, users, items, ratings, observed, tile_rows, tile_cols, tile_count):
    tiles = ratings[0, 0]
    words = observed[0, 0]
    slots = tiles.shape[0]
    rank = users.shape[-1]
    pad = slots + 8
    shard_rows = items.shape[0]
    direct = shard_rows % BLOCK == 0 and n_row & (n_row - 1) == 0
    keys = n_row if direct else 1
    row_at = lax.axis_index("row")
    col_at = lax.axis_index("col")

    def swap_row(x, k):
        return lax.ppermute(x, "row", [(i, i ^ k) for i in range(n_row)])

    def swap_col(x):
        return lax.ppermute(x, "col", [(i, i ^ 1) for i in range(n_col)])

    peer_users = swap_col(users)
    if direct:
        shards = [items] + [swap_row(items, k) for k in range(1, n_row)]
    else:
        shards = [lax.all_gather(items, "row", axis=0, tiled=True)]
    wide = shards[0].shape[0]

    info = jnp.stack([tile_count[0, 0], row_at.astype(jnp.int32)])
    meta, tiles_in, words_in = pl.pallas_call(
        functools.partial(plan_kernel, slots, pad, wide // BLOCK, keys),
        out_shape=(
            jax.ShapeDtypeStruct((3 * pad + keys + 8,), jnp.int32),
            pltpu.VMEM(tiles.shape, tiles.dtype),
            pltpu.VMEM(words.shape, words.dtype),
        ),
        in_specs=[smem(), smem(), smem(), anywhere(), anywhere()],
        out_specs=(smem(), vmem(), vmem()),
        scratch_shapes=[pltpu.SMEM((keys + 1,), jnp.int32), pltpu.SemaphoreType.DMA((2,))],
        compiler_params=params(),
        name="plan",
    )(info, tile_rows[0, 0], tile_cols[0, 0], tiles, words)

    first = col_at == 0
    panel = jnp.concatenate(
        [jnp.where(first, users, peer_users), jnp.where(first, peer_users, users)], axis=0
    )
    cost = pl.CostEstimate(
        flops=4 * slots * BLOCK * BLOCK * rank // keys,
        bytes_accessed=(slots // keys) * BLOCK * BLOCK * 4,
        transcendentals=0,
    )
    total = None
    terms = None
    for key in range(keys):
        last = key == keys - 1
        shapes = [pltpu.VMEM(panel.shape, jnp.float32)]
        if last:
            shapes.append(jax.ShapeDtypeStruct(panel.shape, jnp.bfloat16))
        operands = [meta, tiles_in, words_in, panel, shards[key]] + ([total] if key else [])
        outs = pl.pallas_call(
            functools.partial(user_kernel, pad, key, last),
            out_shape=tuple(shapes),
            in_specs=[smem()] + [vmem()] * (len(operands) - 1),
            out_specs=tuple([vmem()] * len(shapes)),
            input_output_aliases={5: 0} if key else {},
            scratch_shapes=[pltpu.VMEM((wide, rank), jnp.bfloat16)],
            compiler_params=params(),
            cost_estimate=cost,
            name="user_terms",
        )(*operands)
        total = outs[0]
        terms = outs[-1]

    peer_terms = swap_col(terms)
    fresh, turned = pl.pallas_call(
        fresh_kernel,
        out_shape=(pltpu.VMEM(panel.shape, jnp.bfloat16), pltpu.VMEM(panel.shape, jnp.bfloat16)),
        in_specs=[vmem()] * 3,
        out_specs=(vmem(), vmem()),
        compiler_params=params(),
        name="fresh",
    )(terms, peer_terms, panel)
    users_new = lax.dynamic_slice_in_dim(fresh, col_at * users.shape[0], users.shape[0], 0)

    def item_terms(key, kind):
        return pl.pallas_call(
            functools.partial(item_kernel, pad, key),
            out_shape=jax.ShapeDtypeStruct((wide, rank), kind),
            in_specs=[smem()] + [vmem()] * 5,
            out_specs=vmem(),
            scratch_shapes=[
                pltpu.VMEM((wide, rank), jnp.float32),
                pltpu.VMEM((wide, rank), jnp.bfloat16),
            ],
            compiler_params=params(),
            cost_estimate=cost,
            name="item_terms",
        )(meta, tiles_in, words_in, fresh, turned, shards[key])

    if direct:
        arrived = [swap_row(item_terms(k, jnp.bfloat16), k) for k in range(n_row - 1, 0, -1)]
        item_grad = item_terms(0, jnp.float32)
        for part in arrived:
            item_grad = item_grad + part.astype(jnp.float32)
    else:
        item_grad = lax.psum_scatter(
            item_terms(0, jnp.float32), "row", scatter_dimension=0, tiled=True
        )
    values = items.astype(jnp.float32)
    items_new = (values - 0.005 * (item_grad + 0.05 * values)).astype(jnp.bfloat16)
    return (users_new, items_new)


def solution(mesh):
    return jax.shard_map(
        functools.partial(body, mesh.shape["row"], mesh.shape["col"]),
        mesh=mesh,
        in_specs=(
            P(("groups", "row", "col"), None),
            P(("groups", "row", "col"), None),
            P(("groups", "row"), "col", None, None, None),
            P(("groups", "row"), "col", None, None, None),
            P(("groups", "row"), "col", None),
            P(("groups", "row"), "col", None),
            P(("groups", "row"), "col"),
        ),
        out_specs=(P(("groups", "row", "col"), None), P(("groups", "row", "col"), None)),
        check_vma=False,
    )
```

time: 251 us -> 119 us (0.47)
  waiting for transfers between devices: 113 us -> 1.58 us
  matrix products: 108 us -> 0 us
  Pallas kernels: 0 us -> 78.2 us
  starting transfers between devices: 0.12 us -> 29.3 us
  between operations: 14.7 us -> 1.57 us
  blocking collectives: 4.65 us -> 0 us
    dot_general x7 -> x0, matrix products: 108 us -> none  [the longest x1 31.4 us: body(): jnp.einsum('tbc,tck->tbk', residual, item_tiles, preferred_element_type=j...]
    pallas_call x0 -> x18, Pallas kernels: none -> 78.2 us  [the longest x8 36.8 us: item_terms(): pl.pallas_call(functools.partial(item_kernel, pad, key), out_shape=jax.Sh...]
    reduce_scatter x2 -> x0, waiting for transfers between devices: 75.9 us -> none  [the longest x1 69.1 us: body(): lax.psum_scatter(item_partial, 'row', scatter_dimension=0, tiled=True)]
    all_gather x1 -> x0, waiting for transfers between devices: 36.6 us -> none  [body(): item_panel = lax.all_gather(items, 'row', axis=0, tiled=True)]
    ppermute x0 -> x16, starting transfers between devices: none -> 29.3 us  [the longest x14 24.3 us: swap_row(): return lax.ppermute(x, 'row', [(i, i ^ k) for i in range(n_row)])]
    all_gather x2 -> x0, blocking collectives: 4.65 us -> none  [the longest x1 2.47 us: body(): user_panel = lax.all_gather(users, 'col', axis=0, tiled=True)]
    unnamed x12 -> x10, local copies, waits for them, and re-layouts: 0.03 us -> 3.35 us
    dot_general x1 -> x0, local copies, waits for them, and re-layouts: 2.56 us -> none  [segment_total(): jnp.einsum('tv,tbk->vbk', selector, grads, precision=lax.Precision.HIGHEST)]
  transfers between devices with their start and end apart: 3 -> 16, of which waited for: 3 -> 1; matrix products, arithmetic and copies ran while one was open for 2% -> 1% of each run, Pallas kernels for 0% -> 59%
where the time goes in v1:
time: 119 us; the launch traced here: 117 us
  Pallas kernels  78.2 us (66%)
  starting transfers between devices  29.3 us (25%)
  local copies, waits for them, and re-layouts  4.08 us (3%)
  other arithmetic  2.48 us (2%)
  waiting for transfers between devices  1.58 us (1%)
  between operations  1.57 us (1%)
    pallas_call x8, Pallas kernels, item_terms(): pl.pallas_call(functools.partial(item_kernel, pad, key), out_shape=jax.Sh...  36.8 us
    pallas_call x8, Pallas kernels, body(): pl.pallas_call(functools.partial(user_kernel, pad, key, last), out_shape=...  34.8 us
    ppermute x14, starting transfers between devices, swap_row(): return lax.ppermute(x, 'row', [(i, i ^ k) for i in range(n_row)])  24.3 us
    pallas_call x1, Pallas kernels, body(): pl.pallas_call(functools.partial(plan_kernel, slots, pad, wide // BLOCK,...  6.3 us
    ppermute x2, starting transfers between devices, swap_col(): return lax.ppermute(x, 'col', [(i, i ^ 1) for i in range(n_col)])  4.97 us
    unnamed x10, local copies, waits for them, and re-layouts  3.35 us
  transfers between devices with their start and end apart: 16, of which 1 were waited for; matrix products, arithmetic and copies ran while one was open for 1% of the time, Pallas kernels for 59%

profile of v1, /device:TPU:0, one launch (start us, length us, event | category | flops | bytes accessed | tf_op | source)
XLA Modules:
  0.0 117.2 jit_solution(242012618922651797)
XLA Ops:
  0.6 0.5 collective-permute-start
  1.2 2.6 %collective-permute-start.7 = (bf16[512,128]{1,0:T(8,128)(2,1)}, bf16[512,128]{1,0:T(8,128)(2,1)S(1)}, u32[]{:S(2)}, u32[]{:S(2)}) collective-permute-start(bf16[512,128]{1,0:T(8,128)(2,1)} %shard.3), channel_id=1, source_target_pairs={{0,2},{2,0},{4,6},{6,4},{8,10},{10,8},{12,14},{14,12},{1,3},{3,1},... | collective-permute-start | bytes 393224 | tf_op jit(solution)/shard_map/ppermute | solution.py:183
  3.8 1.6 %collective-permute-start.6 = (bf16[512,128]{1,0:T(8,128)(2,1)}, bf16[512,128]{1,0:T(8,128)(2,1)S(1)}, u32[]{:S(2)}, u32[]{:S(2)}) collective-permute-start(bf16[512,128]{1,0:T(8,128)(2,1)} %shard.3), channel_id=1, source_target_pairs={{0,4},{2,6},{4,0},{6,2},{8,12},{10,14},{12,8},{14,10},{1,5},{3,7},... | collective-permute-start | bytes 393224 | tf_op jit(solution)/shard_map/ppermute | solution.py:183
  5.3 0.0 collective-permute-start.5
  5.3 3.0 %collective-permute-start.4 = (bf16[512,128]{1,0:T(8,128)(2,1)}, bf16[512,128]{1,0:T(8,128)(2,1)S(1)}, u32[]{:S(2)}, u32[]{:S(2)}) collective-permute-start(bf16[512,128]{1,0:T(8,128)(2,1)} %shard.3), channel_id=1, source_target_pairs={{0,8},{2,10},{4,12},{6,14},{8,0},{10,2},{12,4},{14,6},{1,9},{3,11}... | collective-permute-start | bytes 393224 | tf_op jit(solution)/shard_map/ppermute | solution.py:183
  9.0 0.6 pad_add_fusion.info
  9.6 6.3 %plan.1 = (s32[616]{0:T(1024)}, bf16[192,128,128]{2,1,0:T(8,128)(2,1)S(1)}, s32[192,16,128]{2,1,0:T(8,128)S(1)}) custom-call(s32[2]{0:T(128)} %pad_add_fusion.info, s32[192]{0:T(256)} %bitcast.9, s32[192]{0:T(256)} %bitcast.10, bf16[192,128,128]{2,1,0:T(8,128)(2,1)} %bitcast.7, s32[192,16,128]{2,1,0:T(8,128)} %bitcast.8), custom_call_target="tpu_custom_call" | custom-call | tf_op jit(solution)/shard_map/plan/pallas_call | solution.py:196
  15.9 2.7 %copy-done = bf16[192,128,128]{2,1,0:T(8,128)(2,1)} copy-done((bf16[192,128,128]{2,1,0:T(8,128)(2,1)}, bf16[192,128,128]{2,1,0:T(8,128)(2,1)S(1)}, u32[]{:S(2)}) %copy-start) | copy-done | bytes 6291480
  18.5 0.0 collective-permute-done
  18.5 0.0 collective-permute-start.3
  18.6 0.0 collective-permute-done.7.shard
  18.6 5.0 %collective-permute-start.2 = (bf16[512,128]{1,0:T(8,128)(2,1)S(1)}, bf16[512,128]{1,0:T(8,128)(2,1)S(1)}, u32[]{:S(2)}, u32[]{:S(2)}) collective-permute-start(bf16[512,128]{1,0:T(8,128)(2,1)S(1)} %copy-done.1), channel_id=1, source_target_pairs={{0,12},{2,14},{4,8},{6,10},{8,4},{10,6},{12,0},{14,2},{1,13},{3,15... | collective-permute-start | bytes 393224 | tf_op jit(solution)/shard_map/ppermute | solution.py:183
  23.6 0.0 collective-permute-done.6.shard
  23.6 1.2 %collective-permute-start.1 = (bf16[512,128]{1,0:T(8,128)(2,1)S(1)}, bf16[512,128]{1,0:T(8,128)(2,1)S(1)}, u32[]{:S(2)}, u32[]{:S(2)}) collective-permute-start(bf16[512,128]{1,0:T(8,128)(2,1)S(1)} %copy-done.1), channel_id=1, source_target_pairs={{0,14},{2,12},{4,10},{6,8},{8,6},{10,4},{12,2},{14,0},{1,15},{3,13... | collective-permute-start | bytes 393224 | tf_op jit(solution)/shard_map/ppermute | solution.py:183
  24.8 0.7 copy-done.2
  25.5 4.5 %user_terms.8.rest_0_ = f32[2048,128]{1,0:T(8,128)S(1)} custom-call(s32[616]{0:T(1024)S(1)} %copy-done.2, bf16[192,128,128]{2,1,0:T(8,128)(2,1)} %copy-done, s32[192,16,128]{2,1,0:T(8,128)S(1)} %get-tuple-element.10.words, bf16[2048,128]{1,0:T(8,128)(2,1)S(1)} %pad_maximum_fusion.users, bf16[512,128]{1,0:T(8,128)(2,1)S(1)} %copy-done.1), custom_call_target="tpu_custom_call" | custom-call | flops 201326592 | bytes 1572864 | tf_op jit(solution)/shard_map/user_terms/pallas_call | solution.py:227
  30.0 4.2 %user_terms.9.rest_0_ = f32[2048,128]{1,0:T(8,128)S(1)} custom-call(s32[616]{0:T(1024)S(1)} %copy-done.2, bf16[192,128,128]{2,1,0:T(8,128)(2,1)} %copy-done, s32[192,16,128]{2,1,0:T(8,128)S(1)} %get-tuple-element.10.words, bf16[2048,128]{1,0:T(8,128)(2,1)S(1)} %pad_maximum_fusion.users, ...), custom_call_target="tpu_custom_call", output_to_operand_aliasing={{}: (5, {})} | custom-call | flops 201326592 | bytes 1572864 | tf_op jit(solution)/shard_map/user_terms/pallas_call | solution.py:227
  34.2 4.2 %user_terms.10.rest_0_ = f32[2048,128]{1,0:T(8,128)S(1)} custom-call(s32[616]{0:T(1024)S(1)} %copy-done.2, bf16[192,128,128]{2,1,0:T(8,128)(2,1)} %copy-done, s32[192,16,128]{2,1,0:T(8,128)S(1)} %get-tuple-element.10.words, bf16[2048,128]{1,0:T(8,128)(2,1)S(1)} %pad_maximum_fusion.users, ...), custom_call_target="tpu_custom_call", output_to_operand_aliasing={{}: (5, {})} | custom-call | flops 201326592 | bytes 1572864 | tf_op jit(solution)/shard_map/user_terms/pallas_call | solution.py:227
  38.4 4.5 %user_terms.11.rest_0_ = f32[2048,128]{1,0:T(8,128)S(1)} custom-call(s32[616]{0:T(1024)S(1)} %copy-done.2, bf16[192,128,128]{2,1,0:T(8,128)(2,1)} %copy-done, s32[192,16,128]{2,1,0:T(8,128)S(1)} %get-tuple-element.10.words, bf16[2048,128]{1,0:T(8,128)(2,1)S(1)} %pad_maximum_fusion.users, ...), custom_call_target="tpu_custom_call", output_to_operand_aliasing={{}: (5, {})} | custom-call | flops 201326592 | bytes 1572864 | tf_op jit(solution)/shard_map/user_terms/pallas_call | solution.py:227
  42.9 4.5 %user_terms.12.rest_0_ = f32[2048,128]{1,0:T(8,128)S(1)} custom-call(s32[616]{0:T(1024)S(1)} %copy-done.2, bf16[192,128,128]{2,1,0:T(8,128)(2,1)} %copy-done, s32[192,16,128]{2,1,0:T(8,128)S(1)} %get-tuple-element.10.words, bf16[2048,128]{1,0:T(8,128)(2,1)S(1)} %pad_maximum_fusion.users, ...), custom_call_target="tpu_custom_call", output_to_operand_aliasing={{}: (5, {})} | custom-call | flops 201326592 | bytes 1572864 | tf_op jit(solution)/shard_map/user_terms/pallas_call | solution.py:227
  47.5 0.0 collective-permute-done.3.shard
  47.5 4.5 %user_terms.13.rest_0_ = f32[2048,128]{1,0:T(8,128)S(1)} custom-call(s32[616]{0:T(1024)S(1)} %copy-done.2, bf16[192,128,128]{2,1,0:T(8,128)(2,1)} %copy-done, s32[192,16,128]{2,1,0:T(8,128)S(1)} %get-tuple-element.10.words, bf16[2048,128]{1,0:T(8,128)(2,1)S(1)} %pad_maximum_fusion.users, ...), custom_call_target="tpu_custom_call", output_to_operand_aliasing={{}: (5, {})} | custom-call | flops 201326592 | bytes 1572864 | tf_op jit(solution)/shard_map/user_terms/pallas_call | solution.py:227
  52.0 4.5 %user_terms.14.rest_0_ = f32[2048,128]{1,0:T(8,128)S(1)} custom-call(s32[616]{0:T(1024)S(1)} %copy-done.2, bf16[192,128,128]{2,1,0:T(8,128)(2,1)} %copy-done, s32[192,16,128]{2,1,0:T(8,128)S(1)} %get-tuple-element.10.words, bf16[2048,128]{1,0:T(8,128)(2,1)S(1)} %pad_maximum_fusion.users, ...), custom_call_target="tpu_custom_call", output_to_operand_aliasing={{}: (5, {})} | custom-call | flops 201326592 | bytes 1572864 | tf_op jit(solution)/shard_map/user_terms/pallas_call | solution.py:227
  56.5 0.0 collective-permute-done.1.shard
  56.5 3.9 %user_terms.15 = (f32[2048,128]{1,0:T(8,128)S(1)}, bf16[2048,128]{1,0:T(8,128)(2,1)S(1)}) custom-call(s32[616]{0:T(1024)S(1)} %copy-done.2, bf16[192,128,128]{2,1,0:T(8,128)(2,1)} %copy-done, s32[192,16,128]{2,1,0:T(8,128)S(1)} %get-tuple-element.10.words, bf16[2048,128]{1,0:T(8,128)(2,1)S(1)} %pad_maximum_fusion.users, ...), custom_call_target="tpu_custom_call", output_to_operand_aliasing={{0}: (5, {})} | custom-call | flops 201326592 | bytes 1572864 | tf_op jit(solution)/shard_map/user_terms/pallas_call | solution.py:227
  60.5 4.5 %collective-permute-start.8 = (bf16[2048,128]{1,0:T(8,128)(2,1)S(1)}, bf16[2048,128]{1,0:T(8,128)(2,1)S(1)}, u32[]{:S(2)}, u32[]{:S(2)}) collective-permute-start(bf16[2048,128]{1,0:T(8,128)(2,1)S(1)} %get-tuple-element.11.mine), channel_id=1, source_target_pairs={{0,1},{1,0},{2,3},{3,2},{4,5},{5,4},{6,7},{7,6},{8,9},{9,8},{10,11... | collective-permute-start | bytes 1572872 | tf_op jit(solution)/shard_map/ppermute | solution.py:186
  64.9 1.5 %collective-permute-done.8.theirs = bf16[2048,128]{1,0:T(8,128)(2,1)S(1)} collective-permute-done((bf16[2048,128]{1,0:T(8,128)(2,1)S(1)}, bf16[2048,128]{1,0:T(8,128)(2,1)S(1)}, u32[]{:S(2)}, u32[]{:S(2)}) %collective-permute-start.8) | collective-permute-done | bytes 524320 | tf_op jit(solution)/shard_map/ppermute | solution.py:186
  66.4 0.4 fresh.1
  66.8 4.7 %item_terms.9 = bf16[512,128]{1,0:T(8,128)(2,1)} custom-call(s32[616]{0:T(1024)S(1)} %copy-done.2, bf16[192,128,128]{2,1,0:T(8,128)(2,1)} %copy-done, s32[192,16,128]{2,1,0:T(8,128)S(1)} %get-tuple-element.10.words, bf16[2048,128]{1,0:T(8,128)(2,1)S(1)} %get-tuple-element.12.fresh, bf16[2048,128]{1,0:T(8,128)(2,1)S(1)} %get-tuple-element.13.turned, ...), custom_call_target="tpu_custom_call" | custom-call | flops 201326592 | bytes 1572864 | tf_op jit(solution)/shard_map/item_terms/pallas_call | solution.py:253
  71.5 3.8 %collective-permute-start.9 = (bf16[512,128]{1,0:T(8,128)(2,1)}, bf16[512,128]{1,0:T(8,128)(2,1)}, u32[]{:S(2)}, u32[]{:S(2)}) collective-permute-start(bf16[512,128]{1,0:T(8,128)(2,1)} %item_terms.9), channel_id=1, source_target_pairs={{0,14},{2,12},{4,10},{6,8},{8,6},{10,4},{12,2},{14,0},{1,15},{3,13... | collective-permute-start | bytes 393224 | tf_op jit(solution)/shard_map/ppermute | solution.py:183
  75.3 4.7 %item_terms.10 = bf16[512,128]{1,0:T(8,128)(2,1)S(1)} custom-call(s32[616]{0:T(1024)S(1)} %copy-done.2, bf16[192,128,128]{2,1,0:T(8,128)(2,1)} %copy-done, s32[192,16,128]{2,1,0:T(8,128)S(1)} %get-tuple-element.10.words, bf16[2048,128]{1,0:T(8,128)(2,1)S(1)} %get-tuple-element.12.fresh, bf16[2048,128]{1,0:T(8,128)(2,1)S(1)} %get-tuple-element.13.turned, ...), custom_call_target="tpu_custom_call" | custom-call | flops 201326592 | bytes 1572864 | tf_op jit(solution)/shard_map/item_terms/pallas_call | solution.py:253
  80.0 0.1 collective-permute-start.10
  80.1 4.7 %item_terms.11 = bf16[512,128]{1,0:T(8,128)(2,1)S(1)} custom-call(s32[616]{0:T(1024)S(1)} %copy-done.3, bf16[192,128,128]{2,1,0:T(8,128)(2,1)} %copy-done, s32[192,16,128]{2,1,0:T(8,128)S(1)} %get-tuple-element.10.words, bf16[2048,128]{1,0:T(8,128)(2,1)S(1)} %get-tuple-element.12.fresh, bf16[2048,128]{1,0:T(8,128)(2,1)S(1)} %get-tuple-element.13.turned, ...), custom_call_target="tpu_custom_call" | custom-call | flops 201326592 | bytes 1572864 | tf_op jit(solution)/shard_map/item_terms/pallas_call | solution.py:253
  84.8 0.1 collective-permute-start.11
  84.8 4.7 %item_terms.12 = bf16[512,128]{1,0:T(8,128)(2,1)S(1)} custom-call(s32[616]{0:T(1024)S(1)} %copy-done.3, bf16[192,128,128]{2,1,0:T(8,128)(2,1)} %copy-done, s32[192,16,128]{2,1,0:T(8,128)S(1)} %get-tuple-element.10.words, bf16[2048,128]{1,0:T(8,128)(2,1)S(1)} %get-tuple-element.12.fresh, bf16[2048,128]{1,0:T(8,128)(2,1)S(1)} %get-tuple-element.13.turned, ...), custom_call_target="tpu_custom_call" | custom-call | flops 201326592 | bytes 1572864 | tf_op jit(solution)/shard_map/item_terms/pallas_call | solution.py:253
  89.5 3.9 %collective-permute-start.12 = (bf16[512,128]{1,0:T(8,128)(2,1)S(1)}, bf16[512,128]{1,0:T(8,128)(2,1)S(1)}, u32[]{:S(2)}, u32[]{:S(2)}) collective-permute-start(bf16[512,128]{1,0:T(8,128)(2,1)S(1)} %item_terms.12), channel_id=1, source_target_pairs={{0,8},{2,10},{4,12},{6,14},{8,0},{10,2},{12,4},{14,6},{1,9},{3,11}... | collective-permute-start | bytes 393224 | tf_op jit(solution)/shard_map/ppermute | solution.py:183
  93.4 4.7 %item_terms.13 = bf16[512,128]{1,0:T(8,128)(2,1)S(1)} custom-call(s32[616]{0:T(1024)S(1)} %copy-done.3, bf16[192,128,128]{2,1,0:T(8,128)(2,1)} %copy-done, s32[192,16,128]{2,1,0:T(8,128)S(1)} %get-tuple-element.10.words, bf16[2048,128]{1,0:T(8,128)(2,1)S(1)} %get-tuple-element.12.fresh, bf16[2048,128]{1,0:T(8,128)(2,1)S(1)} %get-tuple-element.13.turned, ...), custom_call_target="tpu_custom_call" | custom-call | flops 201326592 | bytes 1572864 | tf_op jit(solution)/shard_map/item_terms/pallas_call | solution.py:253
  98.1 0.5 collective-permute-start.13
  98.6 4.3 %item_terms.15 = bf16[512,128]{1,0:T(8,128)(2,1)S(1)} custom-call(s32[616]{0:T(1024)S(1)} %copy-done.3, bf16[192,128,128]{2,1,0:T(8,128)(2,1)} %copy-done, s32[192,16,128]{2,1,0:T(8,128)S(1)} %get-tuple-element.10.words, bf16[2048,128]{1,0:T(8,128)(2,1)S(1)} %get-tuple-element.12.fresh, bf16[2048,128]{1,0:T(8,128)(2,1)S(1)} %get-tuple-element.13.turned, ...), custom_call_target="tpu_custom_call" | custom-call | flops 201326592 | bytes 1572864 | tf_op jit(solution)/shard_map/item_terms/pallas_call | solution.py:253
  102.9 4.3 %item_terms.14 = bf16[512,128]{1,0:T(8,128)(2,1)S(1)} custom-call(s32[616]{0:T(1024)S(1)} %copy-done.3, bf16[192,128,128]{2,1,0:T(8,128)(2,1)} %copy-done, s32[192,16,128]{2,1,0:T(8,128)S(1)} %get-tuple-element.10.words, bf16[2048,128]{1,0:T(8,128)(2,1)S(1)} %get-tuple-element.12.fresh, bf16[2048,128]{1,0:T(8,128)(2,1)S(1)} %get-tuple-element.13.turned, ...), custom_call_target="tpu_custom_call" | custom-call | flops 201326592 | bytes 1572864 | tf_op jit(solution)/shard_map/item_terms/pallas_call | solution.py:253
  107.3 0.0 collective-permute-done.9
  107.3 2.7 %collective-permute-start.14 = (bf16[512,128]{1,0:T(8,128)(2,1)S(1)}, bf16[512,128]{1,0:T(8,128)(2,1)S(1)}, u32[]{:S(2)}, u32[]{:S(2)}) collective-permute-start(bf16[512,128]{1,0:T(8,128)(2,1)S(1)} %item_terms.14), channel_id=1, source_target_pairs={{0,4},{2,6},{4,0},{6,2},{8,12},{10,14},{12,8},{14,10},{1,5},{3,7},... | collective-permute-start | bytes 393224 | tf_op jit(solution)/shard_map/ppermute | solution.py:183
  110.0 4.7 %item_terms.8 = f32[512,128]{1,0:T(8,128)S(1)} custom-call(s32[616]{0:T(1024)S(1)} %copy-done.3, bf16[192,128,128]{2,1,0:T(8,128)(2,1)} %copy-done, s32[192,16,128]{2,1,0:T(8,128)S(1)} %get-tuple-element.10.words, bf16[2048,128]{1,0:T(8,128)(2,1)S(1)} %get-tuple-element.12.fresh, bf16[2048,128]{1,0:T(8,128)(2,1)S(1)} %get-tuple-element.13.turned, ...), custom_call_target="tpu_custom_call" | custom-call | flops 201326592 | bytes 1572864 | tf_op jit(solution)/shard_map/item_terms/pallas_call | solution.py:253
  114.7 0.7 constant_dynamic-slice_fusion
  115.4 0.0 collective-permute-done.11
  115.4 0.0 collective-permute-done.12
  115.4 0.0 collective-permute-done.13
  115.4 1.8 %fusion.2 = bf16[512,128]{1,0:T(8,128)(2,1)} fusion(bf16[512,128]{1,0:T(8,128)(2,1)S(1)} %copy-done.1, bf16[512,128]{1,0:T(8,128)(2,1)S(1)} %collective-permute-done.15, bf16[512,128]{1,0:T(8,128)(2,1)S(1)} %collective-permute-done.14, bf16[512,128]{1,0:T(8,128)(2,1)S(1)} %collective-permute-done.13, bf16[512,128]{1,0:T(8,128)(2,1)S(1)} %collective-permute-done.12, ...), kind=kLoop, calls=%fused_computation.5 | loop fusion | flops 1310720 | bytes 1441792 | tf_op jit(solution)/shard_map/convert_element_type | solution.py:277
  (17 shorter events, 0.1 us)
Async XLA Ops:
  0.6 17.9 %copy-start.4 = (bf16[1024,128]{1,0:T(8,128)(2,1)S(1)}, bf16[1024,128]{1,0:T(8,128)(2,1)}, u32[]{:S(2)}) copy-start(bf16[1024,128]{1,0:T(8,128)(2,1)} %param.7) | copy-start | bytes 786436
  0.6 17.9 %copy-start.1 = (bf16[512,128]{1,0:T(8,128)(2,1)S(1)}, bf16[512,128]{1,0:T(8,128)(2,1)}, u32[]{:S(2)}) copy-start(bf16[512,128]{1,0:T(8,128)(2,1)} %shard.3) | copy-start | bytes 393220
  0.6 17.9 %collective-permute-start = (bf16[1024,128]{1,0:T(8,128)(2,1)}, bf16[1024,128]{1,0:T(8,128)(2,1)S(1)}, u32[]{:S(2)}, u32[]{:S(2)}) collective-permute-start(bf16[1024,128]{1,0:T(8,128)(2,1)} %param.7), channel_id=1, source_target_pairs={{0,1},{1,0},{2,3},{3,2},{4,5},{5,4},{6,7},{7,6},{8,9},{9,8},{10,11... | collective-permute-start | bytes 786440 | tf_op jit(solution)/shard_map/ppermute | solution.py:186
  1.2 17.4 %collective-permute-start.7 = (bf16[512,128]{1,0:T(8,128)(2,1)}, bf16[512,128]{1,0:T(8,128)(2,1)S(1)}, u32[]{:S(2)}, u32[]{:S(2)}) collective-permute-start(bf16[512,128]{1,0:T(8,128)(2,1)} %shard.3), channel_id=1, source_target_pairs={{0,2},{2,0},{4,6},{6,4},{8,10},{10,8},{12,14},{14,12},{1,3},{3,1},... | collective-permute-start | bytes 393224 | tf_op jit(solution)/shard_map/ppermute | solution.py:183
  3.8 19.9 %collective-permute-start.6 = (bf16[512,128]{1,0:T(8,128)(2,1)}, bf16[512,128]{1,0:T(8,128)(2,1)S(1)}, u32[]{:S(2)}, u32[]{:S(2)}) collective-permute-start(bf16[512,128]{1,0:T(8,128)(2,1)} %shard.3), channel_id=1, source_target_pairs={{0,4},{2,6},{4,0},{6,2},{8,12},{10,14},{12,8},{14,10},{1,5},{3,7},... | collective-permute-start | bytes 393224 | tf_op jit(solution)/shard_map/ppermute | solution.py:183
  5.3 33.1 %collective-permute-start.5 = (bf16[512,128]{1,0:T(8,128)(2,1)}, bf16[512,128]{1,0:T(8,128)(2,1)S(1)}, u32[]{:S(2)}, u32[]{:S(2)}) collective-permute-start(bf16[512,128]{1,0:T(8,128)(2,1)} %shard.3), channel_id=1, source_target_pairs={{0,6},{2,4},{4,2},{6,0},{8,14},{10,12},{12,10},{14,8},{1,7},{3,5},... | collective-permute-start | bytes 393224 | tf_op jit(solution)/shard_map/ppermute | solution.py:183
  5.3 37.6 %collective-permute-start.4 = (bf16[512,128]{1,0:T(8,128)(2,1)}, bf16[512,128]{1,0:T(8,128)(2,1)S(1)}, u32[]{:S(2)}, u32[]{:S(2)}) collective-permute-start(bf16[512,128]{1,0:T(8,128)(2,1)} %shard.3), channel_id=1, source_target_pairs={{0,8},{2,10},{4,12},{6,14},{8,0},{10,2},{12,4},{14,6},{1,9},{3,11}... | collective-permute-start | bytes 393224 | tf_op jit(solution)/shard_map/ppermute | solution.py:183
  15.9 2.7 %copy-start = (bf16[192,128,128]{2,1,0:T(8,128)(2,1)}, bf16[192,128,128]{2,1,0:T(8,128)(2,1)S(1)}, u32[]{:S(2)}) copy-start(bf16[192,128,128]{2,1,0:T(8,128)(2,1)S(1)} %get-tuple-element.9.tiles) | copy-start | bytes 18874372
  18.5 28.9 %collective-permute-start.3 = (bf16[512,128]{1,0:T(8,128)(2,1)S(1)}, bf16[512,128]{1,0:T(8,128)(2,1)S(1)}, u32[]{:S(2)}, u32[]{:S(2)}) collective-permute-start(bf16[512,128]{1,0:T(8,128)(2,1)S(1)} %copy-done.1), channel_id=1, source_target_pairs={{0,10},{2,8},{4,14},{6,12},{8,2},{10,0},{12,6},{14,4},{1,11},{3,9}... | collective-permute-start | bytes 393224 | tf_op jit(solution)/shard_map/ppermute | solution.py:183
  18.6 33.4 %collective-permute-start.2 = (bf16[512,128]{1,0:T(8,128)(2,1)S(1)}, bf16[512,128]{1,0:T(8,128)(2,1)S(1)}, u32[]{:S(2)}, u32[]{:S(2)}) collective-permute-start(bf16[512,128]{1,0:T(8,128)(2,1)S(1)} %copy-done.1), channel_id=1, source_target_pairs={{0,12},{2,14},{4,8},{6,10},{8,4},{10,6},{12,0},{14,2},{1,13},{3,15... | collective-permute-start | bytes 393224 | tf_op jit(solution)/shard_map/ppermute | solution.py:183
  23.6 32.9 %collective-permute-start.1 = (bf16[512,128]{1,0:T(8,128)(2,1)S(1)}, bf16[512,128]{1,0:T(8,128)(2,1)S(1)}, u32[]{:S(2)}, u32[]{:S(2)}) collective-permute-start(bf16[512,128]{1,0:T(8,128)(2,1)S(1)} %copy-done.1), channel_id=1, source_target_pairs={{0,14},{2,12},{4,10},{6,8},{8,6},{10,4},{12,2},{14,0},{1,15},{3,13... | collective-permute-start | bytes 393224 | tf_op jit(solution)/shard_map/ppermute | solution.py:183
  24.8 0.7 copy-start.2
  60.5 6.0 %collective-permute-start.8 = (bf16[2048,128]{1,0:T(8,128)(2,1)S(1)}, bf16[2048,128]{1,0:T(8,128)(2,1)S(1)}, u32[]{:S(2)}, u32[]{:S(2)}) collective-permute-start(bf16[2048,128]{1,0:T(8,128)(2,1)S(1)} %get-tuple-element.11.mine), channel_id=1, source_target_pairs={{0,1},{1,0},{2,3},{3,2},{4,5},{5,4},{6,7},{7,6},{8,9},{9,8},{10,11... | collective-permute-start | bytes 1572872 | tf_op jit(solution)/shard_map/ppermute | solution.py:186
  71.5 8.6 %copy-start.3 = (s32[616]{0:T(1024)S(1)}, s32[616]{0:T(1024)}, u32[]{:S(2)}) copy-start(s32[616]{0:T(1024)} %get-tuple-element.8.meta) | copy-start | bytes 7396
  71.5 35.8 %collective-permute-start.9 = (bf16[512,128]{1,0:T(8,128)(2,1)}, bf16[512,128]{1,0:T(8,128)(2,1)}, u32[]{:S(2)}, u32[]{:S(2)}) collective-permute-start(bf16[512,128]{1,0:T(8,128)(2,1)} %item_terms.9), channel_id=1, source_target_pairs={{0,14},{2,12},{4,10},{6,8},{8,6},{10,4},{12,2},{14,0},{1,15},{3,13... | collective-permute-start | bytes 393224 | tf_op jit(solution)/shard_map/ppermute | solution.py:183
  80.0 30.0 %collective-permute-start.10 = (bf16[512,128]{1,0:T(8,128)(2,1)S(1)}, bf16[512,128]{1,0:T(8,128)(2,1)}, u32[]{:S(2)}, u32[]{:S(2)}) collective-permute-start(bf16[512,128]{1,0:T(8,128)(2,1)S(1)} %item_terms.10), channel_id=1, source_target_pairs={{0,12},{2,14},{4,8},{6,10},{8,4},{10,6},{12,0},{14,2},{1,13},{3,15... | collective-permute-start | bytes 393224 | tf_op jit(solution)/shard_map/ppermute | solution.py:183
  84.8 30.6 %collective-permute-start.11 = (bf16[512,128]{1,0:T(8,128)(2,1)S(1)}, bf16[512,128]{1,0:T(8,128)(2,1)S(1)}, u32[]{:S(2)}, u32[]{:S(2)}) collective-permute-start(bf16[512,128]{1,0:T(8,128)(2,1)S(1)} %item_terms.11), channel_id=1, source_target_pairs={{0,10},{2,8},{4,14},{6,12},{8,2},{10,0},{12,6},{14,4},{1,11},{3,9}... | collective-permute-start | bytes 393224 | tf_op jit(solution)/shard_map/ppermute | solution.py:183
  89.5 25.9 %collective-permute-start.12 = (bf16[512,128]{1,0:T(8,128)(2,1)S(1)}, bf16[512,128]{1,0:T(8,128)(2,1)S(1)}, u32[]{:S(2)}, u32[]{:S(2)}) collective-permute-start(bf16[512,128]{1,0:T(8,128)(2,1)S(1)} %item_terms.12), channel_id=1, source_target_pairs={{0,8},{2,10},{4,12},{6,14},{8,0},{10,2},{12,4},{14,6},{1,9},{3,11}... | collective-permute-start | bytes 393224 | tf_op jit(solution)/shard_map/ppermute | solution.py:183
  98.1 17.3 %collective-permute-start.13 = (bf16[512,128]{1,0:T(8,128)(2,1)S(1)}, bf16[512,128]{1,0:T(8,128)(2,1)S(1)}, u32[]{:S(2)}, u32[]{:S(2)}) collective-permute-start(bf16[512,128]{1,0:T(8,128)(2,1)S(1)} %item_terms.13), channel_id=1, source_target_pairs={{0,6},{2,4},{4,2},{6,0},{8,14},{10,12},{12,10},{14,8},{1,7},{3,5},... | collective-permute-start | bytes 393224 | tf_op jit(solution)/shard_map/ppermute | solution.py:183
  107.3 8.1 %collective-permute-start.14 = (bf16[512,128]{1,0:T(8,128)(2,1)S(1)}, bf16[512,128]{1,0:T(8,128)(2,1)S(1)}, u32[]{:S(2)}, u32[]{:S(2)}) collective-permute-start(bf16[512,128]{1,0:T(8,128)(2,1)S(1)} %item_terms.14), channel_id=1, source_target_pairs={{0,4},{2,6},{4,0},{6,2},{8,12},{10,14},{12,8},{14,10},{1,5},{3,7},... | collective-permute-start | bytes 393224 | tf_op jit(solution)/shard_map/ppermute | solution.py:183
  109.9 5.5 %collective-permute-start.15 = (bf16[512,128]{1,0:T(8,128)(2,1)S(1)}, bf16[512,128]{1,0:T(8,128)(2,1)S(1)}, u32[]{:S(2)}, u32[]{:S(2)}) collective-permute-start(bf16[512,128]{1,0:T(8,128)(2,1)S(1)} %item_terms.15), channel_id=1, source_target_pairs={{0,2},{2,0},{4,6},{6,4},{8,10},{10,8},{12,14},{14,12},{1,3},{3,1},... | collective-permute-start | bytes 393224 | tf_op jit(solution)/shard_map/ppermute | solution.py:183

commit v2 on v0

v2 whole, which is shorter than its diff:
```python
import functools

import jax
import jax.numpy as jnp
from jax import lax
from jax.experimental import pallas as pl
from jax.experimental.pallas import tpu as pltpu
from jax.sharding import PartitionSpec as P

BLOCK = 128
UNROLL = 16
FIELD = 10
VMEM_LIMIT = 16 * 1024 * 1024
PLAN_LIMIT = 50 * 1024 * 1024

NN = (((1,), (0,)), ((), ()))

vmem = functools.partial(pl.BlockSpec, memory_space=pltpu.VMEM)
smem = functools.partial(pl.BlockSpec, memory_space=pltpu.SMEM)
anywhere = functools.partial(pl.BlockSpec, memory_space=pl.ANY)


def params(limit=VMEM_LIMIT):
    return pltpu.CompilerParams(vmem_limit_bytes=limit)


def dot(a, b):
    return lax.dot_general(a, b, NN, preferred_element_type=jnp.float32)


def rows_of(index):
    return pl.ds(pl.multiple_of(index * BLOCK, BLOCK), BLOCK)


def tile(index):
    return slice(index * BLOCK, (index + 1) * BLOCK)


def plan_kernel(
    shard_tiles, group, stages, info, rows, cols, ratings, observed, meta, tiles, words, sems
):
    copy_tiles = pltpu.make_async_copy(ratings, tiles, sems.at[0])
    copy_words = pltpu.make_async_copy(observed, words, sems.at[1])
    copy_tiles.start()
    copy_words.start()
    count = info[0]
    me = info[1]
    ends = meta.shape[0] - 2

    def put(t, places):
        low, high = places
        v = cols[t]
        near = jnp.int32(1)
        if stages > 1:
            key = jnp.bitwise_xor(v // shard_tiles, me)
            near = jnp.where(key < group, 1, 0)
            v = (key % group) * shard_tiles + v % shard_tiles
        meta[jnp.where(near == 1, low, high)] = t + (rows[t] << FIELD) + (v << 2 * FIELD)
        return low + near, high - 1 + near

    low, _ = lax.fori_loop(0, count, put, (jnp.int32(0), count - 1))
    for at in range(UNROLL):
        meta[count + at] = 0
    meta[ends] = low
    meta[ends + 1] = count
    copy_tiles.wait()
    copy_words.wait()


def stage_loop(stage, meta, step_of):
    ends = meta.shape[0] - 2
    low = meta[ends] if stage else 0
    high = meta[ends + stage]
    mask = (1 << FIELD) - 1

    def step(i, _):
        entries = []
        for j in range(UNROLL):
            at = low + i * UNROLL + j
            word = meta[at]
            entries.append(
                (word & mask, (word >> FIELD) & mask, word >> 2 * FIELD, at < high)
            )
        step_of(entries)
        return _

    lax.fori_loop(0, (high - low + UNROLL - 1) // UNROLL, step, 0)


def masked_residual(predicted, tiles, words, slot, live):
    bit = jnp.left_shift(1, lax.broadcasted_iota(jnp.int32, (8, BLOCK), 0))
    bit = jnp.where(live, bit, 0)
    parts = []
    for w in range(BLOCK // 8):
        seen = jnp.broadcast_to(words[slot, pl.ds(w, 1), :], (8, BLOCK)) & bit
        gap = predicted[8 * w : 8 * w + 8] - tiles[slot, pl.ds(8 * w, 8), :].astype(jnp.float32)
        parts.append(jnp.where(seen != 0, gap, 0.0))
    return jnp.concatenate(parts, axis=0).astype(jnp.bfloat16)


def lay_items(shards, panel, flipped):
    per = shards[0].shape[0] // BLOCK
    for s, shard in enumerate(shards):
        for v in range(per):
            block = shard[tile(v)]
            panel[tile(s * per + v)] = block
            flipped[tile(s * per + v)] = block.T


def user_kernel(stage, group, last, *refs):
    if stage == 0:
        info, meta, tiles, words, mine, theirs = refs[:6]
        shards = refs[6 : 6 + group]
        users, flipped, total = refs[6 + group : 9 + group]
        count = mine.shape[0]
        lead = info[2] == 0
        users[:count] = jnp.where(lead, mine[...], theirs[...])
        users[count:] = jnp.where(lead, theirs[...], mine[...])
        total[...] = jnp.zeros_like(total)
    else:
        meta, tiles, words, users = refs[:4]
        shards = refs[4 : 4 + group]
        flipped, total = refs[5 + group : 7 + group]
    panel = refs[-1]
    lay_items(shards, panel, flipped)

    def step_of(entries):
        terms = []
        for slot, u, v, live in entries:
            predicted = dot(users[rows_of(u), :], flipped[rows_of(v), :])
            residual = masked_residual(predicted, tiles, words, slot, live)
            terms.append(dot(residual, panel[rows_of(v), :]))
        for (slot, u, v, live), term in zip(entries, terms):
            total[rows_of(u), :] += term

    stage_loop(stage, meta, step_of)
    if last:
        refs[-2][...] = total[...].astype(jnp.bfloat16)


def item_kernel(stage, group, first, *refs):
    if first:
        meta, tiles, words, mine, theirs, users, flipped = refs[:7]
        outs = refs[7 : 7 + group]
        fresh, turned = refs[7 + group : 9 + group]
        for u in range(users.shape[0] // BLOCK):
            values = users[tile(u)].astype(jnp.float32)
            gradient = mine[tile(u)].astype(jnp.float32) + theirs[tile(u)].astype(jnp.float32)
            new = (values - 0.02 * (gradient + 0.05 * values)).astype(jnp.bfloat16)
            fresh[tile(u)] = new
            turned[tile(u)] = new.T
    else:
        meta, tiles, words, fresh, turned, flipped = refs[:6]
        outs = refs[6 : 6 + group]
    total = refs[-1]
    total[...] = jnp.zeros_like(total)

    def step_of(entries):
        terms = []
        for slot, u, v, live in entries:
            predicted = dot(fresh[rows_of(u), :], flipped[rows_of(v), :])
            residual = masked_residual(predicted, tiles, words, slot, live)
            terms.append(dot(turned[rows_of(u), :], residual))
        for (slot, u, v, live), term in zip(entries, terms):
            total[rows_of(v), :] += term

    stage_loop(stage, meta, step_of)
    size = outs[0].shape[0]
    for s, out in enumerate(outs):
        out[...] = total[s * size : (s + 1) * size].astype(out.dtype)


def finish_kernel(items, *refs):
    out = refs[-1]
    for v in range(items.shape[0] // BLOCK):
        gradient = refs[0][tile(v)].astype(jnp.float32)
        for part in refs[1:-1]:
            gradient = gradient + part[tile(v)].astype(jnp.float32)
        values = items[tile(v)].astype(jnp.float32)
        out[tile(v)] = (values - 0.005 * (gradient.T + 0.05 * values)).astype(jnp.bfloat16)


def body(n_row, n_col, users, items, ratings, observed, tile_rows, tile_cols, tile_count):
    tiles = ratings[0, 0]
    words = observed[0, 0]
    slots = tiles.shape[0]
    rank = users.shape[-1]
    pad = slots + UNROLL
    direct = items.shape[0] % BLOCK == 0 and n_row & (n_row - 1) == 0 and n_row > 1
    stages = 2 if direct else 1
    group = n_row // 2 if direct else 1
    row_at = lax.axis_index("row")
    col_at = lax.axis_index("col")

    def swap_row(x, k):
        return lax.ppermute(x, "row", [(i, i ^ k) for i in range(n_row)])

    def swap_col(x):
        return lax.ppermute(x, "col", [(i, i ^ 1) for i in range(n_col)])

    peer_users = swap_col(users)
    if direct:
        crossed = swap_row(items, group)
        shards = [
            [items] + [swap_row(items, k) for k in range(1, group)],
            [crossed] + [swap_row(crossed, k) for k in range(1, group)],
        ]
    else:
        shards = [[lax.all_gather(items, "row", axis=0, tiled=True)]]
    wide = shards[0][0].shape[0]

    info = jnp.stack([tile_count[0, 0], row_at, col_at]).astype(jnp.int32)
    meta, tiles, words = pl.pallas_call(
        functools.partial(plan_kernel, wide // BLOCK, group, stages),
        out_shape=(
            jax.ShapeDtypeStruct((pad + 2,), jnp.int32),
            pltpu.VMEM(tiles.shape, tiles.dtype),
            pltpu.VMEM(words.shape, words.dtype),
        ),
        in_specs=[smem()] * 3 + [anywhere()] * 2,
        out_specs=(smem(), vmem(), vmem()),
        scratch_shapes=[pltpu.SemaphoreType.DMA((2,))],
        compiler_params=params(PLAN_LIMIT),
        name="plan",
    )(info, tile_rows[0, 0], tile_cols[0, 0], tiles, words)

    cost = pl.CostEstimate(
        flops=4 * slots * BLOCK * BLOCK * rank // stages,
        bytes_accessed=(slots // stages) * BLOCK * BLOCK * 4,
        transcendentals=0,
    )
    user_shape = (n_col * users.shape[0], rank)
    panel_shape = (group * wide, rank)
    flipped = []
    for stage in range(stages):
        last = stage == stages - 1
        shapes = [pltpu.VMEM(panel_shape, jnp.bfloat16), pltpu.VMEM(user_shape, jnp.float32)]
        if stage == 0:
            operands = [info, meta, tiles, words, users, peer_users] + shards[0]
            shapes = [pltpu.VMEM(user_shape, jnp.bfloat16)] + shapes
            aliases = {}
        else:
            operands = [meta, tiles, words, panel] + shards[stage] + [total]
            aliases = {len(operands) - 1: 1}
        if last:
            shapes.append(jax.ShapeDtypeStruct(user_shape, jnp.bfloat16))
        scalars = 2 if stage == 0 else 1
        outs = list(pl.pallas_call(
            functools.partial(user_kernel, stage, group, last),
            out_shape=tuple(shapes),
            in_specs=[smem()] * scalars + [vmem()] * (len(operands) - scalars),
            out_specs=tuple([vmem()] * len(shapes)),
            input_output_aliases=aliases,
            scratch_shapes=[pltpu.VMEM(panel_shape, jnp.bfloat16)],
            compiler_params=params(),
            cost_estimate=cost,
            name="user_terms",
        )(*operands))
        if stage == 0:
            panel = outs.pop(0)
        flipped.append(outs[0])
        total = outs[1]
    terms = outs[-1]
    peer_terms = swap_col(terms)

    fresh = turned = None
    sums = [None] * stages
    for stage in range(stages - 1, -1, -1):
        first = fresh is None
        shapes = [jax.ShapeDtypeStruct((wide, rank), jnp.float32)]
        shapes += [jax.ShapeDtypeStruct((wide, rank), jnp.bfloat16)] * (group - 1)
        if first:
            operands = [meta, tiles, words, terms, peer_terms, panel, flipped[stage]]
            shapes += [pltpu.VMEM(user_shape, jnp.bfloat16)] * 2
        else:
            operands = [meta, tiles, words, fresh, turned, flipped[stage]]
        outs = pl.pallas_call(
            functools.partial(item_kernel, stage, group, first),
            out_shape=tuple(shapes),
            in_specs=[smem()] + [vmem()] * (len(operands) - 1),
            out_specs=tuple([vmem()] * len(shapes)),
            scratch_shapes=[pltpu.VMEM(panel_shape, jnp.float32)],
            compiler_params=params(),
            cost_estimate=cost,
            name="item_terms",
        )(*operands)
        if first:
            fresh, turned = outs[group:]
        sums[stage] = [outs[0]] + [swap_row(outs[k], k) for k in range(1, group)]
    users_new = lax.dynamic_slice_in_dim(fresh, col_at * users.shape[0], users.shape[0], 0)

    if direct:
        relay = sums[1][0]
        for part in sums[1][1:]:
            relay = relay + part.astype(jnp.float32)
        parts = sums[0] + [swap_row(relay.astype(jnp.bfloat16), group)]
        items_new = pl.pallas_call(
            finish_kernel,
            out_shape=jax.ShapeDtypeStruct(items.shape, jnp.bfloat16),
            in_specs=[vmem()] * (1 + len(parts)),
            out_specs=vmem(),
            compiler_params=params(),
            name="finish",
        )(items, *parts)
    else:
        turned_terms = jnp.swapaxes(sums[0][0].reshape(-1, BLOCK, BLOCK), 1, 2)
        item_grad = lax.psum_scatter(
            turned_terms.reshape(wide, rank), "row", scatter_dimension=0, tiled=True
        )
        values = items.astype(jnp.float32)
        items_new = (values - 0.005 * (item_grad + 0.05 * values)).astype(jnp.bfloat16)
    return (users_new, items_new)


def solution(mesh):
    return jax.shard_map(
        functools.partial(body, mesh.shape["row"], mesh.shape["col"]),
        mesh=mesh,
        in_specs=(
            P(("groups", "row", "col"), None),
            P(("groups", "row", "col"), None),
            P(("groups", "row"), "col", None, None, None),
            P(("groups", "row"), "col", None, None, None),
            P(("groups", "row"), "col", None),
            P(("groups", "row"), "col", None),
            P(("groups", "row"), "col"),
        ),
        out_specs=(P(("groups", "row", "col"), None), P(("groups", "row", "col"), None)),
        check_vma=False,
    )
```

time: 251 us -> 56.6 us (0.23); the launches traced: 247 us -> 56.4 us
  matrix products: 108 us -> 0 us
  waiting for transfers between devices: 113 us -> 13.8 us
  starting transfers between devices: 0.12 us -> 22.3 us
  Pallas kernels: 0 us -> 16.7 us
  between operations: 14.7 us -> 1.46 us
  blocking collectives: 4.65 us -> 0 us
    dot_general x7 -> x0, matrix products: 108 us -> none  [the longest x1 31.4 us: body(): jnp.einsum('tbc,tck->tbk', residual, item_tiles, preferred_element_type=j...]
    reduce_scatter x2 -> x0, waiting for transfers between devices: 75.9 us -> none  [the longest x1 69.1 us: body(): lax.psum_scatter(item_partial, 'row', scatter_dimension=0, tiled=True)]
    all_gather x1 -> x0, waiting for transfers between devices: 36.6 us -> none  [body(): item_panel = lax.all_gather(items, 'row', axis=0, tiled=True)]
    ppermute x0 -> x16, starting transfers between devices: none -> 22.3 us  [the longest x14 21.7 us: swap_row(): return lax.ppermute(x, 'row', [(i, i ^ k) for i in range(n_row)])]
    pallas_call x0 -> x6, Pallas kernels: none -> 16.7 us  [the longest x2 5.68 us: body(): pl.pallas_call(functools.partial(user_kernel, stage, group, last), out_sh...]
    ppermute x0 -> x16, waiting for transfers between devices: none -> 13.8 us  [the longest x14 11.9 us: swap_row(): return lax.ppermute(x, 'row', [(i, i ^ k) for i in range(n_row)])]
    all_gather x2 -> x0, blocking collectives: 4.65 us -> none  [the longest x1 2.47 us: body(): user_panel = lax.all_gather(users, 'col', axis=0, tiled=True)]
    convert_element_type x2 -> x1, other arithmetic: 2.73 us -> 0.07 us  [body(): parts = sums[0] + [swap_row(relay.astype(jnp.bfloat16), group)]]
  transfers between devices with their start and end apart: 3 -> 16, of which waited for: 3 -> 7; matrix products, arithmetic and copies ran while one was open for 2% -> 3% of each run, Pallas kernels for 0% -> 17%
where the time goes in v2:
time: 56.6 us; the launch traced here: 56.4 us
  starting transfers between devices  22.3 us (39%)
  Pallas kernels  16.7 us (30%)
  waiting for transfers between devices  13.8 us (24%)
  between operations  1.46 us (3%)
  local copies, waits for them, and re-layouts  1.41 us (2%)
  other arithmetic  0.73 us (1%)
    ppermute x14, starting transfers between devices, swap_row(): return lax.ppermute(x, 'row', [(i, i ^ k) for i in range(n_row)])  21.7 us
    ppermute x14, waiting for transfers between devices, swap_row(): return lax.ppermute(x, 'row', [(i, i ^ k) for i in range(n_row)])  11.9 us
    pallas_call x2, Pallas kernels, body(): pl.pallas_call(functools.partial(user_kernel, stage, group, last), out_sh...  5.68 us
    pallas_call x2, Pallas kernels, body(): pl.pallas_call(functools.partial(item_kernel, stage, group, first), out_s...  5.55 us
    pallas_call x1, Pallas kernels, body(): pl.pallas_call(functools.partial(plan_kernel, wide // BLOCK, group, stage...  4.62 us
    ppermute x2, waiting for transfers between devices, swap_col(): return lax.ppermute(x, 'col', [(i, i ^ 1) for i in range(n_col)])  1.9 us
  transfers between devices with their start and end apart: 16, of which 7 were waited for; matrix products, arithmetic and copies ran while one was open for 3% of the time, Pallas kernels for 17%

profile of v2, /device:TPU:0, one launch (start us, length us, event | category | flops | bytes accessed | tf_op | source)
XLA Modules:
  0.0 56.4 jit_solution(9211125939424584985)
XLA Ops:
  0.6 0.0 copy-start.1
  0.6 0.0 copy-start
  0.6 0.5 collective-permute-start
  1.2 3.7 %collective-permute-start.4 = (bf16[512,128]{1,0:T(8,128)(2,1)}, bf16[512,128]{1,0:T(8,128)(2,1)S(1)}, u32[]{:S(2)}, u32[]{:S(2)}) collective-permute-start(bf16[512,128]{1,0:T(8,128)(2,1)} %items.1), channel_id=1, source_target_pairs={{0,8},{2,10},{4,12},{6,14},{8,0},{10,2},{12,4},{14,6},{1,9},{3,11}... | collective-permute-start | bytes 393224 | tf_op jit(solution)/shard_map/ppermute | solution.py:196
  4.8 2.5 %collective-permute-start.3 = (bf16[512,128]{1,0:T(8,128)(2,1)}, bf16[512,128]{1,0:T(8,128)(2,1)S(1)}, u32[]{:S(2)}, u32[]{:S(2)}) collective-permute-start(bf16[512,128]{1,0:T(8,128)(2,1)} %items.1), channel_id=1, source_target_pairs={{0,6},{2,4},{4,2},{6,0},{8,14},{10,12},{12,10},{14,8},{1,7},{3,5},... | collective-permute-start | bytes 393224 | tf_op jit(solution)/shard_map/ppermute | solution.py:196
  7.4 0.4 collective-permute-start.2
  7.8 0.5 collective-permute-start.1
  9.0 3.1 %collective-permute-done.4.refs_4_ = bf16[512,128]{1,0:T(8,128)(2,1)S(1)} collective-permute-done((bf16[512,128]{1,0:T(8,128)(2,1)}, bf16[512,128]{1,0:T(8,128)(2,1)S(1)}, u32[]{:S(2)}, u32[]{:S(2)}) %collective-permute-start.4) | collective-permute-done | bytes 131104 | tf_op jit(solution)/shard_map/ppermute | solution.py:196
  12.0 1.7 %collective-permute-start.7 = (bf16[512,128]{1,0:T(8,128)(2,1)S(1)}, bf16[512,128]{1,0:T(8,128)(2,1)S(1)}, u32[]{:S(2)}, u32[]{:S(2)}) collective-permute-start(bf16[512,128]{1,0:T(8,128)(2,1)S(1)} %collective-permute-done.4.refs_4_), channel_id=1, source_target_pairs={{0,6},{2,4},{4,2},{6,0},{8,14},{10,12},{12,10},{14,8},{1,7},{3,5},... | collective-permute-start | bytes 393224 | tf_op jit(solution)/shard_map/ppermute | solution.py:196
  13.8 0.2 collective-permute-done.3.refs_9_
  14.0 1.2 %collective-permute-start.6 = (bf16[512,128]{1,0:T(8,128)(2,1)S(1)}, bf16[512,128]{1,0:T(8,128)(2,1)S(1)}, u32[]{:S(2)}, u32[]{:S(2)}) collective-permute-start(bf16[512,128]{1,0:T(8,128)(2,1)S(1)} %collective-permute-done.4.refs_4_), channel_id=1, source_target_pairs={{0,4},{2,6},{4,0},{6,2},{8,12},{10,14},{12,8},{14,10},{1,5},{3,7},... | collective-permute-start | bytes 393224 | tf_op jit(solution)/shard_map/ppermute | solution.py:196
  15.2 1.6 %collective-permute-done.2.refs_8_ = bf16[512,128]{1,0:T(8,128)(2,1)S(1)} collective-permute-done((bf16[512,128]{1,0:T(8,128)(2,1)}, bf16[512,128]{1,0:T(8,128)(2,1)S(1)}, u32[]{:S(2)}, u32[]{:S(2)}) %collective-permute-start.2) | collective-permute-done | bytes 131104 | tf_op jit(solution)/shard_map/ppermute | solution.py:196
  16.8 0.4 collective-permute-start.5
  17.2 0.7 %pad_add_fusion.info.refs_0_ = s32[3]{0:T(128)} fusion(s32[1]{0:T(128)} %bitcast.2, s32[1]{0:T(128)} %bitcast.1, s32[1]{0:T(128)} %bitcast.7), kind=kLoop, calls=%fused_computation.1 | loop fusion | flops 6 | bytes 24 | tf_op jit(solution)/shard_map/stack | solution.py:212
  17.9 4.6 %plan.1 = (s32[210]{0:T(256)}, bf16[192,128,128]{2,1,0:T(8,128)(2,1)S(1)}, s32[192,16,128]{2,1,0:T(8,128)S(1)}) custom-call(s32[3]{0:T(128)} %pad_add_fusion.info.refs_0_, s32[192]{0:T(256)} %bitcast.10, s32[192]{0:T(256)} %bitcast.11, bf16[192,128,128]{2,1,0:T(8,128)(2,1)} %bitcast.8, s32[192,16,128]{2,1,0:T(8,128)} %bitcast.9), custom_call_target="tpu_custom_call" | custom-call | tf_op jit(solution)/shard_map/plan/pallas_call | solution.py:213
  22.5 0.0 collective-permute-done.1.refs_7_
  22.5 0.0 collective-permute-done.refs_5_
  22.5 0.0 copy-done.1
  22.5 0.0 copy-done
  22.5 0.0 copy-done.3
  22.5 0.0 copy-start.2
  22.6 0.7 %copy-done.2 = s32[210]{0:T(256)S(1)} copy-done((s32[210]{0:T(256)S(1)}, s32[210]{0:T(256)}, u32[]{:S(2)}) %copy-start.2) | copy-done | bytes 864
  23.2 2.6 %user_terms.2 = (bf16[2048,128]{1,0:T(8,128)(2,1)S(1)}, bf16[2048,128]{1,0:T(8,128)(2,1)S(1)}, f32[2048,128]{1,0:T(8,128)S(1)}) custom-call(s32[3]{0:T(128)S(1)} %copy-done.3, s32[210]{0:T(256)S(1)} %copy-done.2, bf16[192,128,128]{2,1,0:T(8,128)(2,1)S(1)} %get-tuple-element.21.refs_2_.refs_1_, s32[192,16,128]{2,1,0:T(8,128)S(1)} %get-tuple-element.22.refs_3_.refs_2_, ...), custom_call_target="tpu_custom_call" | custom-call | flops 805306368 | bytes 6291456 | tf_op jit(solution)/shard_map/user_terms/pallas_call | solution.py:248
  25.9 0.0 collective-permute-done.7.refs_7_
  25.9 0.0 collective-permute-done.6.refs_6_
  25.9 0.0 collective-permute-done.5.refs_5_
  25.9 3.1 %user_terms.3 = (bf16[2048,128]{1,0:T(8,128)(2,1)S(1)}, f32[2048,128]{1,0:T(8,128)S(1)}, bf16[2048,128]{1,0:T(8,128)(2,1)S(1)}) custom-call(s32[210]{0:T(256)S(1)} %copy-done.2, bf16[192,128,128]{2,1,0:T(8,128)(2,1)S(1)} %get-tuple-element.21.refs_2_.refs_1_, s32[192,16,128]{2,1,0:T(8,128)S(1)} %get-tuple-element.22.refs_3_.refs_2_, ...), custom_call_target="tpu_custom_call", output_to_operand_aliasing={{1}: (8, {})} | custom-call | flops 805306368 | bytes 6291456 | tf_op jit(solution)/shard_map/user_terms/pallas_call | solution.py:248
  29.0 0.1 collective-permute-start.8
  29.0 1.9 %collective-permute-done.8.refs_4_ = bf16[2048,128]{1,0:T(8,128)(2,1)S(1)} collective-permute-done((bf16[2048,128]{1,0:T(8,128)(2,1)S(1)}, bf16[2048,128]{1,0:T(8,128)(2,1)S(1)}, u32[]{:S(2)}, u32[]{:S(2)}) %collective-permute-start.8) | collective-permute-done | bytes 524320 | tf_op jit(solution)/shard_map/ppermute | solution.py:199
  30.9 3.2 %item_terms.2 = (f32[512,128]{1,0:T(8,128)S(1)}, bf16[512,128]{1,0:T(8,128)(2,1)S(1)}, bf16[512,128]{1,0:T(8,128)(2,1)S(1)}, bf16[512,128]{1,0:T(8,128)(2,1)S(1)...) custom-call(s32[210]{0:T(256)S(1)} %copy-done.2, ...), custom_call_target="tpu_custom_call" | custom-call | flops 805306368 | bytes 6291456 | tf_op jit(solution)/shard_map/item_terms/pallas_call | solution.py:277
  34.2 3.1 %collective-permute-start.12 = (bf16[512,128]{1,0:T(8,128)(2,1)S(1)}, bf16[512,128]{1,0:T(8,128)(2,1)S(1)}, u32[]{:S(2)}, u32[]{:S(2)}) collective-permute-start(bf16[512,128]{1,0:T(8,128)(2,1)S(1)} %get-tuple-element.35), channel_id=1, source_target_pairs={{0,2},{2,0},{4,6},{6,4},{8,10},{10,8},{12,14},{14,12},{1,3},{3,1},... | collective-permute-start | bytes 393224 | tf_op jit(solution)/shard_map/ppermute | solution.py:196
  37.3 2.8 %collective-permute-start.13 = (bf16[512,128]{1,0:T(8,128)(2,1)S(1)}, bf16[512,128]{1,0:T(8,128)(2,1)S(1)}, u32[]{:S(2)}, u32[]{:S(2)}) collective-permute-start(bf16[512,128]{1,0:T(8,128)(2,1)S(1)} %get-tuple-element.36), channel_id=1, source_target_pairs={{0,4},{2,6},{4,0},{6,2},{8,12},{10,14},{12,8},{14,10},{1,5},{3,7},... | collective-permute-start | bytes 393224 | tf_op jit(solution)/shard_map/ppermute | solution.py:196
  40.1 0.0 collective-permute-start.14
  40.1 2.3 %item_terms.3 = (f32[512,128]{1,0:T(8,128)S(1)}, bf16[512,128]{1,0:T(8,128)(2,1)S(1)}, bf16[512,128]{1,0:T(8,128)(2,1)S(1)}, bf16[512,128]{1,0:T(8,128)(2,1)S(1)}) custom-call(s32[210]{0:T(256)S(1)} %copy-done.2, bf16[192,128,128]{2,1,0:T(8,128)(2,1)S(1)} %get-tuple-element.21.refs_2_.refs_1_, s32[192,16,128]{2,1,0:T(8,128)S(1)} %get-tuple-element.22.refs_3_.refs_2_, ...), custom_call_target="tpu_custom_call" | custom-call | flops 805306368 | bytes 6291456 | tf_op jit(solution)/shard_map/item_terms/pallas_call | solution.py:277
  42.4 2.1 %collective-permute-start.9 = (bf16[512,128]{1,0:T(8,128)(2,1)S(1)}, bf16[512,128]{1,0:T(8,128)(2,1)S(1)}, u32[]{:S(2)}, u32[]{:S(2)}) collective-permute-start(bf16[512,128]{1,0:T(8,128)(2,1)S(1)} %get-tuple-element.31), channel_id=1, source_target_pairs={{0,2},{2,0},{4,6},{6,4},{8,10},{10,8},{12,14},{14,12},{1,3},{3,1},... | collective-permute-start | bytes 393224 | tf_op jit(solution)/shard_map/ppermute | solution.py:196
  44.5 3.1 %collective-permute-start.10 = (bf16[512,128]{1,0:T(8,128)(2,1)S(1)}, bf16[512,128]{1,0:T(8,128)(2,1)S(1)}, u32[]{:S(2)}, u32[]{:S(2)}) collective-permute-start(bf16[512,128]{1,0:T(8,128)(2,1)S(1)} %get-tuple-element.32), channel_id=1, source_target_pairs={{0,4},{2,6},{4,0},{6,2},{8,12},{10,14},{12,8},{14,10},{1,5},{3,7},... | collective-permute-start | bytes 393224 | tf_op jit(solution)/shard_map/ppermute | solution.py:196
  47.6 0.0 collective-permute-done.12
  47.6 0.0 collective-permute-start.11
  47.6 0.0 collective-permute-done.13
  47.6 0.0 collective-permute-done.14
  47.6 0.1 add_convert_fusion
  47.7 0.1 collective-permute-start.15
  47.8 0.7 %constant_dynamic-slice_fusion = bf16[1024,128]{1,0:T(8,128)(2,1)} fusion(bf16[2048,128]{1,0:T(8,128)(2,1)S(1)} %get-tuple-element.27.refs_3_, s32[]{:T(128)S(6)} %select_n.3), kind=kLoop, calls=%fused_computation.2 | loop fusion | bytes 524292 | tf_op jit(solution)/shard_map/dynamic_slice | solution.py:290
  48.5 0.9 %collective-permute-done.9.refs_1_ = bf16[512,128]{1,0:T(8,128)(2,1)S(1)} collective-permute-done((bf16[512,128]{1,0:T(8,128)(2,1)S(1)}, bf16[512,128]{1,0:T(8,128)(2,1)S(1)}, u32[]{:S(2)}, u32[]{:S(2)}) %collective-permute-start.9) | collective-permute-done | bytes 131104 | tf_op jit(solution)/shard_map/ppermute | solution.py:196
  49.4 5.3 %collective-permute-done.10.refs_2_ = bf16[512,128]{1,0:T(8,128)(2,1)S(1)} collective-permute-done((bf16[512,128]{1,0:T(8,128)(2,1)S(1)}, bf16[512,128]{1,0:T(8,128)(2,1)S(1)}, u32[]{:S(2)}, u32[]{:S(2)}) %collective-permute-start.10) | collective-permute-done | bytes 131104 | tf_op jit(solution)/shard_map/ppermute | solution.py:196
  54.7 0.8 %collective-permute-done.11.refs_3_ = bf16[512,128]{1,0:T(8,128)(2,1)S(1)} collective-permute-done((bf16[512,128]{1,0:T(8,128)(2,1)S(1)}, bf16[512,128]{1,0:T(8,128)(2,1)S(1)}, u32[]{:S(2)}, u32[]{:S(2)}) %collective-permute-start.11) | collective-permute-done | bytes 131104 | tf_op jit(solution)/shard_map/ppermute | solution.py:196
  55.6 0.0 collective-permute-done.15.refs_4_
  55.6 0.8 %finish.1 = bf16[512,128]{1,0:T(8,128)(2,1)} custom-call(bf16[512,128]{1,0:T(8,128)(2,1)S(1)} %copy-done, f32[512,128]{1,0:T(8,128)S(1)} %get-tuple-element.30.refs_0_, bf16[512,128]{1,0:T(8,128)(2,1)S(1)} %collective-permute-done.9.refs_1_, bf16[512,128]{1,0:T(8,128)(2,1)S(1)} %collective-permute-done.10.refs_2_, ...), custom_call_target="tpu_custom_call" | custom-call | tf_op jit(solution)/shard_map/finish/pallas_call | solution.py:297
  (1 shorter events, 0.0 us)
Async XLA Ops:
  0.6 21.9 %copy-start.1 = (bf16[1024,128]{1,0:T(8,128)(2,1)S(1)}, bf16[1024,128]{1,0:T(8,128)(2,1)}, u32[]{:S(2)}) copy-start(bf16[1024,128]{1,0:T(8,128)(2,1)} %refs_4_.1) | copy-start | bytes 786436
  0.6 21.9 %copy-start = (bf16[512,128]{1,0:T(8,128)(2,1)S(1)}, bf16[512,128]{1,0:T(8,128)(2,1)}, u32[]{:S(2)}) copy-start(bf16[512,128]{1,0:T(8,128)(2,1)} %items.1) | copy-start | bytes 393220
  0.6 21.9 %collective-permute-start = (bf16[1024,128]{1,0:T(8,128)(2,1)}, bf16[1024,128]{1,0:T(8,128)(2,1)S(1)}, u32[]{:S(2)}, u32[]{:S(2)}) collective-permute-start(bf16[1024,128]{1,0:T(8,128)(2,1)} %refs_4_.1), channel_id=1, source_target_pairs={{0,1},{1,0},{2,3},{3,2},{4,5},{5,4},{6,7},{7,6},{8,9},{9,8},{10,11... | collective-permute-start | bytes 786440 | tf_op jit(solution)/shard_map/ppermute | solution.py:199
  1.2 10.9 %collective-permute-start.4 = (bf16[512,128]{1,0:T(8,128)(2,1)}, bf16[512,128]{1,0:T(8,128)(2,1)S(1)}, u32[]{:S(2)}, u32[]{:S(2)}) collective-permute-start(bf16[512,128]{1,0:T(8,128)(2,1)} %items.1), channel_id=1, source_target_pairs={{0,8},{2,10},{4,12},{6,14},{8,0},{10,2},{12,4},{14,6},{1,9},{3,11}... | collective-permute-start | bytes 393224 | tf_op jit(solution)/shard_map/ppermute | solution.py:196
  4.8 9.1 %collective-permute-start.3 = (bf16[512,128]{1,0:T(8,128)(2,1)}, bf16[512,128]{1,0:T(8,128)(2,1)S(1)}, u32[]{:S(2)}, u32[]{:S(2)}) collective-permute-start(bf16[512,128]{1,0:T(8,128)(2,1)} %items.1), channel_id=1, source_target_pairs={{0,6},{2,4},{4,2},{6,0},{8,14},{10,12},{12,10},{14,8},{1,7},{3,5},... | collective-permute-start | bytes 393224 | tf_op jit(solution)/shard_map/ppermute | solution.py:196
  7.4 9.4 %collective-permute-start.2 = (bf16[512,128]{1,0:T(8,128)(2,1)}, bf16[512,128]{1,0:T(8,128)(2,1)S(1)}, u32[]{:S(2)}, u32[]{:S(2)}) collective-permute-start(bf16[512,128]{1,0:T(8,128)(2,1)} %items.1), channel_id=1, source_target_pairs={{0,4},{2,6},{4,0},{6,2},{8,12},{10,14},{12,8},{14,10},{1,5},{3,7},... | collective-permute-start | bytes 393224 | tf_op jit(solution)/shard_map/ppermute | solution.py:196
  7.8 14.7 %collective-permute-start.1 = (bf16[512,128]{1,0:T(8,128)(2,1)}, bf16[512,128]{1,0:T(8,128)(2,1)S(1)}, u32[]{:S(2)}, u32[]{:S(2)}) collective-permute-start(bf16[512,128]{1,0:T(8,128)(2,1)} %items.1), channel_id=1, source_target_pairs={{0,2},{2,0},{4,6},{6,4},{8,10},{10,8},{12,14},{14,12},{1,3},{3,1},... | collective-permute-start | bytes 393224 | tf_op jit(solution)/shard_map/ppermute | solution.py:196
  12.0 13.8 %collective-permute-start.7 = (bf16[512,128]{1,0:T(8,128)(2,1)S(1)}, bf16[512,128]{1,0:T(8,128)(2,1)S(1)}, u32[]{:S(2)}, u32[]{:S(2)}) collective-permute-start(bf16[512,128]{1,0:T(8,128)(2,1)S(1)} %collective-permute-done.4.refs_4_), channel_id=1, source_target_pairs={{0,6},{2,4},{4,2},{6,0},{8,14},{10,12},{12,10},{14,8},{1,7},{3,5},... | collective-permute-start | bytes 393224 | tf_op jit(solution)/shard_map/ppermute | solution.py:196
  14.0 11.9 %collective-permute-start.6 = (bf16[512,128]{1,0:T(8,128)(2,1)S(1)}, bf16[512,128]{1,0:T(8,128)(2,1)S(1)}, u32[]{:S(2)}, u32[]{:S(2)}) collective-permute-start(bf16[512,128]{1,0:T(8,128)(2,1)S(1)} %collective-permute-done.4.refs_4_), channel_id=1, source_target_pairs={{0,4},{2,6},{4,0},{6,2},{8,12},{10,14},{12,8},{14,10},{1,5},{3,7},... | collective-permute-start | bytes 393224 | tf_op jit(solution)/shard_map/ppermute | solution.py:196
  16.8 9.1 %collective-permute-start.5 = (bf16[512,128]{1,0:T(8,128)(2,1)S(1)}, bf16[512,128]{1,0:T(8,128)(2,1)S(1)}, u32[]{:S(2)}, u32[]{:S(2)}) collective-permute-start(bf16[512,128]{1,0:T(8,128)(2,1)S(1)} %collective-permute-done.4.refs_4_), channel_id=1, source_target_pairs={{0,2},{2,0},{4,6},{6,4},{8,10},{10,8},{12,14},{14,12},{1,3},{3,1},... | collective-permute-start | bytes 393224 | tf_op jit(solution)/shard_map/ppermute | solution.py:196
  17.9 4.7 %copy-start.3 = (s32[3]{0:T(128)S(1)}, s32[3]{0:T(128)}, u32[]{:S(2)}) copy-start(s32[3]{0:T(128)} %pad_add_fusion.info.refs_0_) | copy-start | bytes 40
  22.5 0.7 %copy-start.2 = (s32[210]{0:T(256)S(1)}, s32[210]{0:T(256)}, u32[]{:S(2)}) copy-start(s32[210]{0:T(256)} %get-tuple-element.20.refs_1_.refs_0_) | copy-start | bytes 2524
  29.0 2.0 %collective-permute-start.8 = (bf16[2048,128]{1,0:T(8,128)(2,1)S(1)}, bf16[2048,128]{1,0:T(8,128)(2,1)S(1)}, u32[]{:S(2)}, u32[]{:S(2)}) collective-permute-start(bf16[2048,128]{1,0:T(8,128)(2,1)S(1)} %get-tuple-element.25.refs_3_), channel_id=1, source_target_pairs={{0,1},{1,0},{2,3},{3,2},{4,5},{5,4},{6,7},{7,6},{8,9},{9,8},{10,11... | collective-permute-start | bytes 1572872 | tf_op jit(solution)/shard_map/ppermute | solution.py:199
  34.2 13.4 %collective-permute-start.12 = (bf16[512,128]{1,0:T(8,128)(2,1)S(1)}, bf16[512,128]{1,0:T(8,128)(2,1)S(1)}, u32[]{:S(2)}, u32[]{:S(2)}) collective-permute-start(bf16[512,128]{1,0:T(8,128)(2,1)S(1)} %get-tuple-element.35), channel_id=1, source_target_pairs={{0,2},{2,0},{4,6},{6,4},{8,10},{10,8},{12,14},{14,12},{1,3},{3,1},... | collective-permute-start | bytes 393224 | tf_op jit(solution)/shard_map/ppermute | solution.py:196
  37.3 10.3 %collective-permute-start.13 = (bf16[512,128]{1,0:T(8,128)(2,1)S(1)}, bf16[512,128]{1,0:T(8,128)(2,1)S(1)}, u32[]{:S(2)}, u32[]{:S(2)}) collective-permute-start(bf16[512,128]{1,0:T(8,128)(2,1)S(1)} %get-tuple-element.36), channel_id=1, source_target_pairs={{0,4},{2,6},{4,0},{6,2},{8,12},{10,14},{12,8},{14,10},{1,5},{3,7},... | collective-permute-start | bytes 393224 | tf_op jit(solution)/shard_map/ppermute | solution.py:196
  40.1 7.6 %collective-permute-start.14 = (bf16[512,128]{1,0:T(8,128)(2,1)S(1)}, bf16[512,128]{1,0:T(8,128)(2,1)S(1)}, u32[]{:S(2)}, u32[]{:S(2)}) collective-permute-start(bf16[512,128]{1,0:T(8,128)(2,1)S(1)} %get-tuple-element.37), channel_id=1, source_target_pairs={{0,6},{2,4},{4,2},{6,0},{8,14},{10,12},{12,10},{14,8},{1,7},{3,5},... | collective-permute-start | bytes 393224 | tf_op jit(solution)/shard_map/ppermute | solution.py:196
  42.4 7.0 %collective-permute-start.9 = (bf16[512,128]{1,0:T(8,128)(2,1)S(1)}, bf16[512,128]{1,0:T(8,128)(2,1)S(1)}, u32[]{:S(2)}, u32[]{:S(2)}) collective-permute-start(bf16[512,128]{1,0:T(8,128)(2,1)S(1)} %get-tuple-element.31), channel_id=1, source_target_pairs={{0,2},{2,0},{4,6},{6,4},{8,10},{10,8},{12,14},{14,12},{1,3},{3,1},... | collective-permute-start | bytes 393224 | tf_op jit(solution)/shard_map/ppermute | solution.py:196
  44.5 10.3 %collective-permute-start.10 = (bf16[512,128]{1,0:T(8,128)(2,1)S(1)}, bf16[512,128]{1,0:T(8,128)(2,1)S(1)}, u32[]{:S(2)}, u32[]{:S(2)}) collective-permute-start(bf16[512,128]{1,0:T(8,128)(2,1)S(1)} %get-tuple-element.32), channel_id=1, source_target_pairs={{0,4},{2,6},{4,0},{6,2},{8,12},{10,14},{12,8},{14,10},{1,5},{3,7},... | collective-permute-start | bytes 393224 | tf_op jit(solution)/shard_map/ppermute | solution.py:196
  47.6 8.0 %collective-permute-start.11 = (bf16[512,128]{1,0:T(8,128)(2,1)S(1)}, bf16[512,128]{1,0:T(8,128)(2,1)S(1)}, u32[]{:S(2)}, u32[]{:S(2)}) collective-permute-start(bf16[512,128]{1,0:T(8,128)(2,1)S(1)} %get-tuple-element.33), channel_id=1, source_target_pairs={{0,6},{2,4},{4,2},{6,0},{8,14},{10,12},{12,10},{14,8},{1,7},{3,5},... | collective-permute-start | bytes 393224 | tf_op jit(solution)/shard_map/ppermute | solution.py:196
  47.7 7.9 %collective-permute-start.15 = (bf16[512,128]{1,0:T(8,128)(2,1)S(1)}, bf16[512,128]{1,0:T(8,128)(2,1)S(1)}, u32[]{:S(2)}, u32[]{:S(2)}) collective-permute-start(bf16[512,128]{1,0:T(8,128)(2,1)S(1)} %add_convert_fusion), channel_id=1, source_target_pairs={{0,8},{2,10},{4,12},{6,14},{8,0},{10,2},{12,4},{14,6},{1,9},{3,11}... | collective-permute-start | bytes 393224 | tf_op jit(solution)/shard_map/ppermute | solution.py:196

commit v3 on v2

--- a/solution.py
+++ b/solution.py
@@ -10,6 +10,7 @@
 BLOCK = 128
 UNROLL = 16
 FIELD = 10
+PLAN_UNROLL = 8
 VMEM_LIMIT = 16 * 1024 * 1024
 PLAN_LIMIT = 50 * 1024 * 1024
 
@@ -36,35 +37,38 @@
     return slice(index * BLOCK, (index + 1) * BLOCK)
 
 
-def plan_kernel(
-    shard_tiles, group, stages, info, rows, cols, ratings, observed, meta, tiles, words, sems
-):
-    copy_tiles = pltpu.make_async_copy(ratings, tiles, sems.at[0])
-    copy_words = pltpu.make_async_copy(observed, words, sems.at[1])
-    copy_tiles.start()
-    copy_words.start()
-    count = info[0]
-    me = info[1]
+def plan_kernel(shard_tiles, group, stages, live, rows, cols, meta):
+    count = live[0, 0]
+    me = lax.axis_index("row")
     ends = meta.shape[0] - 2
-
-    def put(t, places):
+    spare = meta.shape[0] - 3
+
+    def put(i, places):
         low, high = places
-        v = cols[t]
-        near = jnp.int32(1)
-        if stages > 1:
-            key = jnp.bitwise_xor(v // shard_tiles, me)
-            near = jnp.where(key < group, 1, 0)
-            v = (key % group) * shard_tiles + v % shard_tiles
-        meta[jnp.where(near == 1, low, high)] = t + (rows[t] << FIELD) + (v << 2 * FIELD)
-        return low + near, high - 1 + near
-
-    low, _ = lax.fori_loop(0, count, put, (jnp.int32(0), count - 1))
+        packed = []
+        for j in range(PLAN_UNROLL):
+            t = i * PLAN_UNROLL + j
+            at = jnp.minimum(t, rows.shape[0] - 1)
+            v = cols[at]
+            near = jnp.int32(1)
+            if stages > 1:
+                key = (v ^ (me * shard_tiles)) & (2 * group * shard_tiles - 1)
+                near = jnp.where(key < (group + 1) * shard_tiles, 1, 0)
+                v = jnp.where(near == 1, key, key - (group + 1) * shard_tiles)
+            packed.append((t, near, at + (rows[at] << FIELD) + (v << 2 * FIELD)))
+        for t, near, word in packed:
+            live = jnp.where(t < count, 1, 0)
+            meta[jnp.where(live == 0, spare, jnp.where(near == 1, low, high))] = word
+            low = low + near * live
+            high = high - (1 - near) * live
+        return low, high
+
+    trips = (count + PLAN_UNROLL - 1) // PLAN_UNROLL
+    low, _ = lax.fori_loop(0, trips, put, (jnp.int32(0), count - 1))
     for at in range(UNROLL):
         meta[count + at] = 0
     meta[ends] = low
     meta[ends + 1] = count
-    copy_tiles.wait()
-    copy_words.wait()
 
 
 def stage_loop(stage, meta, step_of):
@@ -109,11 +113,11 @@
 
 def user_kernel(stage, group, last, *refs):
     if stage == 0:
-        info, meta, tiles, words, mine, theirs = refs[:6]
-        shards = refs[6 : 6 + group]
-        users, flipped, total = refs[6 + group : 9 + group]
+        meta, tiles, words, mine, theirs = refs[:5]
+        shards = refs[5 : 5 + group]
+        users, flipped, total = refs[5 + group : 8 + group]
         count = mine.shape[0]
-        lead = info[2] == 0
+        lead = lax.axis_index("col") == 0
         users[:count] = jnp.where(lead, mine[...], theirs[...])
         users[count:] = jnp.where(lead, theirs[...], mine[...])
         total[...] = jnp.zeros_like(total)
@@ -186,10 +190,11 @@
     slots = tiles.shape[0]
     rank = users.shape[-1]
     pad = slots + UNROLL
-    direct = items.shape[0] % BLOCK == 0 and n_row & (n_row - 1) == 0 and n_row > 1
+    per = items.shape[0] // BLOCK
+    direct = items.shape[0] == per * BLOCK and n_row > 2
+    direct = direct and (n_row & (n_row - 1)) == 0 and (per & (per - 1)) == 0
     stages = 2 if direct else 1
     group = n_row // 2 if direct else 1
-    row_at = lax.axis_index("row")
     col_at = lax.axis_index("col")
 
     def swap_row(x, k):
@@ -201,42 +206,40 @@
     peer_users = swap_col(users)
     if direct:
         crossed = swap_row(items, group)
-        shards = [
-            [items] + [swap_row(items, k) for k in range(1, group)],
-            [crossed] + [swap_row(crossed, k) for k in range(1, group)],
-        ]
+        shards = [[items] + [swap_row(items, k) for k in range(1, group)]]
     else:
         shards = [[lax.all_gather(items, "row", axis=0, tiled=True)]]
     wide = shards[0][0].shape[0]
 
-    info = jnp.stack([tile_count[0, 0], row_at, col_at]).astype(jnp.int32)
-    meta, tiles, words = pl.pallas_call(
+    meta = pl.pallas_call(
         functools.partial(plan_kernel, wide // BLOCK, group, stages),
-        out_shape=(
-            jax.ShapeDtypeStruct((pad + 2,), jnp.int32),
-            pltpu.VMEM(tiles.shape, tiles.dtype),
-            pltpu.VMEM(words.shape, words.dtype),
-        ),
-        in_specs=[smem()] * 3 + [anywhere()] * 2,
-        out_specs=(smem(), vmem(), vmem()),
-        scratch_shapes=[pltpu.SemaphoreType.DMA((2,))],
-        compiler_params=params(PLAN_LIMIT),
+        out_shape=pltpu.SMEM((pad + 3,), jnp.int32),
+        in_specs=[smem()] * 3,
+        out_specs=smem(),
+        compiler_params=params(),
+        cost_estimate=pl.CostEstimate(flops=10**10, bytes_accessed=0, transcendentals=0),
         name="plan",
-    )(info, tile_rows[0, 0], tile_cols[0, 0], tiles, words)
+    )(tile_count, tile_rows[0, 0], tile_cols[0, 0])
+
+    if direct:
+        crossed, meta = lax.optimization_barrier((crossed, meta))
+        shards[0].append(crossed)
+        shards.append([swap_row(crossed, k) for k in range(1, group)])
 
     cost = pl.CostEstimate(
-        flops=4 * slots * BLOCK * BLOCK * rank // stages,
+        flops=20 * slots * BLOCK * BLOCK * rank // stages,
         bytes_accessed=(slots // stages) * BLOCK * BLOCK * 4,
         transcendentals=0,
     )
     user_shape = (n_col * users.shape[0], rank)
-    panel_shape = (group * wide, rank)
     flipped = []
     for stage in range(stages):
+        size = len(shards[stage])
+        panel_shape = (size * wide, rank)
         last = stage == stages - 1
         shapes = [pltpu.VMEM(panel_shape, jnp.bfloat16), pltpu.VMEM(user_shape, jnp.float32)]
         if stage == 0:
-            operands = [info, meta, tiles, words, users, peer_users] + shards[0]
+            operands = [meta, tiles, words, users, peer_users] + shards[0]
             shapes = [pltpu.VMEM(user_shape, jnp.bfloat16)] + shapes
             aliases = {}
         else:
@@ -244,11 +247,10 @@
             aliases = {len(operands) - 1: 1}
         if last:
             shapes.append(jax.ShapeDtypeStruct(user_shape, jnp.bfloat16))
-        scalars = 2 if stage == 0 else 1
         outs = list(pl.pallas_call(
-            functools.partial(user_kernel, stage, group, last),
+            functools.partial(user_kernel, stage, size, last),
             out_shape=tuple(shapes),
-            in_specs=[smem()] * scalars + [vmem()] * (len(operands) - scalars),
+            in_specs=[smem()] + [vmem()] * (len(operands) - 1),
             out_specs=tuple([vmem()] * len(shapes)),
             input_output_aliases=aliases,
             scratch_shapes=[pltpu.VMEM(panel_shape, jnp.bfloat16)],
@@ -264,36 +266,41 @@
     peer_terms = swap_col(terms)
 
     fresh = turned = None
-    sums = [None] * stages
     for stage in range(stages - 1, -1, -1):
         first = fresh is None
-        shapes = [jax.ShapeDtypeStruct((wide, rank), jnp.float32)]
-        shapes += [jax.ShapeDtypeStruct((wide, rank), jnp.bfloat16)] * (group - 1)
+        size = len(shards[stage])
+        kinds = [jnp.bfloat16] * size
+        if stage == 0:
+            kinds[0] = kinds[-1] = jnp.float32
+        shapes = [jax.ShapeDtypeStruct((wide, rank), kind) for kind in kinds]
         if first:
             operands = [meta, tiles, words, terms, peer_terms, panel, flipped[stage]]
             shapes += [pltpu.VMEM(user_shape, jnp.bfloat16)] * 2
         else:
             operands = [meta, tiles, words, fresh, turned, flipped[stage]]
         outs = pl.pallas_call(
-            functools.partial(item_kernel, stage, group, first),
+            functools.partial(item_kernel, stage, size, first),
             out_shape=tuple(shapes),
             in_specs=[smem()] + [vmem()] * (len(operands) - 1),
             out_specs=tuple([vmem()] * len(shapes)),
-            scratch_shapes=[pltpu.VMEM(panel_shape, jnp.float32)],
+            scratch_shapes=[pltpu.VMEM((size * wide, rank), jnp.float32)],
             compiler_params=params(),
             cost_estimate=cost,
             name="item_terms",
         )(*operands)
         if first:
-            fresh, turned = outs[group:]
-        sums[stage] = [outs[0]] + [swap_row(outs[k], k) for k in range(1, group)]
+            fresh, turned = outs[size:]
+        if stage:
+            far = [swap_row(out, k + 1) for k, out in enumerate(outs[:size])]
+        else:
+            near = [outs[0]] + [swap_row(outs[k], k) for k in range(1, group)]
+            relay = outs[size - 1]
     users_new = lax.dynamic_slice_in_dim(fresh, col_at * users.shape[0], users.shape[0], 0)
 
     if direct:
-        relay = sums[1][0]
-        for part in sums[1][1:]:
+        for part in far:
             relay = relay + part.astype(jnp.float32)
-        parts = sums[0] + [swap_row(relay.astype(jnp.bfloat16), group)]
+        parts = near + [swap_row(relay.astype(jnp.bfloat16), group)]
         items_new = pl.pallas_call(
             finish_kernel,
             out_shape=jax.ShapeDtypeStruct(items.shape, jnp.bfloat16),
@@ -303,7 +310,7 @@
             name="finish",
         )(items, *parts)
     else:
-        turned_terms = jnp.swapaxes(sums[0][0].reshape(-1, BLOCK, BLOCK), 1, 2)
+        turned_terms = jnp.swapaxes(near[0].reshape(-1, BLOCK, BLOCK), 1, 2)
         item_grad = lax.psum_scatter(
             turned_terms.reshape(wide, rank), "row", scatter_dimension=0, tiled=True
         )

time: 56.6 us -> 51.1 us (0.903)
  Pallas kernels: 16.7 us -> 12.9 us
  waiting for transfers between devices: 13.8 us -> 11.5 us
  local copies, waits for them, and re-layouts: 1.41 us -> 2.08 us
  other arithmetic: 0.73 us -> 0.07 us
    pallas_call x1, Pallas kernels: 4.62 us -> 1.89 us  [body(): pl.pallas_call(functools.partial(plan_kernel, wide // BLOCK, group, stage...]
    ppermute x14, waiting for transfers between devices: 11.9 us -> 9.57 us  [swap_row(): return lax.ppermute(x, 'row', [(i, i ^ k) for i in range(n_row)])]
    pallas_call x4, Pallas kernels: 11.2 us -> 10.2 us  [the longest x2 5.16 us: body(): pl.pallas_call(functools.partial(user_kernel, stage, size, last), out_sha...]
    ppermute x14, starting transfers between devices: 21.7 us -> 22.5 us  [swap_row(): return lax.ppermute(x, 'row', [(i, i ^ k) for i in range(n_row)])]
    unnamed x8 -> x12, local copies, waits for them, and re-layouts: 0.69 us -> 1.37 us
    another operation x1 -> x0, other arithmetic: 0.67 us -> none  [body(): info = jnp.stack([tile_count[0, 0], row_at, col_at]).astype(jnp.int32)]
  transfers between devices with their start and end apart: 16 -> 16, of which waited for: 7 -> 7; matrix products, arithmetic and copies ran while one was open for 3% -> 2% of each run, Pallas kernels for 17% -> 16%
where the time goes in v3:
time: 51.1 us; the launch traced here: 50.6 us
  starting transfers between devices  22.6 us (44%)
  Pallas kernels  12.9 us (25%)
  waiting for transfers between devices  11.5 us (23%)
  local copies, waits for them, and re-layouts  2.08 us (4%)
  between operations  1.43 us (3%)
    ppermute x14, starting transfers between devices, swap_row(): return lax.ppermute(x, 'row', [(i, i ^ k) for i in range(n_row)])  22.5 us
    ppermute x14, waiting for transfers between devices, swap_row(): return lax.ppermute(x, 'row', [(i, i ^ k) for i in range(n_row)])  9.57 us
    pallas_call x2, Pallas kernels, body(): pl.pallas_call(functools.partial(user_kernel, stage, size, last), out_sha...  5.16 us
    pallas_call x2, Pallas kernels, body(): pl.pallas_call(functools.partial(item_kernel, stage, size, first), out_sh...  5.07 us
    ppermute x2, waiting for transfers between devices, swap_col(): return lax.ppermute(x, 'col', [(i, i ^ 1) for i in range(n_col)])  1.9 us
    pallas_call x1, Pallas kernels, body(): pl.pallas_call(functools.partial(plan_kernel, wide // BLOCK, group, stage...  1.89 us
    unnamed x12, local copies, waits for them, and re-layouts  1.37 us
  transfers between devices with their start and end apart: 16, of which 7 were waited for; matrix products, arithmetic and copies ran while one was open for 2% of the time, Pallas kernels for 16%

profile of v3, /device:TPU:0, one launch (start us, length us, event | category | flops | bytes accessed | tf_op | source)
XLA Modules:
  0.0 50.6 jit_solution(13927386452932675958)
XLA Ops:
  0.6 4.1 %collective-permute-start = (bf16[512,128]{1,0:T(8,128)(2,1)}, bf16[512,128]{1,0:T(8,128)(2,1)S(1)}, u32[]{:S(2)}, u32[]{:S(2)}) collective-permute-start(bf16[512,128]{1,0:T(8,128)(2,1)} %items.1), channel_id=1, source_target_pairs={{0,8},{2,10},{4,12},{6,14},{8,0},{10,2},{12,4},{14,6},{1,9},{3,11}... | collective-permute-start | bytes 393224 | tf_op jit(solution)/shard_map/ppermute | solution.py:201
  4.7 1.5 %collective-permute-start.2 = (bf16[512,128]{1,0:T(8,128)(2,1)}, bf16[512,128]{1,0:T(8,128)(2,1)S(1)}, u32[]{:S(2)}, u32[]{:S(2)}) collective-permute-start(bf16[512,128]{1,0:T(8,128)(2,1)} %items.1), channel_id=1, source_target_pairs={{0,2},{2,0},{4,6},{6,4},{8,10},{10,8},{12,14},{14,12},{1,3},{3,1},... | collective-permute-start | bytes 393224 | tf_op jit(solution)/shard_map/ppermute | solution.py:201
  6.3 1.6 %collective-permute-start.3 = (bf16[512,128]{1,0:T(8,128)(2,1)}, bf16[512,128]{1,0:T(8,128)(2,1)S(1)}, u32[]{:S(2)}, u32[]{:S(2)}) collective-permute-start(bf16[512,128]{1,0:T(8,128)(2,1)} %items.1), channel_id=1, source_target_pairs={{0,4},{2,6},{4,0},{6,2},{8,12},{10,14},{12,8},{14,10},{1,5},{3,7},... | collective-permute-start | bytes 393224 | tf_op jit(solution)/shard_map/ppermute | solution.py:201
  7.8 0.4 collective-permute-start.4
  8.2 0.0 collective-permute-start.1
  8.9 0.0 copy-start.4
  8.9 0.7 %copy-done.4 = s32[1,1,192]{2,1,0:T(1,128)S(1)} copy-done((s32[1,1,192]{2,1,0:T(1,128)S(1)}, s32[1,1,192]{2,1,0:T(1,128)}, u32[]{:S(2)}) %copy-start.4) | copy-done | bytes 792
  9.6 0.0 copy-start.5
  9.6 0.7 %copy-done.5 = s32[1,1,192]{2,1,0:T(1,128)S(1)} copy-done((s32[1,1,192]{2,1,0:T(1,128)S(1)}, s32[1,1,192]{2,1,0:T(1,128)}, u32[]{:S(2)}) %copy-start.5) | copy-done | bytes 792
  10.2 1.9 %plan.1.refs_0_ = s32[211]{0:T(256)S(4)} custom-call(s32[1,1]{1,0:T(1,128)S(6)} %copy.11.live, s32[192]{0:T(256)S(1)} %bitcast.12, s32[192]{0:T(256)S(1)} %bitcast.13), custom_call_target="tpu_custom_call" | custom-call | flops 10000000000 | tf_op jit(solution)/shard_map/plan/pallas_call | solution.py:214
  12.1 0.0 collective-permute-done.refs_9_
  12.2 2.4 %collective-permute-start.5 = (bf16[512,128]{1,0:T(8,128)(2,1)S(1)}, bf16[512,128]{1,0:T(8,128)(2,1)S(1)}, u32[]{:S(2)}, u32[]{:S(2)}) collective-permute-start(bf16[512,128]{1,0:T(8,128)(2,1)S(1)} %collective-permute-done.refs_9_), channel_id=1, source_target_pairs={{0,2},{2,0},{4,6},{6,4},{8,10},{10,8},{12,14},{14,12},{1,3},{3,1},... | collective-permute-start | bytes 393224 | tf_op jit(solution)/shard_map/ppermute | solution.py:201
  14.5 0.0 collective-permute-done.2.refs_6_
  14.5 0.2 collective-permute-start.6
  14.7 0.0 collective-permute-done.3.refs_7_
  14.7 1.4 %collective-permute-start.7 = (bf16[512,128]{1,0:T(8,128)(2,1)S(1)}, bf16[512,128]{1,0:T(8,128)(2,1)S(1)}, u32[]{:S(2)}, u32[]{:S(2)}) collective-permute-start(bf16[512,128]{1,0:T(8,128)(2,1)S(1)} %collective-permute-done.refs_9_), channel_id=1, source_target_pairs={{0,6},{2,4},{4,2},{6,0},{8,14},{10,12},{12,10},{14,8},{1,7},{3,5},... | collective-permute-start | bytes 393224 | tf_op jit(solution)/shard_map/ppermute | solution.py:201
  16.1 0.0 collective-permute-done.4.refs_8_
  16.1 0.0 collective-permute-done.1.refs_4_
  16.1 0.0 copy-done
  16.1 0.0 copy-done.1
  16.1 0.0 copy-done.2
  16.1 0.0 copy-done.3
  16.1 3.2 %user_terms.2 = (bf16[2048,128]{1,0:T(8,128)(2,1)S(1)}, bf16[2560,128]{1,0:T(8,128)(2,1)S(1)}, f32[2048,128]{1,0:T(8,128)S(1)}) custom-call(s32[211]{0:T(256)S(4)} %plan.1.refs_0_, bf16[192,128,128]{2,1,0:T(8,128)(2,1)S(1)} %bitcast.4, s32[192,16,128]{2,1,0:T(8,128)S(1)} %bitcast.8, bf16[1024,128]{1,0:T(8,128)(2,1)S(1)} %copy-done.3, ...), custom_call_target="tpu_custom_call" | custom-call | flops 4026531840 | bytes 6291456 | tf_op jit(solution)/shard_map/user_terms/pallas_call | solution.py:250
  19.4 0.0 collective-permute-done.5.refs_4_
  19.4 1.4 %collective-permute-done.6.refs_5_ = bf16[512,128]{1,0:T(8,128)(2,1)S(1)} collective-permute-done((bf16[512,128]{1,0:T(8,128)(2,1)S(1)}, bf16[512,128]{1,0:T(8,128)(2,1)S(1)}, u32[]{:S(2)}, u32[]{:S(2)}) %collective-permute-start.6) | collective-permute-done | bytes 131104 | tf_op jit(solution)/shard_map/ppermute | solution.py:201
  20.8 1.3 %collective-permute-done.7.refs_6_ = bf16[512,128]{1,0:T(8,128)(2,1)S(1)} collective-permute-done((bf16[512,128]{1,0:T(8,128)(2,1)S(1)}, bf16[512,128]{1,0:T(8,128)(2,1)S(1)}, u32[]{:S(2)}, u32[]{:S(2)}) %collective-permute-start.7) | collective-permute-done | bytes 131104 | tf_op jit(solution)/shard_map/ppermute | solution.py:201
  22.1 1.9 %user_terms.3 = (bf16[1536,128]{1,0:T(8,128)(2,1)S(1)}, f32[2048,128]{1,0:T(8,128)S(1)}, bf16[2048,128]{1,0:T(8,128)(2,1)S(1)}) custom-call(s32[211]{0:T(256)S(4)} %plan.1.refs_0_, bf16[192,128,128]{2,1,0:T(8,128)(2,1)S(1)} %bitcast.5, s32[192,16,128]{2,1,0:T(8,128)S(1)} %bitcast.9, ...), custom_call_target="tpu_custom_call", output_to_operand_aliasing={{1}: (7, {})} | custom-call | flops 4026531840 | bytes 6291456 | tf_op jit(solution)/shard_map/user_terms/pallas_call | solution.py:250
  24.0 0.1 collective-permute-start.8
  24.1 1.9 %collective-permute-done.8.refs_4_ = bf16[2048,128]{1,0:T(8,128)(2,1)S(1)} collective-permute-done((bf16[2048,128]{1,0:T(8,128)(2,1)S(1)}, bf16[2048,128]{1,0:T(8,128)(2,1)S(1)}, u32[]{:S(2)}, u32[]{:S(2)}) %collective-permute-start.8) | collective-permute-done | bytes 524320 | tf_op jit(solution)/shard_map/ppermute | solution.py:204
  26.0 2.1 %item_terms.2 = (bf16[512,128]{1,0:T(8,128)(2,1)S(1)}, bf16[512,128]{1,0:T(8,128)(2,1)S(1)}, bf16[512,128]{1,0:T(8,128)(2,1)S(1)}, bf16[2048,128]{1,0:T(8,128)(2,1)S(1)}, bf16[2048,128]{1,0:T(8,128)(2,1)S(1)}) custom-call(s32[211]{0:T(256)S(4)} %plan.1.refs_0_, bf16[192,128,128]{2,1,0:T(8,128)(2,1)S(1)} %bitcast.6, s32[192,16,128]{2,1,0:T(8,128)S(1)} %bitcast.10, ...), custom_call_target="tpu_custom_call" | custom-call | flops 4026531840 | bytes 6291456 | tf_op jit(solution)/shard_map/item_terms/pallas_call | solution.py:281
  28.1 3.9 %collective-permute-start.12 = (bf16[512,128]{1,0:T(8,128)(2,1)S(1)}, bf16[512,128]{1,0:T(8,128)(2,1)S(1)}, u32[]{:S(2)}, u32[]{:S(2)}) collective-permute-start(bf16[512,128]{1,0:T(8,128)(2,1)S(1)} %get-tuple-element.33), channel_id=1, source_target_pairs={{0,2},{2,0},{4,6},{6,4},{8,10},{10,8},{12,14},{14,12},{1,3},{3,1},... | collective-permute-start | bytes 393224 | tf_op jit(solution)/shard_map/ppermute | solution.py:201
  32.0 0.0 collective-permute-start.13
  32.0 1.5 %collective-permute-start.14 = (bf16[512,128]{1,0:T(8,128)(2,1)S(1)}, bf16[512,128]{1,0:T(8,128)(2,1)S(1)}, u32[]{:S(2)}, u32[]{:S(2)}) collective-permute-start(bf16[512,128]{1,0:T(8,128)(2,1)S(1)} %get-tuple-element.35), channel_id=1, source_target_pairs={{0,6},{2,4},{4,2},{6,0},{8,14},{10,12},{12,10},{14,8},{1,7},{3,5},... | collective-permute-start | bytes 393224 | tf_op jit(solution)/shard_map/ppermute | solution.py:201
  33.5 3.0 %item_terms.3 = (f32[512,128]{1,0:T(8,128)S(1)}, bf16[512,128]{1,0:T(8,128)(2,1)S(1)}, bf16[512,128]{1,0:T(8,128)(2,1)S(1)}, bf16[512,128]{1,0:T(8,128)(2,1)S(1)}, f32[512,128]{1,0:T(8,128)S(1)}) custom-call(s32[211]{0:T(256)S(4)} %plan.1.refs_0_, bf16[192,128,128]{2,1,0:T(8,128)(2,1)S(1)} %bitcast.7, s32[192,16,128]{2,1,0:T(8,128)S(1)} %bitcast.11, ...), custom_call_target="tpu_custom_call" | custom-call | flops 4026531840 | bytes 6291456 | tf_op jit(solution)/shard_map/item_terms/pallas_call | solution.py:281
  36.5 0.1 collective-permute-start.10
  36.5 4.5 %collective-permute-start.11 = (bf16[512,128]{1,0:T(8,128)(2,1)S(1)}, bf16[512,128]{1,0:T(8,128)(2,1)S(1)}, u32[]{:S(2)}, u32[]{:S(2)}) collective-permute-start(bf16[512,128]{1,0:T(8,128)(2,1)S(1)} %get-tuple-element.31), channel_id=1, source_target_pairs={{0,6},{2,4},{4,2},{6,0},{8,14},{10,12},{12,10},{14,8},{1,7},{3,5},... | collective-permute-start | bytes 393224 | tf_op jit(solution)/shard_map/ppermute | solution.py:201
  41.1 0.0 collective-permute-done.12
  41.1 0.0 collective-permute-start.9
  41.1 0.0 collective-permute-done.13
  41.1 0.0 collective-permute-done.14
  41.1 0.1 add_convert_fusion
  41.2 1.0 %collective-permute-start.15 = (bf16[512,128]{1,0:T(8,128)(2,1)S(1)}, bf16[512,128]{1,0:T(8,128)(2,1)S(1)}, u32[]{:S(2)}, u32[]{:S(2)}) collective-permute-start(bf16[512,128]{1,0:T(8,128)(2,1)S(1)} %add_convert_fusion), channel_id=1, source_target_pairs={{0,8},{2,10},{4,12},{6,14},{8,0},{10,2},{12,4},{14,6},{1,9},{3,11}... | collective-permute-start | bytes 393224 | tf_op jit(solution)/shard_map/ppermute | solution.py:201
  42.2 0.7 %constant_dynamic-slice_fusion = bf16[1024,128]{1,0:T(8,128)(2,1)} fusion(bf16[2048,128]{1,0:T(8,128)(2,1)S(1)} %get-tuple-element.25.refs_3_, s32[]{:T(128)S(6)} %select_n.3), kind=kLoop, calls=%fused_computation.1 | loop fusion | bytes 524292 | tf_op jit(solution)/shard_map/dynamic_slice | solution.py:298
  42.9 1.5 %collective-permute-done.10.refs_2_ = bf16[512,128]{1,0:T(8,128)(2,1)S(1)} collective-permute-done((bf16[512,128]{1,0:T(8,128)(2,1)S(1)}, bf16[512,128]{1,0:T(8,128)(2,1)S(1)}, u32[]{:S(2)}, u32[]{:S(2)}) %collective-permute-start.10) | collective-permute-done | bytes 131104 | tf_op jit(solution)/shard_map/ppermute | solution.py:201
  44.4 2.3 %collective-permute-done.11.refs_3_ = bf16[512,128]{1,0:T(8,128)(2,1)S(1)} collective-permute-done((bf16[512,128]{1,0:T(8,128)(2,1)S(1)}, bf16[512,128]{1,0:T(8,128)(2,1)S(1)}, u32[]{:S(2)}, u32[]{:S(2)}) %collective-permute-start.11) | collective-permute-done | bytes 131104 | tf_op jit(solution)/shard_map/ppermute | solution.py:201
  46.7 0.7 %collective-permute-done.9.refs_1_ = bf16[512,128]{1,0:T(8,128)(2,1)S(1)} collective-permute-done((bf16[512,128]{1,0:T(8,128)(2,1)S(1)}, bf16[512,128]{1,0:T(8,128)(2,1)S(1)}, u32[]{:S(2)}, u32[]{:S(2)}) %collective-permute-start.9) | collective-permute-done | bytes 131104 | tf_op jit(solution)/shard_map/ppermute | solution.py:201
  47.4 2.3 %collective-permute-done.15.refs_4_ = bf16[512,128]{1,0:T(8,128)(2,1)S(1)} collective-permute-done((bf16[512,128]{1,0:T(8,128)(2,1)S(1)}, bf16[512,128]{1,0:T(8,128)(2,1)S(1)}, u32[]{:S(2)}, u32[]{:S(2)}) %collective-permute-start.15) | collective-permute-done | bytes 131104 | tf_op jit(solution)/shard_map/ppermute | solution.py:201
  49.8 0.8 %finish.1 = bf16[512,128]{1,0:T(8,128)(2,1)} custom-call(bf16[512,128]{1,0:T(8,128)(2,1)S(1)} %copy-done, f32[512,128]{1,0:T(8,128)S(1)} %get-tuple-element.28.refs_0_, bf16[512,128]{1,0:T(8,128)(2,1)S(1)} %collective-permute-done.9.refs_1_, bf16[512,128]{1,0:T(8,128)(2,1)S(1)} %collective-permute-done.10.refs_2_, ...), custom_call_target="tpu_custom_call" | custom-call | tf_op jit(solution)/shard_map/finish/pallas_call | solution.py:304
  (4 shorter events, 0.0 us)
Async XLA Ops:
  0.6 11.5 %collective-permute-start = (bf16[512,128]{1,0:T(8,128)(2,1)}, bf16[512,128]{1,0:T(8,128)(2,1)S(1)}, u32[]{:S(2)}, u32[]{:S(2)}) collective-permute-start(bf16[512,128]{1,0:T(8,128)(2,1)} %items.1), channel_id=1, source_target_pairs={{0,8},{2,10},{4,12},{6,14},{8,0},{10,2},{12,4},{14,6},{1,9},{3,11}... | collective-permute-start | bytes 393224 | tf_op jit(solution)/shard_map/ppermute | solution.py:201
  4.7 9.8 %collective-permute-start.2 = (bf16[512,128]{1,0:T(8,128)(2,1)}, bf16[512,128]{1,0:T(8,128)(2,1)S(1)}, u32[]{:S(2)}, u32[]{:S(2)}) collective-permute-start(bf16[512,128]{1,0:T(8,128)(2,1)} %items.1), channel_id=1, source_target_pairs={{0,2},{2,0},{4,6},{6,4},{8,10},{10,8},{12,14},{14,12},{1,3},{3,1},... | collective-permute-start | bytes 393224 | tf_op jit(solution)/shard_map/ppermute | solution.py:201
  6.3 8.5 %collective-permute-start.3 = (bf16[512,128]{1,0:T(8,128)(2,1)}, bf16[512,128]{1,0:T(8,128)(2,1)S(1)}, u32[]{:S(2)}, u32[]{:S(2)}) collective-permute-start(bf16[512,128]{1,0:T(8,128)(2,1)} %items.1), channel_id=1, source_target_pairs={{0,4},{2,6},{4,0},{6,2},{8,12},{10,14},{12,8},{14,10},{1,5},{3,7},... | collective-permute-start | bytes 393224 | tf_op jit(solution)/shard_map/ppermute | solution.py:201
  7.8 8.2 %collective-permute-start.4 = (bf16[512,128]{1,0:T(8,128)(2,1)}, bf16[512,128]{1,0:T(8,128)(2,1)S(1)}, u32[]{:S(2)}, u32[]{:S(2)}) collective-permute-start(bf16[512,128]{1,0:T(8,128)(2,1)} %items.1), channel_id=1, source_target_pairs={{0,6},{2,4},{4,2},{6,0},{8,14},{10,12},{12,10},{14,8},{1,7},{3,5},... | collective-permute-start | bytes 393224 | tf_op jit(solution)/shard_map/ppermute | solution.py:201
  8.2 7.9 %collective-permute-start.1 = (bf16[1024,128]{1,0:T(8,128)(2,1)}, bf16[1024,128]{1,0:T(8,128)(2,1)S(1)}, u32[]{:S(2)}, u32[]{:S(2)}) collective-permute-start(bf16[1024,128]{1,0:T(8,128)(2,1)} %refs_3_.1), channel_id=1, source_target_pairs={{0,1},{1,0},{2,3},{3,2},{4,5},{5,4},{6,7},{7,6},{8,9},{9,8},{10,11... | collective-permute-start | bytes 786440 | tf_op jit(solution)/shard_map/ppermute | solution.py:204
  8.9 0.7 %copy-start.4 = (s32[1,1,192]{2,1,0:T(1,128)S(1)}, s32[1,1,192]{2,1,0:T(1,128)}, u32[]{:S(2)}) copy-start(s32[1,1,192]{2,1,0:T(1,128)} %param.11) | copy-start | bytes 2308
  9.6 0.7 %copy-start.5 = (s32[1,1,192]{2,1,0:T(1,128)S(1)}, s32[1,1,192]{2,1,0:T(1,128)}, u32[]{:S(2)}) copy-start(s32[1,1,192]{2,1,0:T(1,128)} %param.12) | copy-start | bytes 2308
  10.2 5.8 %copy-start = (bf16[512,128]{1,0:T(8,128)(2,1)S(1)}, bf16[512,128]{1,0:T(8,128)(2,1)}, u32[]{:S(2)}) copy-start(bf16[512,128]{1,0:T(8,128)(2,1)} %items.1) | copy-start | bytes 393220
  10.2 5.9 %copy-start.1 = (bf16[1,1,192,128,128]{4,3,2,1,0:T(8,128)(2,1)S(1)}, bf16[1,1,192,128,128]{4,3,2,1,0:T(8,128)(2,1)}, u32[]{:S(2)}) copy-start(bf16[1,1,192,128,128]{4,3,2,1,0:T(8,128)(2,1)} %param.9) | copy-start | bytes 18874372
  10.2 5.9 %copy-start.2 = (s32[1,1,192,16,128]{4,3,2,1,0:T(8,128)S(1)}, s32[1,1,192,16,128]{4,3,2,1,0:T(8,128)}, u32[]{:S(2)}) copy-start(s32[1,1,192,16,128]{4,3,2,1,0:T(8,128)} %param.10) | copy-start | bytes 4718596
  10.2 5.9 %copy-start.3 = (bf16[1024,128]{1,0:T(8,128)(2,1)S(1)}, bf16[1024,128]{1,0:T(8,128)(2,1)}, u32[]{:S(2)}) copy-start(bf16[1024,128]{1,0:T(8,128)(2,1)} %refs_3_.1) | copy-start | bytes 786436
  12.2 7.2 %collective-permute-start.5 = (bf16[512,128]{1,0:T(8,128)(2,1)S(1)}, bf16[512,128]{1,0:T(8,128)(2,1)S(1)}, u32[]{:S(2)}, u32[]{:S(2)}) collective-permute-start(bf16[512,128]{1,0:T(8,128)(2,1)S(1)} %collective-permute-done.refs_9_), channel_id=1, source_target_pairs={{0,2},{2,0},{4,6},{6,4},{8,10},{10,8},{12,14},{14,12},{1,3},{3,1},... | collective-permute-start | bytes 393224 | tf_op jit(solution)/shard_map/ppermute | solution.py:201
  14.5 6.3 %collective-permute-start.6 = (bf16[512,128]{1,0:T(8,128)(2,1)S(1)}, bf16[512,128]{1,0:T(8,128)(2,1)S(1)}, u32[]{:S(2)}, u32[]{:S(2)}) collective-permute-start(bf16[512,128]{1,0:T(8,128)(2,1)S(1)} %collective-permute-done.refs_9_), channel_id=1, source_target_pairs={{0,4},{2,6},{4,0},{6,2},{8,12},{10,14},{12,8},{14,10},{1,5},{3,7},... | collective-permute-start | bytes 393224 | tf_op jit(solution)/shard_map/ppermute | solution.py:201
  14.7 7.3 %collective-permute-start.7 = (bf16[512,128]{1,0:T(8,128)(2,1)S(1)}, bf16[512,128]{1,0:T(8,128)(2,1)S(1)}, u32[]{:S(2)}, u32[]{:S(2)}) collective-permute-start(bf16[512,128]{1,0:T(8,128)(2,1)S(1)} %collective-permute-done.refs_9_), channel_id=1, source_target_pairs={{0,6},{2,4},{4,2},{6,0},{8,14},{10,12},{12,10},{14,8},{1,7},{3,5},... | collective-permute-start | bytes 393224 | tf_op jit(solution)/shard_map/ppermute | solution.py:201
  24.0 2.0 %collective-permute-start.8 = (bf16[2048,128]{1,0:T(8,128)(2,1)S(1)}, bf16[2048,128]{1,0:T(8,128)(2,1)S(1)}, u32[]{:S(2)}, u32[]{:S(2)}) collective-permute-start(bf16[2048,128]{1,0:T(8,128)(2,1)S(1)} %get-tuple-element.23.refs_3_), channel_id=1, source_target_pairs={{0,1},{1,0},{2,3},{3,2},{4,5},{5,4},{6,7},{7,6},{8,9},{9,8},{10,11... | collective-permute-start | bytes 1572872 | tf_op jit(solution)/shard_map/ppermute | solution.py:204
  28.1 13.0 %collective-permute-start.12 = (bf16[512,128]{1,0:T(8,128)(2,1)S(1)}, bf16[512,128]{1,0:T(8,128)(2,1)S(1)}, u32[]{:S(2)}, u32[]{:S(2)}) collective-permute-start(bf16[512,128]{1,0:T(8,128)(2,1)S(1)} %get-tuple-element.33), channel_id=1, source_target_pairs={{0,2},{2,0},{4,6},{6,4},{8,10},{10,8},{12,14},{14,12},{1,3},{3,1},... | collective-permute-start | bytes 393224 | tf_op jit(solution)/shard_map/ppermute | solution.py:201
  32.0 9.1 %collective-permute-start.13 = (bf16[512,128]{1,0:T(8,128)(2,1)S(1)}, bf16[512,128]{1,0:T(8,128)(2,1)S(1)}, u32[]{:S(2)}, u32[]{:S(2)}) collective-permute-start(bf16[512,128]{1,0:T(8,128)(2,1)S(1)} %get-tuple-element.34), channel_id=1, source_target_pairs={{0,4},{2,6},{4,0},{6,2},{8,12},{10,14},{12,8},{14,10},{1,5},{3,7},... | collective-permute-start | bytes 393224 | tf_op jit(solution)/shard_map/ppermute | solution.py:201
  32.0 9.1 %collective-permute-start.14 = (bf16[512,128]{1,0:T(8,128)(2,1)S(1)}, bf16[512,128]{1,0:T(8,128)(2,1)S(1)}, u32[]{:S(2)}, u32[]{:S(2)}) collective-permute-start(bf16[512,128]{1,0:T(8,128)(2,1)S(1)} %get-tuple-element.35), channel_id=1, source_target_pairs={{0,6},{2,4},{4,2},{6,0},{8,14},{10,12},{12,10},{14,8},{1,7},{3,5},... | collective-permute-start | bytes 393224 | tf_op jit(solution)/shard_map/ppermute | solution.py:201
  36.5 7.9 %collective-permute-start.10 = (bf16[512,128]{1,0:T(8,128)(2,1)S(1)}, bf16[512,128]{1,0:T(8,128)(2,1)S(1)}, u32[]{:S(2)}, u32[]{:S(2)}) collective-permute-start(bf16[512,128]{1,0:T(8,128)(2,1)S(1)} %get-tuple-element.30), channel_id=1, source_target_pairs={{0,4},{2,6},{4,0},{6,2},{8,12},{10,14},{12,8},{14,10},{1,5},{3,7},... | collective-permute-start | bytes 393224 | tf_op jit(solution)/shard_map/ppermute | solution.py:201
  36.5 10.1 %collective-permute-start.11 = (bf16[512,128]{1,0:T(8,128)(2,1)S(1)}, bf16[512,128]{1,0:T(8,128)(2,1)S(1)}, u32[]{:S(2)}, u32[]{:S(2)}) collective-permute-start(bf16[512,128]{1,0:T(8,128)(2,1)S(1)} %get-tuple-element.31), channel_id=1, source_target_pairs={{0,6},{2,4},{4,2},{6,0},{8,14},{10,12},{12,10},{14,8},{1,7},{3,5},... | collective-permute-start | bytes 393224 | tf_op jit(solution)/shard_map/ppermute | solution.py:201
  41.1 6.4 %collective-permute-start.9 = (bf16[512,128]{1,0:T(8,128)(2,1)S(1)}, bf16[512,128]{1,0:T(8,128)(2,1)S(1)}, u32[]{:S(2)}, u32[]{:S(2)}) collective-permute-start(bf16[512,128]{1,0:T(8,128)(2,1)S(1)} %get-tuple-element.29), channel_id=1, source_target_pairs={{0,2},{2,0},{4,6},{6,4},{8,10},{10,8},{12,14},{14,12},{1,3},{3,1},... | collective-permute-start | bytes 393224 | tf_op jit(solution)/shard_map/ppermute | solution.py:201
  41.2 8.6 %collective-permute-start.15 = (bf16[512,128]{1,0:T(8,128)(2,1)S(1)}, bf16[512,128]{1,0:T(8,128)(2,1)S(1)}, u32[]{:S(2)}, u32[]{:S(2)}) collective-permute-start(bf16[512,128]{1,0:T(8,128)(2,1)S(1)} %add_convert_fusion), channel_id=1, source_target_pairs={{0,8},{2,10},{4,12},{6,14},{8,0},{10,2},{12,4},{14,6},{1,9},{3,11}... | collective-permute-start | bytes 393224 | tf_op jit(solution)/shard_map/ppermute | solution.py:201

commit v4 on v3

v4 whole, which is shorter than its diff:
```python
import functools

import jax
import jax.numpy as jnp
from jax import lax
from jax.experimental import pallas as pl
from jax.experimental.pallas import tpu as pltpu
from jax.sharding import PartitionSpec as P

BLOCK = 128
UNROLL = 24
TAIL = 8
FIELD = 10
PLAN_UNROLL = 8
VMEM_LIMIT = 16 * 1024 * 1024

NN = (((1,), (0,)), ((), ()))

vmem = functools.partial(pl.BlockSpec, memory_space=pltpu.VMEM)
smem = functools.partial(pl.BlockSpec, memory_space=pltpu.SMEM)
anywhere = functools.partial(pl.BlockSpec, memory_space=pl.ANY)


def params(limit=VMEM_LIMIT):
    return pltpu.CompilerParams(vmem_limit_bytes=limit)


def dot(a, b):
    return lax.dot_general(a, b, NN, preferred_element_type=jnp.float32)


def rows_of(index):
    return pl.ds(pl.multiple_of(index * BLOCK, BLOCK), BLOCK)


def tile(index):
    return slice(index * BLOCK, (index + 1) * BLOCK)


def plan_kernel(shard_tiles, keys, edges, live, rows, cols, total, meta):
    count = live[0, 0]
    me = lax.axis_index("row")
    stages = len(edges)
    region = (meta.shape[0] - stages) // stages

    def put(i, places):
        places = list(places)
        packed = []
        for j in range(PLAN_UNROLL):
            t = i * PLAN_UNROLL + j
            at = jnp.minimum(t, rows.shape[0] - 1)
            v = cols[at]
            if stages > 1:
                v = (v ^ (me * shard_tiles)) & (keys * shard_tiles - 1)
            packed.append((t, v, at + (rows[at] << FIELD)))
        for t, v, word in packed:
            spot, base = places[0], jnp.int32(0)
            inside = [v < edges[0]]
            for stage in range(1, stages):
                past = v >= edges[stage - 1]
                spot = jnp.where(past, stage * region + places[stage], spot)
                base = jnp.where(past, edges[stage - 1], base)
                inside.append(past & (v < edges[stage]))
            meta[spot] = word + ((v - base) << 2 * FIELD)
            for stage in range(stages):
                places[stage] += jnp.where(inside[stage] & (t < count), 1, 0)
        return tuple(places)

    trips = (count + PLAN_UNROLL - 1) // PLAN_UNROLL
    places = lax.fori_loop(0, trips, put, (jnp.int32(0),) * stages)
    for stage in range(stages):
        for at in range(UNROLL):
            meta[stage * region + places[stage] + at] = 0
        meta[stages * region + stage] = places[stage]


def stage_loop(stage, stages, meta, step_of):
    region = (meta.shape[0] - stages) // stages
    live = meta[stages * region + stage]
    mask = (1 << FIELD) - 1

    def group(start, size):
        entries = []
        for j in range(size):
            at = start + j
            word = meta[stage * region + at]
            entries.append(
                (word & mask, (word >> FIELD) & mask, word >> 2 * FIELD, at < live)
            )
        step_of(entries)

    def step(i, _):
        group(i * UNROLL, UNROLL)
        return _

    whole = (live + UNROLL - TAIL - 1) // UNROLL
    lax.fori_loop(0, whole, step, 0)

    @pl.when(whole * UNROLL < live)
    def _():
        group(whole * UNROLL, TAIL)


def masked_residual(predicted, tiles, words, slot, live):
    bit = jnp.left_shift(1, lax.broadcasted_iota(jnp.int32, (8, BLOCK), 0))
    bit = jnp.where(live, bit, 0)
    parts = []
    for w in range(BLOCK // 8):
        seen = jnp.broadcast_to(words[slot, pl.ds(w, 1), :], (8, BLOCK)) & bit
        gap = predicted[8 * w : 8 * w + 8] - tiles[slot, pl.ds(8 * w, 8), :].astype(jnp.float32)
        parts.append(jnp.where(seen != 0, gap, 0.0))
    return jnp.concatenate(parts, axis=0).astype(jnp.bfloat16)


def lay_items(shards, panel, flipped):
    per = shards[0].shape[0] // BLOCK
    for s, shard in enumerate(shards):
        for v in range(per):
            block = shard[tile(v)]
            panel[tile(s * per + v)] = block
            flipped[tile(s * per + v)] = block.T


def clear_kernel(total):
    total[...] = jnp.zeros_like(total)


def user_kernel(stage, stages, group, last, *refs):
    meta, tiles, words = refs[:3]
    shards = refs[3 : 3 + group]
    if stage == 0:
        mine, theirs = refs[3 + group : 5 + group]
        flipped, total, users = refs[6 + group : 9 + group]
        count = mine.shape[0]
        lead = lax.axis_index("col") == 0
        users[:count] = jnp.where(lead, mine[...], theirs[...])
        users[count:] = jnp.where(lead, theirs[...], mine[...])
    else:
        users = refs[3 + group]
        flipped, total = refs[5 + group : 7 + group]
    panel = refs[-1]
    lay_items(shards, panel, flipped)

    def step_of(entries):
        terms = []
        for slot, u, v, live in entries:
            predicted = dot(users[rows_of(u), :], flipped[rows_of(v), :])
            residual = masked_residual(predicted, tiles, words, slot, live)
            terms.append(dot(residual, panel[rows_of(v), :]))
        for (slot, u, v, live), term in zip(entries, terms):
            total[rows_of(u), :] += term

    stage_loop(stage, stages, meta, step_of)
    if last:
        refs[-2][...] = total[...].astype(jnp.bfloat16)


def item_kernel(parts, stages, first, *refs):
    meta, tiles, words = refs[:3]
    flips = refs[3 : 3 + len(parts)]
    refs = refs[3 + len(parts) :]
    total = refs[-1]
    if first:
        mine, theirs, users = refs[:3]
        outs = refs[3:-3]
        fresh, turned = refs[-3:-1]
        for u in range(users.shape[0] // BLOCK):
            values = users[tile(u)].astype(jnp.float32)
            gradient = mine[tile(u)].astype(jnp.float32) + theirs[tile(u)].astype(jnp.float32)
            new = (values - 0.02 * (gradient + 0.05 * values)).astype(jnp.bfloat16)
            fresh[tile(u)] = new
            turned[tile(u)] = new.T
    else:
        fresh, turned = refs[:2]
        outs = refs[2:-1]
    total[...] = jnp.zeros_like(total)
    base = 0
    for stage, flipped in zip(parts, flips):

        def step_of(entries, base=base, flipped=flipped):
            terms = []
            for slot, u, v, live in entries:
                predicted = dot(fresh[rows_of(u), :], flipped[rows_of(v), :])
                residual = masked_residual(predicted, tiles, words, slot, live)
                terms.append(dot(turned[rows_of(u), :], residual))
            for (slot, u, v, live), term in zip(entries, terms):
                total[rows_of(v + base), :] += term

        stage_loop(stage, stages, meta, step_of)
        base += flipped.shape[0] // BLOCK
    size = outs[0].shape[0]
    for s, out in enumerate(outs):
        out[...] = total[s * size : (s + 1) * size].astype(out.dtype)


def finish_kernel(items, *refs):
    out = refs[-1]
    for v in range(items.shape[0] // BLOCK):
        gradient = refs[0][tile(v)].astype(jnp.float32)
        for part in refs[1:-1]:
            gradient = gradient + part[tile(v)].astype(jnp.float32)
        values = items[tile(v)].astype(jnp.float32)
        out[tile(v)] = (values - 0.005 * (gradient.T + 0.05 * values)).astype(jnp.bfloat16)


def body(n_row, n_col, users, items, ratings, observed, tile_rows, tile_cols, tile_count):
    tiles = ratings[0, 0]
    words = observed[0, 0]
    slots = tiles.shape[0]
    rank = users.shape[-1]
    pad = slots + UNROLL
    per = items.shape[0] // BLOCK
    direct = items.shape[0] == per * BLOCK and n_row > 2
    direct = direct and (n_row & (n_row - 1)) == 0 and (per & (per - 1)) == 0
    keys = n_row if direct else 1
    half = n_row // 2
    groups = [[0]]
    if direct:
        groups = [list(range(half + 1)), list(range(half + 1, n_row))]
    stages = len(groups)
    col_at = lax.axis_index("col")

    def swap_row(x, k):
        return lax.ppermute(x, "row", [(i, i ^ k) for i in range(n_row)])

    def swap_col(x):
        return lax.ppermute(x, "col", [(i, i ^ 1) for i in range(n_col)])

    peer_users = swap_col(users)
    user_shape = (n_col * users.shape[0], rank)
    total = pl.pallas_call(
        clear_kernel,
        out_shape=pltpu.VMEM(user_shape, jnp.float32),
        out_specs=vmem(),
        compiler_params=params(),
        cost_estimate=pl.CostEstimate(flops=10**10, bytes_accessed=0, transcendentals=0),
        name="clear",
    )()
    shards = [items]
    if direct:
        shards += [swap_row(items, k) for k in range(1, half)]
        crossed = swap_row(items, half)
        shards += [crossed] + [swap_row(crossed, k) for k in range(1, half)]
    else:
        shards = [lax.all_gather(items, "row", axis=0, tiled=True)]
    wide = shards[0].shape[0]
    shard_tiles = wide // BLOCK
    edges = [(group[-1] + 1) * shard_tiles for group in groups]

    meta = pl.pallas_call(
        functools.partial(plan_kernel, shard_tiles, keys, edges),
        out_shape=pltpu.SMEM((stages * pad + stages,), jnp.int32),
        in_specs=[smem()] * 3 + [anywhere()],
        out_specs=smem(),
        compiler_params=params(),
        name="plan",
    )(tile_count, tile_rows[0, 0], tile_cols[0, 0], total)

    cost = pl.CostEstimate(
        flops=20 * slots * BLOCK * BLOCK * rank // stages,
        bytes_accessed=(slots // stages) * BLOCK * BLOCK * 4,
        transcendentals=0,
    )
    flipped = []
    for stage, group in enumerate(groups):
        last = stage == stages - 1
        size = len(group)
        panel_shape = (size * wide, rank)
        shapes = [pltpu.VMEM(panel_shape, jnp.bfloat16), pltpu.VMEM(user_shape, jnp.float32)]
        operands = [meta, tiles, words] + [shards[key] for key in group]
        operands += [users, peer_users, total] if stage == 0 else [panel, total]
        if stage == 0:
            shapes.append(pltpu.VMEM(user_shape, jnp.bfloat16))
        if last:
            shapes.append(jax.ShapeDtypeStruct(user_shape, jnp.bfloat16))
        outs = pl.pallas_call(
            functools.partial(user_kernel, stage, stages, size, last),
            out_shape=tuple(shapes),
            in_specs=[smem()] + [vmem()] * (len(operands) - 1),
            out_specs=tuple([vmem()] * len(shapes)),
            input_output_aliases={len(operands) - 1: 1},
            scratch_shapes=[pltpu.VMEM(panel_shape, jnp.bfloat16)],
            compiler_params=params(),
            cost_estimate=cost,
            name="user_terms",
        )(*operands)
        flipped.append(outs[0])
        total = outs[1]
        if stage == 0:
            panel = outs[2]
    terms = outs[-1]
    peer_terms = swap_col(terms)

    sums = [None] * keys
    for parts in ([range(1, stages)] if direct else []) + [range(1)]:
        first = 0 not in parts or not direct
        named = [key for stage in parts for key in groups[stage]]
        shapes = [
            jax.ShapeDtypeStruct(
                (wide, rank), jnp.float32 if key in (0, half) else jnp.bfloat16
            )
            for key in named
        ]
        operands = [meta, tiles, words] + [flipped[stage] for stage in parts]
        if first:
            operands += [terms, peer_terms, panel]
            shapes += [pltpu.VMEM(user_shape, jnp.bfloat16)] * 2
        else:
            operands += [fresh, turned]
        outs = pl.pallas_call(
            functools.partial(item_kernel, tuple(parts), stages, first),
            out_shape=tuple(shapes),
            in_specs=[smem()] + [vmem()] * (len(operands) - 1),
            out_specs=tuple([vmem()] * len(shapes)),
            scratch_shapes=[pltpu.VMEM((len(named) * wide, rank), jnp.float32)],
            compiler_params=params(),
            cost_estimate=cost,
            name="item_terms",
        )(*operands)
        if first:
            fresh, turned = outs[-2:]
        for key, out in zip(named, outs):
            sums[key] = out if key in (0, half) else swap_row(out, key % half)
    users_new = lax.dynamic_slice_in_dim(fresh, col_at * users.shape[0], users.shape[0], 0)

    if direct:
        relay = sums[half]
        for part in sums[half + 1 :]:
            relay = relay + part.astype(jnp.float32)
        parts = sums[:half] + [swap_row(relay.astype(jnp.bfloat16), half)]
        items_new = pl.pallas_call(
            finish_kernel,
            out_shape=jax.ShapeDtypeStruct(items.shape, jnp.bfloat16),
            in_specs=[vmem()] * (1 + len(parts)),
            out_specs=vmem(),
            compiler_params=params(),
            name="finish",
        )(items, *parts)
    else:
        turned_terms = jnp.swapaxes(sums[0].reshape(-1, BLOCK, BLOCK), 1, 2)
        item_grad = lax.psum_scatter(
            turned_terms.reshape(wide, rank), "row", scatter_dimension=0, tiled=True
        )
        values = items.astype(jnp.float32)
        items_new = (values - 0.005 * (item_grad + 0.05 * values)).astype(jnp.bfloat16)
    return (users_new, items_new)


def solution(mesh):
    return jax.shard_map(
        functools.partial(body, mesh.shape["row"], mesh.shape["col"]),
        mesh=mesh,
        in_specs=(
            P(("groups", "row", "col"), None),
            P(("groups", "row", "col"), None),
            P(("groups", "row"), "col", None, None, None),
            P(("groups", "row"), "col", None, None, None),
            P(("groups", "row"), "col", None),
            P(("groups", "row"), "col", None),
            P(("groups", "row"), "col"),
        ),
        out_specs=(P(("groups", "row", "col"), None), P(("groups", "row", "col"), None)),
        check_vma=False,
    )
```

time: 51.1 us -> 48.4 us (0.947)
  Pallas kernels: 12.9 us -> 10.4 us
  local copies, waits for them, and re-layouts: 2.08 us -> 0.74 us
  starting transfers between devices: 22.6 us -> 23.8 us
    pallas_call x5 -> x6, Pallas kernels: 12.1 us -> 9.6 us  [the longest x2 4.01 us: body(): pl.pallas_call(functools.partial(item_kernel, tuple(parts), stages, first...]
    unnamed x12, local copies, waits for them, and re-layouts: 1.37 us -> 0.03 us
    ppermute x14, starting transfers between devices: 22.5 us -> 23.7 us  [swap_row(): return lax.ppermute(x, 'row', [(i, i ^ k) for i in range(n_row)])]
  transfers between devices with their start and end apart: 16 -> 16, of which waited for: 7 -> 8; matrix products, arithmetic and copies ran while one was open for 2% -> 2% of each run, Pallas kernels for 16% -> 12%
where the time goes in v4:
time: 48.4 us; the launch traced here: 48 us
  starting transfers between devices  23.8 us (49%)
  waiting for transfers between devices  11.5 us (24%)
  Pallas kernels  10.4 us (21%)
  between operations  1.44 us (3%)
  local copies, waits for them, and re-layouts  0.74 us (2%)
    ppermute x14, starting transfers between devices, swap_row(): return lax.ppermute(x, 'row', [(i, i ^ k) for i in range(n_row)])  23.7 us
    ppermute x14, waiting for transfers between devices, swap_row(): return lax.ppermute(x, 'row', [(i, i ^ k) for i in range(n_row)])  9.64 us
    pallas_call x2, Pallas kernels, body(): pl.pallas_call(functools.partial(item_kernel, tuple(parts), stages, first...  4.01 us
    pallas_call x2, Pallas kernels, body(): pl.pallas_call(functools.partial(user_kernel, stage, stages, size, last),...  4 us
    ppermute x2, waiting for transfers between devices, swap_col(): return lax.ppermute(x, 'col', [(i, i ^ 1) for i in range(n_col)])  1.9 us
    pallas_call x1, Pallas kernels, body(): pl.pallas_call(functools.partial(plan_kernel, shard_tiles, keys, edges),...  1.52 us
  transfers between devices with their start and end apart: 16, of which 8 were waited for; matrix products, arithmetic and copies ran while one was open for 2% of the time, Pallas kernels for 12%

profile of v4, /device:TPU:0, one launch (start us, length us, event | category | flops | bytes accessed | tf_op | source)
XLA Modules:
  0.0 48.0 jit_solution(5083420712371218981)
XLA Ops:
  0.6 0.0 copy-start
  0.6 0.0 copy-start.5
  0.7 0.0 copy-start.1
  0.7 0.0 copy-start.2
  0.7 0.0 copy-start.3
  0.7 0.0 copy-start.4
  0.7 4.1 %collective-permute-start = (bf16[512,128]{1,0:T(8,128)(2,1)}, bf16[512,128]{1,0:T(8,128)(2,1)S(1)}, u32[]{:S(2)}, u32[]{:S(2)}) collective-permute-start(bf16[512,128]{1,0:T(8,128)(2,1)} %items.1), channel_id=1, source_target_pairs={{0,8},{2,10},{4,12},{6,14},{8,0},{10,2},{12,4},{14,6},{1,9},{3,11}... | collective-permute-start | bytes 393224 | tf_op jit(solution)/shard_map/ppermute | solution.py:224
  4.8 1.5 %collective-permute-start.4 = (bf16[512,128]{1,0:T(8,128)(2,1)}, bf16[512,128]{1,0:T(8,128)(2,1)S(1)}, u32[]{:S(2)}, u32[]{:S(2)}) collective-permute-start(bf16[512,128]{1,0:T(8,128)(2,1)} %items.1), channel_id=1, source_target_pairs={{0,2},{2,0},{4,6},{6,4},{8,10},{10,8},{12,14},{14,12},{1,3},{3,1},... | collective-permute-start | bytes 393224 | tf_op jit(solution)/shard_map/ppermute | solution.py:224
  6.3 1.6 %collective-permute-start.5 = (bf16[512,128]{1,0:T(8,128)(2,1)}, bf16[512,128]{1,0:T(8,128)(2,1)S(1)}, u32[]{:S(2)}, u32[]{:S(2)}) collective-permute-start(bf16[512,128]{1,0:T(8,128)(2,1)} %items.1), channel_id=1, source_target_pairs={{0,4},{2,6},{4,0},{6,2},{8,12},{10,14},{12,8},{14,10},{1,5},{3,7},... | collective-permute-start | bytes 393224 | tf_op jit(solution)/shard_map/ppermute | solution.py:224
  7.9 0.4 collective-permute-start.6
  8.3 0.0 collective-permute-start.7
  8.3 0.1 clear.1.total.refs_10_
  9.0 1.5 %plan.1.refs_0_ = s32[434]{0:T(512)S(4)} custom-call(s32[1,1]{1,0:T(1,128)S(6)} %copy.13.live, s32[192]{0:T(256)S(1)} %bitcast.4, s32[192]{0:T(256)S(1)} %bitcast.5, f32[2048,128]{1,0:T(8,128)S(1)} %clear.1.total.refs_10_), custom_call_target="tpu_custom_call" | custom-call | tf_op jit(solution)/shard_map/plan/pallas_call | solution.py:250
  10.6 0.9 %collective-permute-done.refs_7_ = bf16[512,128]{1,0:T(8,128)(2,1)S(1)} collective-permute-done((bf16[512,128]{1,0:T(8,128)(2,1)}, bf16[512,128]{1,0:T(8,128)(2,1)S(1)}, u32[]{:S(2)}, u32[]{:S(2)}) %collective-permute-start) | collective-permute-done | bytes 131104 | tf_op jit(solution)/shard_map/ppermute | solution.py:224
  11.4 1.6 %collective-permute-start.1 = (bf16[512,128]{1,0:T(8,128)(2,1)S(1)}, bf16[512,128]{1,0:T(8,128)(2,1)S(1)}, u32[]{:S(2)}, u32[]{:S(2)}) collective-permute-start(bf16[512,128]{1,0:T(8,128)(2,1)S(1)} %collective-permute-done.refs_7_), channel_id=1, source_target_pairs={{0,2},{2,0},{4,6},{6,4},{8,10},{10,8},{12,14},{14,12},{1,3},{3,1},... | collective-permute-start | bytes 393224 | tf_op jit(solution)/shard_map/ppermute | solution.py:224
  13.0 0.0 collective-permute-done.4.refs_4_
  13.0 1.4 %collective-permute-start.2 = (bf16[512,128]{1,0:T(8,128)(2,1)S(1)}, bf16[512,128]{1,0:T(8,128)(2,1)S(1)}, u32[]{:S(2)}, u32[]{:S(2)}) collective-permute-start(bf16[512,128]{1,0:T(8,128)(2,1)S(1)} %collective-permute-done.refs_7_), channel_id=1, source_target_pairs={{0,4},{2,6},{4,0},{6,2},{8,12},{10,14},{12,8},{14,10},{1,5},{3,7},... | collective-permute-start | bytes 393224 | tf_op jit(solution)/shard_map/ppermute | solution.py:224
  14.3 0.0 collective-permute-done.5.refs_5_
  14.3 0.8 %collective-permute-start.3 = (bf16[512,128]{1,0:T(8,128)(2,1)S(1)}, bf16[512,128]{1,0:T(8,128)(2,1)S(1)}, u32[]{:S(2)}, u32[]{:S(2)}) collective-permute-start(bf16[512,128]{1,0:T(8,128)(2,1)S(1)} %collective-permute-done.refs_7_), channel_id=1, source_target_pairs={{0,6},{2,4},{4,2},{6,0},{8,14},{10,12},{12,10},{14,8},{1,7},{3,5},... | collective-permute-start | bytes 393224 | tf_op jit(solution)/shard_map/ppermute | solution.py:224
  15.2 0.7 %collective-permute-done.6.refs_6_ = bf16[512,128]{1,0:T(8,128)(2,1)S(1)} collective-permute-done((bf16[512,128]{1,0:T(8,128)(2,1)}, bf16[512,128]{1,0:T(8,128)(2,1)S(1)}, u32[]{:S(2)}, u32[]{:S(2)}) %collective-permute-start.6) | collective-permute-done | bytes 131104 | tf_op jit(solution)/shard_map/ppermute | solution.py:224
  15.8 0.0 collective-permute-done.7.refs_9_
  15.8 0.0 copy-done
  15.8 2.3 %user_terms.2 = (bf16[2560,128]{1,0:T(8,128)(2,1)S(1)}, f32[2048,128]{1,0:T(8,128)S(1)}, bf16[2048,128]{1,0:T(8,128)(2,1)S(1)}) custom-call(s32[434]{0:T(512)S(4)} %plan.1.refs_0_, bf16[192,128,128]{2,1,0:T(8,128)(2,1)S(1)} %bitcast.6, s32[192,16,128]{2,1,0:T(8,128)S(1)} %bitcast.10, bf16[512,128]{1,0:T(8,128)(2,1)S(1)} %copy-done, ...), custom_call_target="tpu_custom_call", output_to_operand_aliasing={{1}: (10, {})} | custom-call | flops 4026531840 | bytes 6291456 | tf_op jit(solution)/shard_map/user_terms/pallas_call | solution.py:276
  18.1 1.1 %collective-permute-done.1.refs_3_ = bf16[512,128]{1,0:T(8,128)(2,1)S(1)} collective-permute-done((bf16[512,128]{1,0:T(8,128)(2,1)S(1)}, bf16[512,128]{1,0:T(8,128)(2,1)S(1)}, u32[]{:S(2)}, u32[]{:S(2)}) %collective-permute-start.1) | collective-permute-done | bytes 131104 | tf_op jit(solution)/shard_map/ppermute | solution.py:224
  19.2 0.1 collective-permute-done.2.refs_4_
  19.3 2.0 %collective-permute-done.3.refs_5_ = bf16[512,128]{1,0:T(8,128)(2,1)S(1)} collective-permute-done((bf16[512,128]{1,0:T(8,128)(2,1)S(1)}, bf16[512,128]{1,0:T(8,128)(2,1)S(1)}, u32[]{:S(2)}, u32[]{:S(2)}) %collective-permute-start.3) | collective-permute-done | bytes 131104 | tf_op jit(solution)/shard_map/ppermute | solution.py:224
  21.3 1.7 %user_terms.3 = (bf16[1536,128]{1,0:T(8,128)(2,1)S(1)}, f32[2048,128]{1,0:T(8,128)S(1)}, bf16[2048,128]{1,0:T(8,128)(2,1)S(1)}) custom-call(s32[434]{0:T(512)S(4)} %plan.1.refs_0_, bf16[192,128,128]{2,1,0:T(8,128)(2,1)S(1)} %bitcast.7, s32[192,16,128]{2,1,0:T(8,128)S(1)} %bitcast.11, ...), custom_call_target="tpu_custom_call", output_to_operand_aliasing={{1}: (7, {})} | custom-call | flops 4026531840 | bytes 6291456 | tf_op jit(solution)/shard_map/user_terms/pallas_call | solution.py:276
  23.1 0.1 collective-permute-start.8
  23.2 1.9 %collective-permute-done.8.refs_5_ = bf16[2048,128]{1,0:T(8,128)(2,1)S(1)} collective-permute-done((bf16[2048,128]{1,0:T(8,128)(2,1)S(1)}, bf16[2048,128]{1,0:T(8,128)(2,1)S(1)}, u32[]{:S(2)}, u32[]{:S(2)}) %collective-permute-start.8) | collective-permute-done | bytes 524320 | tf_op jit(solution)/shard_map/ppermute | solution.py:227
  25.1 1.9 %item_terms.2 = (bf16[512,128]{1,0:T(8,128)(2,1)S(1)}, bf16[512,128]{1,0:T(8,128)(2,1)S(1)}, bf16[512,128]{1,0:T(8,128)(2,1)S(1)}, bf16[2048,128]{1,0:T(8,128)(2,1)S(1)}, bf16[2048,128]{1,0:T(8,128)(2,1)S(1)}) custom-call(s32[434]{0:T(512)S(4)} %plan.1.refs_0_, bf16[192,128,128]{2,1,0:T(8,128)(2,1)S(1)} %bitcast.8, s32[192,16,128]{2,1,0:T(8,128)S(1)} %bitcast.12, ...), custom_call_target="tpu_custom_call" | custom-call | flops 4026531840 | bytes 6291456 | tf_op jit(solution)/shard_map/item_terms/pallas_call | solution.py:310
  27.0 3.1 %collective-permute-start.12 = (bf16[512,128]{1,0:T(8,128)(2,1)S(1)}, bf16[512,128]{1,0:T(8,128)(2,1)S(1)}, u32[]{:S(2)}, u32[]{:S(2)}) collective-permute-start(bf16[512,128]{1,0:T(8,128)(2,1)S(1)} %get-tuple-element.29), channel_id=1, source_target_pairs={{0,2},{2,0},{4,6},{6,4},{8,10},{10,8},{12,14},{14,12},{1,3},{3,1},... | collective-permute-start | bytes 393224 | tf_op jit(solution)/shard_map/ppermute | solution.py:224
  30.0 1.4 %collective-permute-start.13 = (bf16[512,128]{1,0:T(8,128)(2,1)S(1)}, bf16[512,128]{1,0:T(8,128)(2,1)S(1)}, u32[]{:S(2)}, u32[]{:S(2)}) collective-permute-start(bf16[512,128]{1,0:T(8,128)(2,1)S(1)} %get-tuple-element.30), channel_id=1, source_target_pairs={{0,4},{2,6},{4,0},{6,2},{8,12},{10,14},{12,8},{14,10},{1,5},{3,7},... | collective-permute-start | bytes 393224 | tf_op jit(solution)/shard_map/ppermute | solution.py:224
  31.4 0.1 collective-permute-start.14
  31.6 2.1 %item_terms.3 = (f32[512,128]{1,0:T(8,128)S(1)}, bf16[512,128]{1,0:T(8,128)(2,1)S(1)}, bf16[512,128]{1,0:T(8,128)(2,1)S(1)}, bf16[512,128]{1,0:T(8,128)(2,1)S(1)}, f32[512,128]{1,0:T(8,128)S(1)}) custom-call(s32[434]{0:T(512)S(4)} %plan.1.refs_0_, bf16[192,128,128]{2,1,0:T(8,128)(2,1)S(1)} %bitcast.9, s32[192,16,128]{2,1,0:T(8,128)S(1)} %bitcast.13, ...), custom_call_target="tpu_custom_call" | custom-call | flops 4026531840 | bytes 6291456 | tf_op jit(solution)/shard_map/item_terms/pallas_call | solution.py:310
  33.7 3.6 %collective-permute-start.10 = (bf16[512,128]{1,0:T(8,128)(2,1)S(1)}, bf16[512,128]{1,0:T(8,128)(2,1)S(1)}, u32[]{:S(2)}, u32[]{:S(2)}) collective-permute-start(bf16[512,128]{1,0:T(8,128)(2,1)S(1)} %get-tuple-element.26), channel_id=1, source_target_pairs={{0,4},{2,6},{4,0},{6,2},{8,12},{10,14},{12,8},{14,10},{1,5},{3,7},... | collective-permute-start | bytes 393224 | tf_op jit(solution)/shard_map/ppermute | solution.py:224
  37.3 1.0 %collective-permute-start.11 = (bf16[512,128]{1,0:T(8,128)(2,1)S(1)}, bf16[512,128]{1,0:T(8,128)(2,1)S(1)}, u32[]{:S(2)}, u32[]{:S(2)}) collective-permute-start(bf16[512,128]{1,0:T(8,128)(2,1)S(1)} %get-tuple-element.27), channel_id=1, source_target_pairs={{0,6},{2,4},{4,2},{6,0},{8,14},{10,12},{12,10},{14,8},{1,7},{3,5},... | collective-permute-start | bytes 393224 | tf_op jit(solution)/shard_map/ppermute | solution.py:224
  38.3 0.0 collective-permute-done.12
  38.3 0.5 %collective-permute-start.9 = (bf16[512,128]{1,0:T(8,128)(2,1)S(1)}, bf16[512,128]{1,0:T(8,128)(2,1)S(1)}, u32[]{:S(2)}, u32[]{:S(2)}) collective-permute-start(bf16[512,128]{1,0:T(8,128)(2,1)S(1)} %get-tuple-element.25), channel_id=1, source_target_pairs={{0,2},{2,0},{4,6},{6,4},{8,10},{10,8},{12,14},{14,12},{1,3},{3,1},... | collective-permute-start | bytes 393224 | tf_op jit(solution)/shard_map/ppermute | solution.py:224
  38.8 0.0 collective-permute-done.13
  38.8 0.0 collective-permute-done.14
  38.8 0.1 add_convert_fusion
  38.9 2.6 %collective-permute-start.15 = (bf16[512,128]{1,0:T(8,128)(2,1)S(1)}, bf16[512,128]{1,0:T(8,128)(2,1)S(1)}, u32[]{:S(2)}, u32[]{:S(2)}) collective-permute-start(bf16[512,128]{1,0:T(8,128)(2,1)S(1)} %add_convert_fusion), channel_id=1, source_target_pairs={{0,8},{2,10},{4,12},{6,14},{8,0},{10,2},{12,4},{14,6},{1,9},{3,11}... | collective-permute-start | bytes 393224 | tf_op jit(solution)/shard_map/ppermute | solution.py:224
  41.5 0.7 %constant_dynamic-slice_fusion = bf16[1024,128]{1,0:T(8,128)(2,1)} fusion(bf16[2048,128]{1,0:T(8,128)(2,1)S(1)} %get-tuple-element.21.refs_4_, s32[]{:T(128)S(6)} %select_n.3), kind=kLoop, calls=%fused_computation.1 | loop fusion | bytes 524292 | tf_op jit(solution)/shard_map/dynamic_slice | solution.py:324
  42.3 2.5 %collective-permute-done.10.refs_2_ = bf16[512,128]{1,0:T(8,128)(2,1)S(1)} collective-permute-done((bf16[512,128]{1,0:T(8,128)(2,1)S(1)}, bf16[512,128]{1,0:T(8,128)(2,1)S(1)}, u32[]{:S(2)}, u32[]{:S(2)}) %collective-permute-start.10) | collective-permute-done | bytes 131104 | tf_op jit(solution)/shard_map/ppermute | solution.py:224
  44.8 2.4 %collective-permute-done.11.refs_3_ = bf16[512,128]{1,0:T(8,128)(2,1)S(1)} collective-permute-done((bf16[512,128]{1,0:T(8,128)(2,1)S(1)}, bf16[512,128]{1,0:T(8,128)(2,1)S(1)}, u32[]{:S(2)}, u32[]{:S(2)}) %collective-permute-start.11) | collective-permute-done | bytes 131104 | tf_op jit(solution)/shard_map/ppermute | solution.py:224
  47.2 0.0 collective-permute-done.9.refs_1_
  47.2 0.0 collective-permute-done.15.refs_4_
  47.2 0.8 %finish.1 = bf16[512,128]{1,0:T(8,128)(2,1)} custom-call(bf16[512,128]{1,0:T(8,128)(2,1)S(1)} %copy-done, f32[512,128]{1,0:T(8,128)S(1)} %get-tuple-element.24.refs_0_, bf16[512,128]{1,0:T(8,128)(2,1)S(1)} %collective-permute-done.9.refs_1_, bf16[512,128]{1,0:T(8,128)(2,1)S(1)} %collective-permute-done.10.refs_2_, ...), custom_call_target="tpu_custom_call" | custom-call | tf_op jit(solution)/shard_map/finish/pallas_call | solution.py:331
  (5 shorter events, 0.0 us)
Async XLA Ops:
  0.6 15.2 %copy-start = (bf16[512,128]{1,0:T(8,128)(2,1)S(1)}, bf16[512,128]{1,0:T(8,128)(2,1)}, u32[]{:S(2)}) copy-start(bf16[512,128]{1,0:T(8,128)(2,1)} %items.1) | copy-start | bytes 393220
  0.6 15.2 %copy-start.5 = (bf16[1024,128]{1,0:T(8,128)(2,1)S(1)}, bf16[1024,128]{1,0:T(8,128)(2,1)}, u32[]{:S(2)}) copy-start(bf16[1024,128]{1,0:T(8,128)(2,1)} %refs_8_.1) | copy-start | bytes 786436
  0.7 8.4 %copy-start.1 = (s32[1,1,192]{2,1,0:T(1,128)S(1)}, s32[1,1,192]{2,1,0:T(1,128)}, u32[]{:S(2)}) copy-start(s32[1,1,192]{2,1,0:T(1,128)} %param.11) | copy-start | bytes 2308
  0.7 8.4 %copy-start.2 = (s32[1,1,192]{2,1,0:T(1,128)S(1)}, s32[1,1,192]{2,1,0:T(1,128)}, u32[]{:S(2)}) copy-start(s32[1,1,192]{2,1,0:T(1,128)} %param.12) | copy-start | bytes 2308
  0.7 15.2 %copy-start.3 = (bf16[1,1,192,128,128]{4,3,2,1,0:T(8,128)(2,1)S(1)}, bf16[1,1,192,128,128]{4,3,2,1,0:T(8,128)(2,1)}, u32[]{:S(2)}) copy-start(bf16[1,1,192,128,128]{4,3,2,1,0:T(8,128)(2,1)} %param.9) | copy-start | bytes 18874372
  0.7 15.2 %copy-start.4 = (s32[1,1,192,16,128]{4,3,2,1,0:T(8,128)S(1)}, s32[1,1,192,16,128]{4,3,2,1,0:T(8,128)}, u32[]{:S(2)}) copy-start(s32[1,1,192,16,128]{4,3,2,1,0:T(8,128)} %param.10) | copy-start | bytes 4718596
  0.7 10.7 %collective-permute-start = (bf16[512,128]{1,0:T(8,128)(2,1)}, bf16[512,128]{1,0:T(8,128)(2,1)S(1)}, u32[]{:S(2)}, u32[]{:S(2)}) collective-permute-start(bf16[512,128]{1,0:T(8,128)(2,1)} %items.1), channel_id=1, source_target_pairs={{0,8},{2,10},{4,12},{6,14},{8,0},{10,2},{12,4},{14,6},{1,9},{3,11}... | collective-permute-start | bytes 393224 | tf_op jit(solution)/shard_map/ppermute | solution.py:224
  4.8 8.2 %collective-permute-start.4 = (bf16[512,128]{1,0:T(8,128)(2,1)}, bf16[512,128]{1,0:T(8,128)(2,1)S(1)}, u32[]{:S(2)}, u32[]{:S(2)}) collective-permute-start(bf16[512,128]{1,0:T(8,128)(2,1)} %items.1), channel_id=1, source_target_pairs={{0,2},{2,0},{4,6},{6,4},{8,10},{10,8},{12,14},{14,12},{1,3},{3,1},... | collective-permute-start | bytes 393224 | tf_op jit(solution)/shard_map/ppermute | solution.py:224
  6.3 8.0 %collective-permute-start.5 = (bf16[512,128]{1,0:T(8,128)(2,1)}, bf16[512,128]{1,0:T(8,128)(2,1)S(1)}, u32[]{:S(2)}, u32[]{:S(2)}) collective-permute-start(bf16[512,128]{1,0:T(8,128)(2,1)} %items.1), channel_id=1, source_target_pairs={{0,4},{2,6},{4,0},{6,2},{8,12},{10,14},{12,8},{14,10},{1,5},{3,7},... | collective-permute-start | bytes 393224 | tf_op jit(solution)/shard_map/ppermute | solution.py:224
  7.9 7.9 %collective-permute-start.6 = (bf16[512,128]{1,0:T(8,128)(2,1)}, bf16[512,128]{1,0:T(8,128)(2,1)S(1)}, u32[]{:S(2)}, u32[]{:S(2)}) collective-permute-start(bf16[512,128]{1,0:T(8,128)(2,1)} %items.1), channel_id=1, source_target_pairs={{0,6},{2,4},{4,2},{6,0},{8,14},{10,12},{12,10},{14,8},{1,7},{3,5},... | collective-permute-start | bytes 393224 | tf_op jit(solution)/shard_map/ppermute | solution.py:224
  8.3 7.5 %collective-permute-start.7 = (bf16[1024,128]{1,0:T(8,128)(2,1)}, bf16[1024,128]{1,0:T(8,128)(2,1)S(1)}, u32[]{:S(2)}, u32[]{:S(2)}) collective-permute-start(bf16[1024,128]{1,0:T(8,128)(2,1)} %refs_8_.1), channel_id=1, source_target_pairs={{0,1},{1,0},{2,3},{3,2},{4,5},{5,4},{6,7},{7,6},{8,9},{9,8},{10,11... | collective-permute-start | bytes 786440 | tf_op jit(solution)/shard_map/ppermute | solution.py:227
  11.4 7.8 %collective-permute-start.1 = (bf16[512,128]{1,0:T(8,128)(2,1)S(1)}, bf16[512,128]{1,0:T(8,128)(2,1)S(1)}, u32[]{:S(2)}, u32[]{:S(2)}) collective-permute-start(bf16[512,128]{1,0:T(8,128)(2,1)S(1)} %collective-permute-done.refs_7_), channel_id=1, source_target_pairs={{0,2},{2,0},{4,6},{6,4},{8,10},{10,8},{12,14},{14,12},{1,3},{3,1},... | collective-permute-start | bytes 393224 | tf_op jit(solution)/shard_map/ppermute | solution.py:224
  13.0 6.3 %collective-permute-start.2 = (bf16[512,128]{1,0:T(8,128)(2,1)S(1)}, bf16[512,128]{1,0:T(8,128)(2,1)S(1)}, u32[]{:S(2)}, u32[]{:S(2)}) collective-permute-start(bf16[512,128]{1,0:T(8,128)(2,1)S(1)} %collective-permute-done.refs_7_), channel_id=1, source_target_pairs={{0,4},{2,6},{4,0},{6,2},{8,12},{10,14},{12,8},{14,10},{1,5},{3,7},... | collective-permute-start | bytes 393224 | tf_op jit(solution)/shard_map/ppermute | solution.py:224
  14.3 7.0 %collective-permute-start.3 = (bf16[512,128]{1,0:T(8,128)(2,1)S(1)}, bf16[512,128]{1,0:T(8,128)(2,1)S(1)}, u32[]{:S(2)}, u32[]{:S(2)}) collective-permute-start(bf16[512,128]{1,0:T(8,128)(2,1)S(1)} %collective-permute-done.refs_7_), channel_id=1, source_target_pairs={{0,6},{2,4},{4,2},{6,0},{8,14},{10,12},{12,10},{14,8},{1,7},{3,5},... | collective-permute-start | bytes 393224 | tf_op jit(solution)/shard_map/ppermute | solution.py:224
  23.1 2.0 %collective-permute-start.8 = (bf16[2048,128]{1,0:T(8,128)(2,1)S(1)}, bf16[2048,128]{1,0:T(8,128)(2,1)S(1)}, u32[]{:S(2)}, u32[]{:S(2)}) collective-permute-start(bf16[2048,128]{1,0:T(8,128)(2,1)S(1)} %get-tuple-element.20.refs_4_), channel_id=1, source_target_pairs={{0,1},{1,0},{2,3},{3,2},{4,5},{5,4},{6,7},{7,6},{8,9},{9,8},{10,11... | collective-permute-start | bytes 1572872 | tf_op jit(solution)/shard_map/ppermute | solution.py:227
  27.0 11.3 %collective-permute-start.12 = (bf16[512,128]{1,0:T(8,128)(2,1)S(1)}, bf16[512,128]{1,0:T(8,128)(2,1)S(1)}, u32[]{:S(2)}, u32[]{:S(2)}) collective-permute-start(bf16[512,128]{1,0:T(8,128)(2,1)S(1)} %get-tuple-element.29), channel_id=1, source_target_pairs={{0,2},{2,0},{4,6},{6,4},{8,10},{10,8},{12,14},{14,12},{1,3},{3,1},... | collective-permute-start | bytes 393224 | tf_op jit(solution)/shard_map/ppermute | solution.py:224
  30.0 8.8 %collective-permute-start.13 = (bf16[512,128]{1,0:T(8,128)(2,1)S(1)}, bf16[512,128]{1,0:T(8,128)(2,1)S(1)}, u32[]{:S(2)}, u32[]{:S(2)}) collective-permute-start(bf16[512,128]{1,0:T(8,128)(2,1)S(1)} %get-tuple-element.30), channel_id=1, source_target_pairs={{0,4},{2,6},{4,0},{6,2},{8,12},{10,14},{12,8},{14,10},{1,5},{3,7},... | collective-permute-start | bytes 393224 | tf_op jit(solution)/shard_map/ppermute | solution.py:224
  31.4 7.4 %collective-permute-start.14 = (bf16[512,128]{1,0:T(8,128)(2,1)S(1)}, bf16[512,128]{1,0:T(8,128)(2,1)S(1)}, u32[]{:S(2)}, u32[]{:S(2)}) collective-permute-start(bf16[512,128]{1,0:T(8,128)(2,1)S(1)} %get-tuple-element.31), channel_id=1, source_target_pairs={{0,6},{2,4},{4,2},{6,0},{8,14},{10,12},{12,10},{14,8},{1,7},{3,5},... | collective-permute-start | bytes 393224 | tf_op jit(solution)/shard_map/ppermute | solution.py:224
  33.7 11.1 %collective-permute-start.10 = (bf16[512,128]{1,0:T(8,128)(2,1)S(1)}, bf16[512,128]{1,0:T(8,128)(2,1)S(1)}, u32[]{:S(2)}, u32[]{:S(2)}) collective-permute-start(bf16[512,128]{1,0:T(8,128)(2,1)S(1)} %get-tuple-element.26), channel_id=1, source_target_pairs={{0,4},{2,6},{4,0},{6,2},{8,12},{10,14},{12,8},{14,10},{1,5},{3,7},... | collective-permute-start | bytes 393224 | tf_op jit(solution)/shard_map/ppermute | solution.py:224
  37.3 9.9 %collective-permute-start.11 = (bf16[512,128]{1,0:T(8,128)(2,1)S(1)}, bf16[512,128]{1,0:T(8,128)(2,1)S(1)}, u32[]{:S(2)}, u32[]{:S(2)}) collective-permute-start(bf16[512,128]{1,0:T(8,128)(2,1)S(1)} %get-tuple-element.27), channel_id=1, source_target_pairs={{0,6},{2,4},{4,2},{6,0},{8,14},{10,12},{12,10},{14,8},{1,7},{3,5},... | collective-permute-start | bytes 393224 | tf_op jit(solution)/shard_map/ppermute | solution.py:224
  38.3 8.9 %collective-permute-start.9 = (bf16[512,128]{1,0:T(8,128)(2,1)S(1)}, bf16[512,128]{1,0:T(8,128)(2,1)S(1)}, u32[]{:S(2)}, u32[]{:S(2)}) collective-permute-start(bf16[512,128]{1,0:T(8,128)(2,1)S(1)} %get-tuple-element.25), channel_id=1, source_target_pairs={{0,2},{2,0},{4,6},{6,4},{8,10},{10,8},{12,14},{14,12},{1,3},{3,1},... | collective-permute-start | bytes 393224 | tf_op jit(solution)/shard_map/ppermute | solution.py:224
  38.9 8.2 %collective-permute-start.15 = (bf16[512,128]{1,0:T(8,128)(2,1)S(1)}, bf16[512,128]{1,0:T(8,128)(2,1)S(1)}, u32[]{:S(2)}, u32[]{:S(2)}) collective-permute-start(bf16[512,128]{1,0:T(8,128)(2,1)S(1)} %add_convert_fusion), channel_id=1, source_target_pairs={{0,8},{2,10},{4,12},{6,14},{8,0},{10,2},{12,4},{14,6},{1,9},{3,11}... | collective-permute-start | bytes 393224 | tf_op jit(solution)/shard_map/ppermute | solution.py:224

commit v5 on v4

--- a/solution.py
+++ b/solution.py
@@ -216,7 +216,8 @@
     half = n_row // 2
     groups = [[0]]
     if direct:
-        groups = [list(range(half + 1)), list(range(half + 1, n_row))]
+        groups = [range(half + 1), range(half + 1, n_row - 1), range(n_row - 1, n_row)]
+        groups = [list(group) for group in groups if len(group)]
     stages = len(groups)
     col_at = lax.axis_index("col")
 

time: 48.4 us -> 48 us (level); the launches traced: 48 us -> 48.1 us
  Pallas kernels: 10.4 us -> 18.8 us
  starting transfers between devices: 23.8 us -> 18.4 us
  waiting for transfers between devices: 11.5 us -> 8.69 us
    ppermute x14, starting transfers between devices: 23.7 us -> 18.3 us  [swap_row(): return lax.ppermute(x, 'row', [(i, i ^ k) for i in range(n_row)])]
    pallas_call x2 -> x3, Pallas kernels: 4 us -> 7.49 us  [body(): pl.pallas_call(functools.partial(user_kernel, stage, stages, size, last),...]
    pallas_call x2, Pallas kernels: 4.01 us -> 7.38 us  [body(): pl.pallas_call(functools.partial(item_kernel, tuple(parts), stages, first...]
    ppermute x14, waiting for transfers between devices: 9.64 us -> 6.79 us  [swap_row(): return lax.ppermute(x, 'row', [(i, i ^ k) for i in range(n_row)])]
    pallas_call x1, Pallas kernels: 1.52 us -> 3.02 us  [body(): pl.pallas_call(functools.partial(plan_kernel, shard_tiles, keys, edges),...]
  transfers between devices with their start and end apart: 16 -> 16, of which waited for: 8 -> 6; matrix products, arithmetic and copies ran while one was open for 2% -> 2% of each run, Pallas kernels for 12% -> 27%
where the time goes in v5:
time: 48 us; the launch traced here: 48.1 us
  Pallas kernels  18.8 us (39%)
  starting transfers between devices  18.4 us (38%)
  waiting for transfers between devices  8.69 us (18%)
  between operations  1.51 us (3%)
  local copies, waits for them, and re-layouts  0.75 us (2%)
    ppermute x14, starting transfers between devices, swap_row(): return lax.ppermute(x, 'row', [(i, i ^ k) for i in range(n_row)])  18.3 us
    pallas_call x3, Pallas kernels, body(): pl.pallas_call(functools.partial(user_kernel, stage, stages, size, last),...  7.49 us
    pallas_call x2, Pallas kernels, body(): pl.pallas_call(functools.partial(item_kernel, tuple(parts), stages, first...  7.38 us
    ppermute x14, waiting for transfers between devices, swap_row(): return lax.ppermute(x, 'row', [(i, i ^ k) for i in range(n_row)])  6.79 us
    pallas_call x1, Pallas kernels, body(): pl.pallas_call(functools.partial(plan_kernel, shard_tiles, keys, edges),...  3.02 us
    ppermute x2, waiting for transfers between devices, swap_col(): return lax.ppermute(x, 'col', [(i, i ^ 1) for i in range(n_col)])  1.9 us
  transfers between devices with their start and end apart: 16, of which 6 were waited for; matrix products, arithmetic and copies ran while one was open for 2% of the time, Pallas kernels for 27%

profile of v5, /device:TPU:0, one launch (start us, length us, event | category | flops | bytes accessed | tf_op | source)
XLA Modules:
  0.0 48.1 jit_solution(17808323907667548783)
XLA Ops:
  0.6 0.0 copy-start.2
  0.6 0.0 copy-start.3
  0.7 0.0 copy-start.4
  0.7 0.0 copy-start.5
  0.7 0.0 copy-start
  0.7 0.0 copy-start.1
  0.7 4.1 %collective-permute-start = (bf16[512,128]{1,0:T(8,128)(2,1)}, bf16[512,128]{1,0:T(8,128)(2,1)S(1)}, u32[]{:S(2)}, u32[]{:S(2)}) collective-permute-start(bf16[512,128]{1,0:T(8,128)(2,1)} %items.1), channel_id=1, source_target_pairs={{0,8},{2,10},{4,12},{6,14},{8,0},{10,2},{12,4},{14,6},{1,9},{3,11}... | collective-permute-start | bytes 393224 | tf_op jit(solution)/shard_map/ppermute | solution.py:225
  4.8 1.5 %collective-permute-start.3 = (bf16[512,128]{1,0:T(8,128)(2,1)}, bf16[512,128]{1,0:T(8,128)(2,1)S(1)}, u32[]{:S(2)}, u32[]{:S(2)}) collective-permute-start(bf16[512,128]{1,0:T(8,128)(2,1)} %items.1), channel_id=1, source_target_pairs={{0,2},{2,0},{4,6},{6,4},{8,10},{10,8},{12,14},{14,12},{1,3},{3,1},... | collective-permute-start | bytes 393224 | tf_op jit(solution)/shard_map/ppermute | solution.py:225
  6.3 1.6 %collective-permute-start.4 = (bf16[512,128]{1,0:T(8,128)(2,1)}, bf16[512,128]{1,0:T(8,128)(2,1)S(1)}, u32[]{:S(2)}, u32[]{:S(2)}) collective-permute-start(bf16[512,128]{1,0:T(8,128)(2,1)} %items.1), channel_id=1, source_target_pairs={{0,4},{2,6},{4,0},{6,2},{8,12},{10,14},{12,8},{14,10},{1,5},{3,7},... | collective-permute-start | bytes 393224 | tf_op jit(solution)/shard_map/ppermute | solution.py:225
  7.9 0.4 collective-permute-start.5
  8.3 0.0 collective-permute-start.6
  8.3 0.1 clear.1.total.refs_10_
  9.0 3.0 %plan.1.refs_0_ = s32[651]{0:T(1024)S(4)} custom-call(s32[1,1]{1,0:T(1,128)S(6)} %copy.15.live, s32[192]{0:T(256)S(1)} %bitcast.14, s32[192]{0:T(256)S(1)} %bitcast.15, f32[2048,128]{1,0:T(8,128)S(1)} %clear.1.total.refs_10_), custom_call_target="tpu_custom_call" | custom-call | tf_op jit(solution)/shard_map/plan/pallas_call | solution.py:251
  12.1 0.0 collective-permute-done.refs_7_
  12.1 0.9 %collective-permute-start.1 = (bf16[512,128]{1,0:T(8,128)(2,1)S(1)}, bf16[512,128]{1,0:T(8,128)(2,1)S(1)}, u32[]{:S(2)}, u32[]{:S(2)}) collective-permute-start(bf16[512,128]{1,0:T(8,128)(2,1)S(1)} %collective-permute-done.refs_7_), channel_id=1, source_target_pairs={{0,2},{2,0},{4,6},{6,4},{8,10},{10,8},{12,14},{14,12},{1,3},{3,1},... | collective-permute-start | bytes 393224 | tf_op jit(solution)/shard_map/ppermute | solution.py:225
  13.0 0.0 collective-permute-done.3.refs_4_
  13.0 1.0 %collective-permute-start.2 = (bf16[512,128]{1,0:T(8,128)(2,1)S(1)}, bf16[512,128]{1,0:T(8,128)(2,1)S(1)}, u32[]{:S(2)}, u32[]{:S(2)}) collective-permute-start(bf16[512,128]{1,0:T(8,128)(2,1)S(1)} %collective-permute-done.refs_7_), channel_id=1, source_target_pairs={{0,4},{2,6},{4,0},{6,2},{8,12},{10,14},{12,8},{14,10},{1,5},{3,7},... | collective-permute-start | bytes 393224 | tf_op jit(solution)/shard_map/ppermute | solution.py:225
  14.0 0.0 collective-permute-done.4.refs_5_
  14.0 1.6 %collective-permute-start.7 = (bf16[512,128]{1,0:T(8,128)(2,1)S(1)}, bf16[512,128]{1,0:T(8,128)(2,1)S(1)}, u32[]{:S(2)}, u32[]{:S(2)}) collective-permute-start(bf16[512,128]{1,0:T(8,128)(2,1)S(1)} %collective-permute-done.refs_7_), channel_id=1, source_target_pairs={{0,6},{2,4},{4,2},{6,0},{8,14},{10,12},{12,10},{14,8},{1,7},{3,5},... | collective-permute-start | bytes 393224 | tf_op jit(solution)/shard_map/ppermute | solution.py:225
  15.6 0.2 collective-permute-done.5.refs_6_
  15.8 0.0 collective-permute-done.6.refs_9_
  15.8 4.1 %user_terms.3 = (bf16[2560,128]{1,0:T(8,128)(2,1)S(1)}, f32[2048,128]{1,0:T(8,128)S(1)}, bf16[2048,128]{1,0:T(8,128)(2,1)S(1)}) custom-call(s32[651]{0:T(1024)S(4)} %plan.1.refs_0_, bf16[192,128,128]{2,1,0:T(8,128)(2,1)S(1)} %bitcast.4, s32[192,16,128]{2,1,0:T(8,128)S(1)} %bitcast.9, ...), custom_call_target="tpu_custom_call", output_to_operand_aliasing={{1}: (10, {})} | custom-call | flops 2684354560 | bytes 4194304 | tf_op jit(solution)/shard_map/user_terms/pallas_call | solution.py:277
  20.0 0.0 collective-permute-done.1.refs_3_
  20.0 0.0 collective-permute-done.2.refs_4_
  20.0 2.0 %user_terms.4 = (bf16[1024,128]{1,0:T(8,128)(2,1)S(1)}, f32[2048,128]{1,0:T(8,128)S(1)}) custom-call(s32[651]{0:T(1024)S(4)} %plan.1.refs_0_, bf16[192,128,128]{2,1,0:T(8,128)(2,1)S(1)} %bitcast.5, s32[192,16,128]{2,1,0:T(8,128)S(1)} %bitcast.10, bf16[512,128]{1,0:T(8,128)(2,1)S(1)} %collective-permute-done.1.refs_3_, ...), custom_call_target="tpu_custom_call", output_to_operand_aliasing={{1}: (6, {})} | custom-call | flops 2684354560 | bytes 4194304 | tf_op jit(solution)/shard_map/user_terms/pallas_call | solution.py:277
  22.1 0.0 collective-permute-done.7.refs_3_
  22.1 1.3 %user_terms.5 = (bf16[512,128]{1,0:T(8,128)(2,1)S(1)}, f32[2048,128]{1,0:T(8,128)S(1)}, bf16[2048,128]{1,0:T(8,128)(2,1)S(1)}) custom-call(s32[651]{0:T(1024)S(4)} %plan.1.refs_0_, bf16[192,128,128]{2,1,0:T(8,128)(2,1)S(1)} %bitcast.6, s32[192,16,128]{2,1,0:T(8,128)S(1)} %bitcast.11, ...), custom_call_target="tpu_custom_call", output_to_operand_aliasing={{1}: (5, {})} | custom-call | flops 2684354560 | bytes 4194304 | tf_op jit(solution)/shard_map/user_terms/pallas_call | solution.py:277
  23.4 0.1 collective-permute-start.8
  23.5 1.9 %collective-permute-done.8.refs_6_ = bf16[2048,128]{1,0:T(8,128)(2,1)S(1)} collective-permute-done((bf16[2048,128]{1,0:T(8,128)(2,1)S(1)}, bf16[2048,128]{1,0:T(8,128)(2,1)S(1)}, u32[]{:S(2)}, u32[]{:S(2)}) %collective-permute-start.8) | collective-permute-done | bytes 524320 | tf_op jit(solution)/shard_map/ppermute | solution.py:228
  25.4 3.5 %item_terms.2 = (bf16[512,128]{1,0:T(8,128)(2,1)S(1)}, bf16[512,128]{1,0:T(8,128)(2,1)S(1)}, bf16[512,128]{1,0:T(8,128)(2,1)S(1)}, bf16[2048,128]{1,0:T(8,128)(2,1)S(1)}, bf16[2048,128]{1,0:T(8,128)(2,1)S(1)}) custom-call(s32[651]{0:T(1024)S(4)} %plan.1.refs_0_, bf16[192,128,128]{2,1,0:T(8,128)(2,1)S(1)} %bitcast.7, s32[192,16,128]{2,1,0:T(8,128)S(1)} %bitcast.12, ...), custom_call_target="tpu_custom_call" | custom-call | flops 2684354560 | bytes 4194304 | tf_op jit(solution)/shard_map/item_terms/pallas_call | solution.py:311
  28.9 0.1 collective-permute-start.14
  28.9 0.2 collective-permute-start.13
  29.1 3.3 %collective-permute-start.12 = (bf16[512,128]{1,0:T(8,128)(2,1)S(1)}, bf16[512,128]{1,0:T(8,128)(2,1)S(1)}, u32[]{:S(2)}, u32[]{:S(2)}) collective-permute-start(bf16[512,128]{1,0:T(8,128)(2,1)S(1)} %get-tuple-element.33), channel_id=1, source_target_pairs={{0,2},{2,0},{4,6},{6,4},{8,10},{10,8},{12,14},{14,12},{1,3},{3,1},... | collective-permute-start | bytes 393224 | tf_op jit(solution)/shard_map/ppermute | solution.py:225
  32.4 3.9 %item_terms.3 = (f32[512,128]{1,0:T(8,128)S(1)}, bf16[512,128]{1,0:T(8,128)(2,1)S(1)}, bf16[512,128]{1,0:T(8,128)(2,1)S(1)}, bf16[512,128]{1,0:T(8,128)(2,1)S(1)}, f32[512,128]{1,0:T(8,128)S(1)}) custom-call(s32[651]{0:T(1024)S(4)} %plan.1.refs_0_, bf16[192,128,128]{2,1,0:T(8,128)(2,1)S(1)} %bitcast.8, s32[192,16,128]{2,1,0:T(8,128)S(1)} %bitcast.13, ...), custom_call_target="tpu_custom_call" | custom-call | flops 2684354560 | bytes 4194304 | tf_op jit(solution)/shard_map/item_terms/pallas_call | solution.py:311
  36.3 0.1 collective-permute-start.9
  36.4 0.1 collective-permute-start.10
  36.5 0.0 collective-permute-done.14
  36.5 3.4 %collective-permute-start.11 = (bf16[512,128]{1,0:T(8,128)(2,1)S(1)}, bf16[512,128]{1,0:T(8,128)(2,1)S(1)}, u32[]{:S(2)}, u32[]{:S(2)}) collective-permute-start(bf16[512,128]{1,0:T(8,128)(2,1)S(1)} %get-tuple-element.31), channel_id=1, source_target_pairs={{0,6},{2,4},{4,2},{6,0},{8,14},{10,12},{12,10},{14,8},{1,7},{3,5},... | collective-permute-start | bytes 393224 | tf_op jit(solution)/shard_map/ppermute | solution.py:225
  39.9 0.0 collective-permute-done.13
  39.9 0.0 collective-permute-done.12
  39.9 0.1 add_convert_fusion
  39.9 0.1 collective-permute-start.15
  40.0 0.7 %constant_dynamic-slice_fusion = bf16[1024,128]{1,0:T(8,128)(2,1)} fusion(bf16[2048,128]{1,0:T(8,128)(2,1)S(1)} %get-tuple-element.25.refs_4_, s32[]{:T(128)S(6)} %select_n.3), kind=kLoop, calls=%fused_computation.1 | loop fusion | bytes 524292 | tf_op jit(solution)/shard_map/dynamic_slice | solution.py:325
  40.7 1.0 %collective-permute-done.9.refs_1_ = bf16[512,128]{1,0:T(8,128)(2,1)S(1)} collective-permute-done((bf16[512,128]{1,0:T(8,128)(2,1)S(1)}, bf16[512,128]{1,0:T(8,128)(2,1)S(1)}, u32[]{:S(2)}, u32[]{:S(2)}) %collective-permute-start.9) | collective-permute-done | bytes 131104 | tf_op jit(solution)/shard_map/ppermute | solution.py:225
  41.7 1.1 %collective-permute-done.10.refs_2_ = bf16[512,128]{1,0:T(8,128)(2,1)S(1)} collective-permute-done((bf16[512,128]{1,0:T(8,128)(2,1)S(1)}, bf16[512,128]{1,0:T(8,128)(2,1)S(1)}, u32[]{:S(2)}, u32[]{:S(2)}) %collective-permute-start.10) | collective-permute-done | bytes 131104 | tf_op jit(solution)/shard_map/ppermute | solution.py:225
  42.8 2.2 %collective-permute-done.11.refs_3_ = bf16[512,128]{1,0:T(8,128)(2,1)S(1)} collective-permute-done((bf16[512,128]{1,0:T(8,128)(2,1)S(1)}, bf16[512,128]{1,0:T(8,128)(2,1)S(1)}, u32[]{:S(2)}, u32[]{:S(2)}) %collective-permute-start.11) | collective-permute-done | bytes 131104 | tf_op jit(solution)/shard_map/ppermute | solution.py:225
  45.0 2.3 %collective-permute-done.15.refs_4_ = bf16[512,128]{1,0:T(8,128)(2,1)S(1)} collective-permute-done((bf16[512,128]{1,0:T(8,128)(2,1)S(1)}, bf16[512,128]{1,0:T(8,128)(2,1)S(1)}, u32[]{:S(2)}, u32[]{:S(2)}) %collective-permute-start.15) | collective-permute-done | bytes 131104 | tf_op jit(solution)/shard_map/ppermute | solution.py:225
  47.3 0.8 %finish.1 = bf16[512,128]{1,0:T(8,128)(2,1)} custom-call(bf16[512,128]{1,0:T(8,128)(2,1)S(1)} %copy-done.2, f32[512,128]{1,0:T(8,128)S(1)} %get-tuple-element.28.refs_0_, bf16[512,128]{1,0:T(8,128)(2,1)S(1)} %collective-permute-done.9.refs_1_, bf16[512,128]{1,0:T(8,128)(2,1)S(1)} %collective-permute-done.10.refs_2_, ...), custom_call_target="tpu_custom_call" | custom-call | tf_op jit(solution)/shard_map/finish/pallas_call | solution.py:332
  (6 shorter events, 0.0 us)
Async XLA Ops:
  0.6 15.2 %copy-start.2 = (bf16[512,128]{1,0:T(8,128)(2,1)S(1)}, bf16[512,128]{1,0:T(8,128)(2,1)}, u32[]{:S(2)}) copy-start(bf16[512,128]{1,0:T(8,128)(2,1)} %items.1) | copy-start | bytes 393220
  0.6 15.2 %copy-start.3 = (bf16[1024,128]{1,0:T(8,128)(2,1)S(1)}, bf16[1024,128]{1,0:T(8,128)(2,1)}, u32[]{:S(2)}) copy-start(bf16[1024,128]{1,0:T(8,128)(2,1)} %refs_8_.1) | copy-start | bytes 786436
  0.7 8.4 %copy-start.4 = (s32[1,1,192]{2,1,0:T(1,128)S(1)}, s32[1,1,192]{2,1,0:T(1,128)}, u32[]{:S(2)}) copy-start(s32[1,1,192]{2,1,0:T(1,128)} %param.11) | copy-start | bytes 2308
  0.7 8.4 %copy-start.5 = (s32[1,1,192]{2,1,0:T(1,128)S(1)}, s32[1,1,192]{2,1,0:T(1,128)}, u32[]{:S(2)}) copy-start(s32[1,1,192]{2,1,0:T(1,128)} %param.12) | copy-start | bytes 2308
  0.7 15.1 %copy-start = (bf16[1,1,192,128,128]{4,3,2,1,0:T(8,128)(2,1)S(1)}, bf16[1,1,192,128,128]{4,3,2,1,0:T(8,128)(2,1)}, u32[]{:S(2)}) copy-start(bf16[1,1,192,128,128]{4,3,2,1,0:T(8,128)(2,1)} %param.9) | copy-start | bytes 18874372
  0.7 15.1 %copy-start.1 = (s32[1,1,192,16,128]{4,3,2,1,0:T(8,128)S(1)}, s32[1,1,192,16,128]{4,3,2,1,0:T(8,128)}, u32[]{:S(2)}) copy-start(s32[1,1,192,16,128]{4,3,2,1,0:T(8,128)} %param.10) | copy-start | bytes 4718596
  0.7 11.4 %collective-permute-start = (bf16[512,128]{1,0:T(8,128)(2,1)}, bf16[512,128]{1,0:T(8,128)(2,1)S(1)}, u32[]{:S(2)}, u32[]{:S(2)}) collective-permute-start(bf16[512,128]{1,0:T(8,128)(2,1)} %items.1), channel_id=1, source_target_pairs={{0,8},{2,10},{4,12},{6,14},{8,0},{10,2},{12,4},{14,6},{1,9},{3,11}... | collective-permute-start | bytes 393224 | tf_op jit(solution)/shard_map/ppermute | solution.py:225
  4.8 8.2 %collective-permute-start.3 = (bf16[512,128]{1,0:T(8,128)(2,1)}, bf16[512,128]{1,0:T(8,128)(2,1)S(1)}, u32[]{:S(2)}, u32[]{:S(2)}) collective-permute-start(bf16[512,128]{1,0:T(8,128)(2,1)} %items.1), channel_id=1, source_target_pairs={{0,2},{2,0},{4,6},{6,4},{8,10},{10,8},{12,14},{14,12},{1,3},{3,1},... | collective-permute-start | bytes 393224 | tf_op jit(solution)/shard_map/ppermute | solution.py:225
  6.3 7.7 %collective-permute-start.4 = (bf16[512,128]{1,0:T(8,128)(2,1)}, bf16[512,128]{1,0:T(8,128)(2,1)S(1)}, u32[]{:S(2)}, u32[]{:S(2)}) collective-permute-start(bf16[512,128]{1,0:T(8,128)(2,1)} %items.1), channel_id=1, source_target_pairs={{0,4},{2,6},{4,0},{6,2},{8,12},{10,14},{12,8},{14,10},{1,5},{3,7},... | collective-permute-start | bytes 393224 | tf_op jit(solution)/shard_map/ppermute | solution.py:225
  7.9 7.9 %collective-permute-start.5 = (bf16[512,128]{1,0:T(8,128)(2,1)}, bf16[512,128]{1,0:T(8,128)(2,1)S(1)}, u32[]{:S(2)}, u32[]{:S(2)}) collective-permute-start(bf16[512,128]{1,0:T(8,128)(2,1)} %items.1), channel_id=1, source_target_pairs={{0,6},{2,4},{4,2},{6,0},{8,14},{10,12},{12,10},{14,8},{1,7},{3,5},... | collective-permute-start | bytes 393224 | tf_op jit(solution)/shard_map/ppermute | solution.py:225
  8.3 7.5 %collective-permute-start.6 = (bf16[1024,128]{1,0:T(8,128)(2,1)}, bf16[1024,128]{1,0:T(8,128)(2,1)S(1)}, u32[]{:S(2)}, u32[]{:S(2)}) collective-permute-start(bf16[1024,128]{1,0:T(8,128)(2,1)} %refs_8_.1), channel_id=1, source_target_pairs={{0,1},{1,0},{2,3},{3,2},{4,5},{5,4},{6,7},{7,6},{8,9},{9,8},{10,11... | collective-permute-start | bytes 786440 | tf_op jit(solution)/shard_map/ppermute | solution.py:228
  12.1 7.9 %collective-permute-start.1 = (bf16[512,128]{1,0:T(8,128)(2,1)S(1)}, bf16[512,128]{1,0:T(8,128)(2,1)S(1)}, u32[]{:S(2)}, u32[]{:S(2)}) collective-permute-start(bf16[512,128]{1,0:T(8,128)(2,1)S(1)} %collective-permute-done.refs_7_), channel_id=1, source_target_pairs={{0,2},{2,0},{4,6},{6,4},{8,10},{10,8},{12,14},{14,12},{1,3},{3,1},... | collective-permute-start | bytes 393224 | tf_op jit(solution)/shard_map/ppermute | solution.py:225
  13.0 7.0 %collective-permute-start.2 = (bf16[512,128]{1,0:T(8,128)(2,1)S(1)}, bf16[512,128]{1,0:T(8,128)(2,1)S(1)}, u32[]{:S(2)}, u32[]{:S(2)}) collective-permute-start(bf16[512,128]{1,0:T(8,128)(2,1)S(1)} %collective-permute-done.refs_7_), channel_id=1, source_target_pairs={{0,4},{2,6},{4,0},{6,2},{8,12},{10,14},{12,8},{14,10},{1,5},{3,7},... | collective-permute-start | bytes 393224 | tf_op jit(solution)/shard_map/ppermute | solution.py:225
  14.0 8.0 %collective-permute-start.7 = (bf16[512,128]{1,0:T(8,128)(2,1)S(1)}, bf16[512,128]{1,0:T(8,128)(2,1)S(1)}, u32[]{:S(2)}, u32[]{:S(2)}) collective-permute-start(bf16[512,128]{1,0:T(8,128)(2,1)S(1)} %collective-permute-done.refs_7_), channel_id=1, source_target_pairs={{0,6},{2,4},{4,2},{6,0},{8,14},{10,12},{12,10},{14,8},{1,7},{3,5},... | collective-permute-start | bytes 393224 | tf_op jit(solution)/shard_map/ppermute | solution.py:225
  23.4 2.0 %collective-permute-start.8 = (bf16[2048,128]{1,0:T(8,128)(2,1)S(1)}, bf16[2048,128]{1,0:T(8,128)(2,1)S(1)}, u32[]{:S(2)}, u32[]{:S(2)}) collective-permute-start(bf16[2048,128]{1,0:T(8,128)(2,1)S(1)} %get-tuple-element.24.refs_5_), channel_id=1, source_target_pairs={{0,1},{1,0},{2,3},{3,2},{4,5},{5,4},{6,7},{7,6},{8,9},{9,8},{10,11... | collective-permute-start | bytes 1572872 | tf_op jit(solution)/shard_map/ppermute | solution.py:228
  28.9 7.6 %collective-permute-start.14 = (bf16[512,128]{1,0:T(8,128)(2,1)S(1)}, bf16[512,128]{1,0:T(8,128)(2,1)S(1)}, u32[]{:S(2)}, u32[]{:S(2)}) collective-permute-start(bf16[512,128]{1,0:T(8,128)(2,1)S(1)} %get-tuple-element.35), channel_id=1, source_target_pairs={{0,6},{2,4},{4,2},{6,0},{8,14},{10,12},{12,10},{14,8},{1,7},{3,5},... | collective-permute-start | bytes 393224 | tf_op jit(solution)/shard_map/ppermute | solution.py:225
  28.9 10.9 %collective-permute-start.13 = (bf16[512,128]{1,0:T(8,128)(2,1)S(1)}, bf16[512,128]{1,0:T(8,128)(2,1)S(1)}, u32[]{:S(2)}, u32[]{:S(2)}) collective-permute-start(bf16[512,128]{1,0:T(8,128)(2,1)S(1)} %get-tuple-element.34), channel_id=1, source_target_pairs={{0,4},{2,6},{4,0},{6,2},{8,12},{10,14},{12,8},{14,10},{1,5},{3,7},... | collective-permute-start | bytes 393224 | tf_op jit(solution)/shard_map/ppermute | solution.py:225
  29.1 10.8 %collective-permute-start.12 = (bf16[512,128]{1,0:T(8,128)(2,1)S(1)}, bf16[512,128]{1,0:T(8,128)(2,1)S(1)}, u32[]{:S(2)}, u32[]{:S(2)}) collective-permute-start(bf16[512,128]{1,0:T(8,128)(2,1)S(1)} %get-tuple-element.33), channel_id=1, source_target_pairs={{0,2},{2,0},{4,6},{6,4},{8,10},{10,8},{12,14},{14,12},{1,3},{3,1},... | collective-permute-start | bytes 393224 | tf_op jit(solution)/shard_map/ppermute | solution.py:225
  36.3 5.4 %collective-permute-start.9 = (bf16[512,128]{1,0:T(8,128)(2,1)S(1)}, bf16[512,128]{1,0:T(8,128)(2,1)S(1)}, u32[]{:S(2)}, u32[]{:S(2)}) collective-permute-start(bf16[512,128]{1,0:T(8,128)(2,1)S(1)} %get-tuple-element.29), channel_id=1, source_target_pairs={{0,2},{2,0},{4,6},{6,4},{8,10},{10,8},{12,14},{14,12},{1,3},{3,1},... | collective-permute-start | bytes 393224 | tf_op jit(solution)/shard_map/ppermute | solution.py:225
  36.4 6.4 %collective-permute-start.10 = (bf16[512,128]{1,0:T(8,128)(2,1)S(1)}, bf16[512,128]{1,0:T(8,128)(2,1)S(1)}, u32[]{:S(2)}, u32[]{:S(2)}) collective-permute-start(bf16[512,128]{1,0:T(8,128)(2,1)S(1)} %get-tuple-element.30), channel_id=1, source_target_pairs={{0,4},{2,6},{4,0},{6,2},{8,12},{10,14},{12,8},{14,10},{1,5},{3,7},... | collective-permute-start | bytes 393224 | tf_op jit(solution)/shard_map/ppermute | solution.py:225
  36.5 8.5 %collective-permute-start.11 = (bf16[512,128]{1,0:T(8,128)(2,1)S(1)}, bf16[512,128]{1,0:T(8,128)(2,1)S(1)}, u32[]{:S(2)}, u32[]{:S(2)}) collective-permute-start(bf16[512,128]{1,0:T(8,128)(2,1)S(1)} %get-tuple-element.31), channel_id=1, source_target_pairs={{0,6},{2,4},{4,2},{6,0},{8,14},{10,12},{12,10},{14,8},{1,7},{3,5},... | collective-permute-start | bytes 393224 | tf_op jit(solution)/shard_map/ppermute | solution.py:225
  39.9 7.4 %collective-permute-start.15 = (bf16[512,128]{1,0:T(8,128)(2,1)S(1)}, bf16[512,128]{1,0:T(8,128)(2,1)S(1)}, u32[]{:S(2)}, u32[]{:S(2)}) collective-permute-start(bf16[512,128]{1,0:T(8,128)(2,1)S(1)} %add_convert_fusion), channel_id=1, source_target_pairs={{0,8},{2,10},{4,12},{6,14},{8,0},{10,2},{12,4},{14,6},{1,9},{3,11}... | collective-permute-start | bytes 393224 | tf_op jit(solution)/shard_map/ppermute | solution.py:225

commit v6 on v5

--- a/solution.py
+++ b/solution.py
@@ -10,8 +10,7 @@
 BLOCK = 128
 UNROLL = 24
 TAIL = 8
-FIELD = 10
-PLAN_UNROLL = 8
+FIELD = 8
 VMEM_LIMIT = 16 * 1024 * 1024
 
 NN = (((1,), (0,)), ((), ()))
@@ -37,53 +36,58 @@
     return slice(index * BLOCK, (index + 1) * BLOCK)
 
 
-def plan_kernel(shard_tiles, keys, edges, live, rows, cols, total, meta):
+def plan_kernel(shard_tiles, keys, edges, region, live, rows, cols, total, meta, found, sem):
     count = live[0, 0]
-    me = lax.axis_index("row")
+    slots = cols.shape[1]
     stages = len(edges)
-    region = (meta.shape[0] - stages) // stages
-
-    def put(i, places):
-        places = list(places)
-        packed = []
-        for j in range(PLAN_UNROLL):
-            t = i * PLAN_UNROLL + j
-            at = jnp.minimum(t, rows.shape[0] - 1)
-            v = cols[at]
-            if stages > 1:
-                v = (v ^ (me * shard_tiles)) & (keys * shard_tiles - 1)
-            packed.append((t, v, at + (rows[at] << FIELD)))
-        for t, v, word in packed:
-            spot, base = places[0], jnp.int32(0)
-            inside = [v < edges[0]]
-            for stage in range(1, stages):
-                past = v >= edges[stage - 1]
-                spot = jnp.where(past, stage * region + places[stage], spot)
-                base = jnp.where(past, edges[stage - 1], base)
-                inside.append(past & (v < edges[stage]))
-            meta[spot] = word + ((v - base) << 2 * FIELD)
-            for stage in range(stages):
-                places[stage] += jnp.where(inside[stage] & (t < count), 1, 0)
-        return tuple(places)
-
-    trips = (count + PLAN_UNROLL - 1) // PLAN_UNROLL
-    places = lax.fori_loop(0, trips, put, (jnp.int32(0),) * stages)
-    for stage in range(stages):
-        for at in range(UNROLL):
-            meta[stage * region + places[stage] + at] = 0
-        meta[stages * region + stage] = places[stage]
-
-
-def stage_loop(stage, stages, meta, step_of):
-    region = (meta.shape[0] - stages) // stages
-    live = meta[stages * region + stage]
+    square = (slots, slots)
+    down = lax.broadcasted_iota(jnp.int32, square, 0)
+    across = lax.broadcasted_iota(jnp.int32, square, 1)
+
+    v = cols[...]
+    if stages > 1:
+        v = (v ^ (lax.axis_index("row") * shard_tiles)) & (keys * shard_tiles - 1)
+    stage = jnp.zeros_like(v)
+    first = jnp.zeros_like(v)
+    for i in range(1, stages):
+        past = v >= edges[i - 1]
+        stage = jnp.where(past, i, stage)
+        first = jnp.where(past, edges[i - 1], first)
+    word = across[:1] + (rows[...] << FIELD) + ((v - first) << 2 * FIELD)
+
+    def column(row):
+        spread = jnp.broadcast_to(row.astype(jnp.float32), square)
+        return jnp.sum(jnp.where(down == across, spread, 0.0), axis=1, keepdims=True)
+
+    stage_down = column(stage)
+    word_down = column(word)
+    stage_across = jnp.broadcast_to(stage.astype(jnp.float32), square)
+    ahead = (stage_across == stage_down) & (across < down) & (across < count)
+    place = jnp.sum(jnp.where(ahead, 1.0, 0.0), axis=1, keepdims=True)
+    place = place + stage_down * region
+    here = lax.broadcasted_iota(jnp.int32, (slots, 1), 0) < count
+    place = jnp.where(here, place, -1.0)
+    wide = (slots, found.shape[1])
+    at = lax.broadcasted_iota(jnp.int32, wide, 1).astype(jnp.float32)
+    out = jnp.sum(jnp.where(at == place, word_down, 0.0), axis=0, keepdims=True)
+    for i in range(stages):
+        size = jnp.sum(jnp.where(here & (stage_down == i), 1.0, 0.0), axis=0, keepdims=True)
+        out = jnp.where(at[:1] == stages * region + i, size, out)
+    found[...] = out.astype(jnp.int32)
+    copy = pltpu.make_async_copy(found, meta, sem)
+    copy.start()
+    copy.wait()
+
+
+def stage_loop(stage, stages, region, meta, step_of):
+    live = meta[0, stages * region + stage]
     mask = (1 << FIELD) - 1
 
     def group(start, size):
         entries = []
         for j in range(size):
             at = start + j
-            word = meta[stage * region + at]
+            word = meta[0, stage * region + at]
             entries.append(
                 (word & mask, (word >> FIELD) & mask, word >> 2 * FIELD, at < live)
             )
@@ -125,7 +129,7 @@
     total[...] = jnp.zeros_like(total)
 
 
-def user_kernel(stage, stages, group, last, *refs):
+def user_kernel(stage, stages, region, group, last, *refs):
     meta, tiles, words = refs[:3]
     shards = refs[3 : 3 + group]
     if stage == 0:
@@ -150,12 +154,12 @@
         for (slot, u, v, live), term in zip(entries, terms):
             total[rows_of(u), :] += term
 
-    stage_loop(stage, stages, meta, step_of)
+    stage_loop(stage, stages, region, meta, step_of)
     if last:
         refs[-2][...] = total[...].astype(jnp.bfloat16)
 
 
-def item_kernel(parts, stages, first, *refs):
+def item_kernel(parts, stages, region, first, *refs):
     meta, tiles, words = refs[:3]
     flips = refs[3 : 3 + len(parts)]
     refs = refs[3 + len(parts) :]
@@ -186,7 +190,7 @@
             for (slot, u, v, live), term in zip(entries, terms):
                 total[rows_of(v + base), :] += term
 
-        stage_loop(stage, stages, meta, step_of)
+        stage_loop(stage, stages, region, meta, step_of)
         base += flipped.shape[0] // BLOCK
     size = outs[0].shape[0]
     for s, out in enumerate(outs):
@@ -248,18 +252,20 @@
     shard_tiles = wide // BLOCK
     edges = [(group[-1] + 1) * shard_tiles for group in groups]
 
+    words_out = -(-(stages * pad + stages) // BLOCK) * BLOCK
     meta = pl.pallas_call(
-        functools.partial(plan_kernel, shard_tiles, keys, edges),
-        out_shape=pltpu.SMEM((stages * pad + stages,), jnp.int32),
-        in_specs=[smem()] * 3 + [anywhere()],
+        functools.partial(plan_kernel, shard_tiles, keys, edges, pad),
+        out_shape=pltpu.SMEM((1, words_out), jnp.int32),
+        in_specs=[smem(), vmem(), vmem(), anywhere()],
         out_specs=smem(),
+        scratch_shapes=[pltpu.VMEM((1, words_out), jnp.int32), pltpu.SemaphoreType.DMA],
         compiler_params=params(),
         name="plan",
-    )(tile_count, tile_rows[0, 0], tile_cols[0, 0], total)
+    )(tile_count, tile_rows[0], tile_cols[0], total)
 
     cost = pl.CostEstimate(
-        flops=20 * slots * BLOCK * BLOCK * rank // stages,
-        bytes_accessed=(slots // stages) * BLOCK * BLOCK * 4,
+        flops=slots * BLOCK * BLOCK,
+        bytes_accessed=0,
         transcendentals=0,
     )
     flipped = []
@@ -275,7 +281,7 @@
         if last:
             shapes.append(jax.ShapeDtypeStruct(user_shape, jnp.bfloat16))
         outs = pl.pallas_call(
-            functools.partial(user_kernel, stage, stages, size, last),
+            functools.partial(user_kernel, stage, stages, pad, size, last),
             out_shape=tuple(shapes),
             in_specs=[smem()] + [vmem()] * (len(operands) - 1),
             out_specs=tuple([vmem()] * len(shapes)),
@@ -309,7 +315,7 @@
         else:
             operands += [fresh, turned]
         outs = pl.pallas_call(
-            functools.partial(item_kernel, tuple(parts), stages, first),
+            functools.partial(item_kernel, tuple(parts), stages, pad, first),
             out_shape=tuple(shapes),
             in_specs=[smem()] + [vmem()] * (len(operands) - 1),
             out_specs=tuple([vmem()] * len(shapes)),

time: 48 us -> 48 us (level)
  the two profiles are of different devices: /device:TPU:0 before, /device:TPU:8 now
where the time goes in v6:
time: 48 us; the launch traced here: 47.9 us
  starting transfers between devices  19.7 us (41%)
  Pallas kernels  14.4 us (30%)
  waiting for transfers between devices  11.5 us (24%)
  between operations  1.51 us (3%)
  local copies, waits for them, and re-layouts  0.74 us (2%)
    ppermute x14, starting transfers between devices, swap_row(): return lax.ppermute(x, 'row', [(i, i ^ k) for i in range(n_row)])  19.7 us
    ppermute x14, waiting for transfers between devices, swap_row(): return lax.ppermute(x, 'row', [(i, i ^ k) for i in range(n_row)])  9.58 us
    pallas_call x3, Pallas kernels, body(): pl.pallas_call(functools.partial(user_kernel, stage, stages, pad, size, l...  6.36 us
    pallas_call x2, Pallas kernels, body(): pl.pallas_call(functools.partial(item_kernel, tuple(parts), stages, pad,...  6.32 us
    ppermute x2, waiting for transfers between devices, swap_col(): return lax.ppermute(x, 'col', [(i, i ^ 1) for i in range(n_col)])  1.9 us
  transfers between devices with their start and end apart: 16, of which 4 were waited for; matrix products, arithmetic and copies ran while one was open for 2% of the time, Pallas kernels for 21%

profile of v6, /device:TPU:8, one launch (start us, length us, event | category | flops | bytes accessed | tf_op | source)
XLA Modules:
  0.0 47.9 jit_solution(16182521780020340256)
XLA Ops:
  0.6 0.0 copy-start.2
  0.6 0.0 copy-start.3
  0.7 0.0 copy-start.4
  0.7 0.0 copy-start.5
  0.7 0.0 copy-start
  0.7 0.0 copy-start.1
  0.7 2.7 %collective-permute-start = (bf16[512,128]{1,0:T(8,128)(2,1)}, bf16[512,128]{1,0:T(8,128)(2,1)S(1)}, u32[]{:S(2)}, u32[]{:S(2)}) collective-permute-start(bf16[512,128]{1,0:T(8,128)(2,1)} %items.1), channel_id=1, source_target_pairs={{0,8},{2,10},{4,12},{6,14},{8,0},{10,2},{12,4},{14,6},{1,9},{3,11}... | collective-permute-start | bytes 393224 | tf_op jit(solution)/shard_map/ppermute | solution.py:229
  3.3 1.5 %collective-permute-start.3 = (bf16[512,128]{1,0:T(8,128)(2,1)}, bf16[512,128]{1,0:T(8,128)(2,1)S(1)}, u32[]{:S(2)}, u32[]{:S(2)}) collective-permute-start(bf16[512,128]{1,0:T(8,128)(2,1)} %items.1), channel_id=1, source_target_pairs={{0,2},{2,0},{4,6},{6,4},{8,10},{10,8},{12,14},{14,12},{1,3},{3,1},... | collective-permute-start | bytes 393224 | tf_op jit(solution)/shard_map/ppermute | solution.py:229
  4.9 0.4 collective-permute-start.4
  5.3 1.5 %collective-permute-start.5 = (bf16[512,128]{1,0:T(8,128)(2,1)}, bf16[512,128]{1,0:T(8,128)(2,1)S(1)}, u32[]{:S(2)}, u32[]{:S(2)}) collective-permute-start(bf16[512,128]{1,0:T(8,128)(2,1)} %items.1), channel_id=1, source_target_pairs={{0,6},{2,4},{4,2},{6,0},{8,14},{10,12},{12,10},{14,8},{1,7},{3,5},... | collective-permute-start | bytes 393224 | tf_op jit(solution)/shard_map/ppermute | solution.py:229
  6.8 0.0 collective-permute-start.6
  6.8 2.3 %collective-permute-done.refs_7_ = bf16[512,128]{1,0:T(8,128)(2,1)S(1)} collective-permute-done((bf16[512,128]{1,0:T(8,128)(2,1)}, bf16[512,128]{1,0:T(8,128)(2,1)S(1)}, u32[]{:S(2)}, u32[]{:S(2)}) %collective-permute-start) | collective-permute-done | bytes 131104 | tf_op jit(solution)/shard_map/ppermute | solution.py:229
  9.2 1.5 %collective-permute-start.1 = (bf16[512,128]{1,0:T(8,128)(2,1)S(1)}, bf16[512,128]{1,0:T(8,128)(2,1)S(1)}, u32[]{:S(2)}, u32[]{:S(2)}) collective-permute-start(bf16[512,128]{1,0:T(8,128)(2,1)S(1)} %collective-permute-done.refs_7_), channel_id=1, source_target_pairs={{0,2},{2,0},{4,6},{6,4},{8,10},{10,8},{12,14},{14,12},{1,3},{3,1},... | collective-permute-start | bytes 393224 | tf_op jit(solution)/shard_map/ppermute | solution.py:229
  10.7 0.0 collective-permute-done.3.refs_4_
  10.7 1.3 %collective-permute-start.2 = (bf16[512,128]{1,0:T(8,128)(2,1)S(1)}, bf16[512,128]{1,0:T(8,128)(2,1)S(1)}, u32[]{:S(2)}, u32[]{:S(2)}) collective-permute-start(bf16[512,128]{1,0:T(8,128)(2,1)S(1)} %collective-permute-done.refs_7_), channel_id=1, source_target_pairs={{0,4},{2,6},{4,0},{6,2},{8,12},{10,14},{12,8},{14,10},{1,5},{3,7},... | collective-permute-start | bytes 393224 | tf_op jit(solution)/shard_map/ppermute | solution.py:229
  12.0 0.0 collective-permute-done.4.refs_5_
  12.0 1.0 %collective-permute-start.7 = (bf16[512,128]{1,0:T(8,128)(2,1)S(1)}, bf16[512,128]{1,0:T(8,128)(2,1)S(1)}, u32[]{:S(2)}, u32[]{:S(2)}) collective-permute-start(bf16[512,128]{1,0:T(8,128)(2,1)S(1)} %collective-permute-done.refs_7_), channel_id=1, source_target_pairs={{0,6},{2,4},{4,2},{6,0},{8,14},{10,12},{12,10},{14,8},{1,7},{3,5},... | collective-permute-start | bytes 393224 | tf_op jit(solution)/shard_map/ppermute | solution.py:229
  13.0 0.1 clear.1.total.refs_10_
  13.8 0.8 %plan.1.refs_0_ = s32[1,768]{1,0:T(1,128)S(4)} custom-call(s32[1,1]{1,0:T(1,128)S(6)} %copy.15.live, s32[1,192]{1,0:T(1,128)S(1)} %bitcast.14, s32[1,192]{1,0:T(1,128)S(1)} %bitcast.15, f32[2048,128]{1,0:T(8,128)S(1)} %clear.1.total.refs_10_), custom_call_target="tpu_custom_call" | custom-call | tf_op jit(solution)/shard_map/plan/pallas_call | solution.py:256
  14.6 0.0 collective-permute-done.5.refs_6_
  14.6 0.0 collective-permute-done.6.refs_9_
  14.7 3.8 %user_terms.3 = (bf16[2560,128]{1,0:T(8,128)(2,1)S(1)}, f32[2048,128]{1,0:T(8,128)S(1)}, bf16[2048,128]{1,0:T(8,128)(2,1)S(1)}) custom-call(s32[1,768]{1,0:T(1,128)S(4)} %plan.1.refs_0_, bf16[192,128,128]{2,1,0:T(8,128)(2,1)S(1)} %bitcast.4, s32[192,16,128]{2,1,0:T(8,128)S(1)} %bitcast.9, ...), custom_call_target="tpu_custom_call", output_to_operand_aliasing={{1}: (10, {})} | custom-call | flops 3145728 | tf_op jit(solution)/shard_map/user_terms/pallas_call | solution.py:283
  18.5 0.0 collective-permute-done.1.refs_3_
  18.5 0.0 collective-permute-done.2.refs_4_
  18.5 1.7 %user_terms.4 = (bf16[1024,128]{1,0:T(8,128)(2,1)S(1)}, f32[2048,128]{1,0:T(8,128)S(1)}) custom-call(s32[1,768]{1,0:T(1,128)S(4)} %plan.1.refs_0_, bf16[192,128,128]{2,1,0:T(8,128)(2,1)S(1)} %bitcast.5, s32[192,16,128]{2,1,0:T(8,128)S(1)} %bitcast.10, bf16[512,128]{1,0:T(8,128)(2,1)S(1)} %collective-permute-done.1.refs_3_, ...), custom_call_target="tpu_custom_call", output_to_operand_aliasing={{1}: (6, {})} | custom-call | flops 3145728 | tf_op jit(solution)/shard_map/user_terms/pallas_call | solution.py:283
  20.2 0.0 collective-permute-done.7.refs_3_
  20.2 0.9 %user_terms.5 = (bf16[512,128]{1,0:T(8,128)(2,1)S(1)}, f32[2048,128]{1,0:T(8,128)S(1)}, bf16[2048,128]{1,0:T(8,128)(2,1)S(1)}) custom-call(s32[1,768]{1,0:T(1,128)S(4)} %plan.1.refs_0_, bf16[192,128,128]{2,1,0:T(8,128)(2,1)S(1)} %bitcast.6, s32[192,16,128]{2,1,0:T(8,128)S(1)} %bitcast.11, ...), custom_call_target="tpu_custom_call", output_to_operand_aliasing={{1}: (5, {})} | custom-call | flops 3145728 | tf_op jit(solution)/shard_map/user_terms/pallas_call | solution.py:283
  21.1 0.1 collective-permute-start.8
  21.2 1.9 %collective-permute-done.8.refs_6_ = bf16[2048,128]{1,0:T(8,128)(2,1)S(1)} collective-permute-done((bf16[2048,128]{1,0:T(8,128)(2,1)S(1)}, bf16[2048,128]{1,0:T(8,128)(2,1)S(1)}, u32[]{:S(2)}, u32[]{:S(2)}) %collective-permute-start.8) | collective-permute-done | bytes 524320 | tf_op jit(solution)/shard_map/ppermute | solution.py:232
  23.1 2.7 %item_terms.2 = (bf16[512,128]{1,0:T(8,128)(2,1)S(1)}, bf16[512,128]{1,0:T(8,128)(2,1)S(1)}, bf16[512,128]{1,0:T(8,128)(2,1)S(1)}, bf16[2048,128]{1,0:T(8,128)(2,1)S(1)}, bf16[2048,128]{1,0:T(8,128)(2,1)S(1)}) custom-call(s32[1,768]{1,0:T(1,128)S(4)} %plan.1.refs_0_, bf16[192,128,128]{2,1,0:T(8,128)(2,1)S(1)} %bitcast.7, s32[192,16,128]{2,1,0:T(8,128)S(1)} %bitcast.12, ...), custom_call_target="tpu_custom_call" | custom-call | flops 3145728 | tf_op jit(solution)/shard_map/item_terms/pallas_call | solution.py:317
  25.8 0.7 %collective-permute-start.14 = (bf16[512,128]{1,0:T(8,128)(2,1)S(1)}, bf16[512,128]{1,0:T(8,128)(2,1)S(1)}, u32[]{:S(2)}, u32[]{:S(2)}) collective-permute-start(bf16[512,128]{1,0:T(8,128)(2,1)S(1)} %get-tuple-element.35), channel_id=1, source_target_pairs={{0,6},{2,4},{4,2},{6,0},{8,14},{10,12},{12,10},{14,8},{1,7},{3,5},... | collective-permute-start | bytes 393224 | tf_op jit(solution)/shard_map/ppermute | solution.py:229
  26.5 0.0 collective-permute-start.13
  26.5 2.9 %collective-permute-start.12 = (bf16[512,128]{1,0:T(8,128)(2,1)S(1)}, bf16[512,128]{1,0:T(8,128)(2,1)S(1)}, u32[]{:S(2)}, u32[]{:S(2)}) collective-permute-start(bf16[512,128]{1,0:T(8,128)(2,1)S(1)} %get-tuple-element.33), channel_id=1, source_target_pairs={{0,2},{2,0},{4,6},{6,4},{8,10},{10,8},{12,14},{14,12},{1,3},{3,1},... | collective-permute-start | bytes 393224 | tf_op jit(solution)/shard_map/ppermute | solution.py:229
  29.3 3.6 %item_terms.3 = (f32[512,128]{1,0:T(8,128)S(1)}, bf16[512,128]{1,0:T(8,128)(2,1)S(1)}, bf16[512,128]{1,0:T(8,128)(2,1)S(1)}, bf16[512,128]{1,0:T(8,128)(2,1)S(1)}, f32[512,128]{1,0:T(8,128)S(1)}) custom-call(s32[1,768]{1,0:T(1,128)S(4)} %plan.1.refs_0_, bf16[192,128,128]{2,1,0:T(8,128)(2,1)S(1)} %bitcast.8, s32[192,16,128]{2,1,0:T(8,128)S(1)} %bitcast.13, ...), custom_call_target="tpu_custom_call" | custom-call | flops 3145728 | tf_op jit(solution)/shard_map/item_terms/pallas_call | solution.py:317
  33.0 0.1 collective-permute-start.9
  33.0 0.1 collective-permute-start.10
  33.1 0.0 collective-permute-done.14
  33.1 3.4 %collective-permute-start.11 = (bf16[512,128]{1,0:T(8,128)(2,1)S(1)}, bf16[512,128]{1,0:T(8,128)(2,1)S(1)}, u32[]{:S(2)}, u32[]{:S(2)}) collective-permute-start(bf16[512,128]{1,0:T(8,128)(2,1)S(1)} %get-tuple-element.31), channel_id=1, source_target_pairs={{0,6},{2,4},{4,2},{6,0},{8,14},{10,12},{12,10},{14,8},{1,7},{3,5},... | collective-permute-start | bytes 393224 | tf_op jit(solution)/shard_map/ppermute | solution.py:229
  36.5 0.0 collective-permute-done.13
  36.5 0.0 collective-permute-done.12
  36.5 0.1 add_convert_fusion
  36.6 2.6 %collective-permute-start.15 = (bf16[512,128]{1,0:T(8,128)(2,1)S(1)}, bf16[512,128]{1,0:T(8,128)(2,1)S(1)}, u32[]{:S(2)}, u32[]{:S(2)}) collective-permute-start(bf16[512,128]{1,0:T(8,128)(2,1)S(1)} %add_convert_fusion), channel_id=1, source_target_pairs={{0,8},{2,10},{4,12},{6,14},{8,0},{10,2},{12,4},{14,6},{1,9},{3,11}... | collective-permute-start | bytes 393224 | tf_op jit(solution)/shard_map/ppermute | solution.py:229
  39.2 0.7 %constant_dynamic-slice_fusion = bf16[1024,128]{1,0:T(8,128)(2,1)} fusion(bf16[2048,128]{1,0:T(8,128)(2,1)S(1)} %get-tuple-element.25.refs_4_, s32[]{:T(128)S(6)} %select_n.3), kind=kLoop, calls=%fused_computation.1 | loop fusion | bytes 524292 | tf_op jit(solution)/shard_map/dynamic_slice | solution.py:331
  39.9 0.0 collective-permute-done.9.refs_1_
  39.9 0.0 collective-permute-done.10.refs_2_
  39.9 1.9 %collective-permute-done.11.refs_3_ = bf16[512,128]{1,0:T(8,128)(2,1)S(1)} collective-permute-done((bf16[512,128]{1,0:T(8,128)(2,1)S(1)}, bf16[512,128]{1,0:T(8,128)(2,1)S(1)}, u32[]{:S(2)}, u32[]{:S(2)}) %collective-permute-start.11) | collective-permute-done | bytes 131104 | tf_op jit(solution)/shard_map/ppermute | solution.py:229
  41.8 5.3 %collective-permute-done.15.refs_4_ = bf16[512,128]{1,0:T(8,128)(2,1)S(1)} collective-permute-done((bf16[512,128]{1,0:T(8,128)(2,1)S(1)}, bf16[512,128]{1,0:T(8,128)(2,1)S(1)}, u32[]{:S(2)}, u32[]{:S(2)}) %collective-permute-start.15) | collective-permute-done | bytes 131104 | tf_op jit(solution)/shard_map/ppermute | solution.py:229
  47.1 0.8 %finish.1 = bf16[512,128]{1,0:T(8,128)(2,1)} custom-call(bf16[512,128]{1,0:T(8,128)(2,1)S(1)} %copy-done.2, f32[512,128]{1,0:T(8,128)S(1)} %get-tuple-element.28.refs_0_, bf16[512,128]{1,0:T(8,128)(2,1)S(1)} %collective-permute-done.9.refs_1_, bf16[512,128]{1,0:T(8,128)(2,1)S(1)} %collective-permute-done.10.refs_2_, ...), custom_call_target="tpu_custom_call" | custom-call | tf_op jit(solution)/shard_map/finish/pallas_call | solution.py:338
  (6 shorter events, 0.0 us)
Async XLA Ops:
  0.6 14.0 %copy-start.2 = (bf16[512,128]{1,0:T(8,128)(2,1)S(1)}, bf16[512,128]{1,0:T(8,128)(2,1)}, u32[]{:S(2)}) copy-start(bf16[512,128]{1,0:T(8,128)(2,1)} %items.1) | copy-start | bytes 393220
  0.6 14.0 %copy-start.3 = (bf16[1024,128]{1,0:T(8,128)(2,1)S(1)}, bf16[1024,128]{1,0:T(8,128)(2,1)}, u32[]{:S(2)}) copy-start(bf16[1024,128]{1,0:T(8,128)(2,1)} %refs_8_.1) | copy-start | bytes 786436
  0.7 13.1 %copy-start.4 = (s32[1,1,192]{2,1,0:T(1,128)S(1)}, s32[1,1,192]{2,1,0:T(1,128)}, u32[]{:S(2)}) copy-start(s32[1,1,192]{2,1,0:T(1,128)} %param.11) | copy-start | bytes 2308
  0.7 13.1 %copy-start.5 = (s32[1,1,192]{2,1,0:T(1,128)S(1)}, s32[1,1,192]{2,1,0:T(1,128)}, u32[]{:S(2)}) copy-start(s32[1,1,192]{2,1,0:T(1,128)} %param.12) | copy-start | bytes 2308
  0.7 14.0 %copy-start = (bf16[1,1,192,128,128]{4,3,2,1,0:T(8,128)(2,1)S(1)}, bf16[1,1,192,128,128]{4,3,2,1,0:T(8,128)(2,1)}, u32[]{:S(2)}) copy-start(bf16[1,1,192,128,128]{4,3,2,1,0:T(8,128)(2,1)} %param.9) | copy-start | bytes 18874372
  0.7 14.0 %copy-start.1 = (s32[1,1,192,16,128]{4,3,2,1,0:T(8,128)S(1)}, s32[1,1,192,16,128]{4,3,2,1,0:T(8,128)}, u32[]{:S(2)}) copy-start(s32[1,1,192,16,128]{4,3,2,1,0:T(8,128)} %param.10) | copy-start | bytes 4718596
  0.7 8.5 %collective-permute-start = (bf16[512,128]{1,0:T(8,128)(2,1)}, bf16[512,128]{1,0:T(8,128)(2,1)S(1)}, u32[]{:S(2)}, u32[]{:S(2)}) collective-permute-start(bf16[512,128]{1,0:T(8,128)(2,1)} %items.1), channel_id=1, source_target_pairs={{0,8},{2,10},{4,12},{6,14},{8,0},{10,2},{12,4},{14,6},{1,9},{3,11}... | collective-permute-start | bytes 393224 | tf_op jit(solution)/shard_map/ppermute | solution.py:229
  3.3 7.3 %collective-permute-start.3 = (bf16[512,128]{1,0:T(8,128)(2,1)}, bf16[512,128]{1,0:T(8,128)(2,1)S(1)}, u32[]{:S(2)}, u32[]{:S(2)}) collective-permute-start(bf16[512,128]{1,0:T(8,128)(2,1)} %items.1), channel_id=1, source_target_pairs={{0,2},{2,0},{4,6},{6,4},{8,10},{10,8},{12,14},{14,12},{1,3},{3,1},... | collective-permute-start | bytes 393224 | tf_op jit(solution)/shard_map/ppermute | solution.py:229
  4.9 7.1 %collective-permute-start.4 = (bf16[512,128]{1,0:T(8,128)(2,1)}, bf16[512,128]{1,0:T(8,128)(2,1)S(1)}, u32[]{:S(2)}, u32[]{:S(2)}) collective-permute-start(bf16[512,128]{1,0:T(8,128)(2,1)} %items.1), channel_id=1, source_target_pairs={{0,4},{2,6},{4,0},{6,2},{8,12},{10,14},{12,8},{14,10},{1,5},{3,7},... | collective-permute-start | bytes 393224 | tf_op jit(solution)/shard_map/ppermute | solution.py:229
  5.3 9.3 %collective-permute-start.5 = (bf16[512,128]{1,0:T(8,128)(2,1)}, bf16[512,128]{1,0:T(8,128)(2,1)S(1)}, u32[]{:S(2)}, u32[]{:S(2)}) collective-permute-start(bf16[512,128]{1,0:T(8,128)(2,1)} %items.1), channel_id=1, source_target_pairs={{0,6},{2,4},{4,2},{6,0},{8,14},{10,12},{12,10},{14,8},{1,7},{3,5},... | collective-permute-start | bytes 393224 | tf_op jit(solution)/shard_map/ppermute | solution.py:229
  6.8 7.8 %collective-permute-start.6 = (bf16[1024,128]{1,0:T(8,128)(2,1)}, bf16[1024,128]{1,0:T(8,128)(2,1)S(1)}, u32[]{:S(2)}, u32[]{:S(2)}) collective-permute-start(bf16[1024,128]{1,0:T(8,128)(2,1)} %refs_8_.1), channel_id=1, source_target_pairs={{0,1},{1,0},{2,3},{3,2},{4,5},{5,4},{6,7},{7,6},{8,9},{9,8},{10,11... | collective-permute-start | bytes 786440 | tf_op jit(solution)/shard_map/ppermute | solution.py:232
  9.2 9.3 %collective-permute-start.1 = (bf16[512,128]{1,0:T(8,128)(2,1)S(1)}, bf16[512,128]{1,0:T(8,128)(2,1)S(1)}, u32[]{:S(2)}, u32[]{:S(2)}) collective-permute-start(bf16[512,128]{1,0:T(8,128)(2,1)S(1)} %collective-permute-done.refs_7_), channel_id=1, source_target_pairs={{0,2},{2,0},{4,6},{6,4},{8,10},{10,8},{12,14},{14,12},{1,3},{3,1},... | collective-permute-start | bytes 393224 | tf_op jit(solution)/shard_map/ppermute | solution.py:229
  10.7 7.8 %collective-permute-start.2 = (bf16[512,128]{1,0:T(8,128)(2,1)S(1)}, bf16[512,128]{1,0:T(8,128)(2,1)S(1)}, u32[]{:S(2)}, u32[]{:S(2)}) collective-permute-start(bf16[512,128]{1,0:T(8,128)(2,1)S(1)} %collective-permute-done.refs_7_), channel_id=1, source_target_pairs={{0,4},{2,6},{4,0},{6,2},{8,12},{10,14},{12,8},{14,10},{1,5},{3,7},... | collective-permute-start | bytes 393224 | tf_op jit(solution)/shard_map/ppermute | solution.py:229
  12.0 8.2 %collective-permute-start.7 = (bf16[512,128]{1,0:T(8,128)(2,1)S(1)}, bf16[512,128]{1,0:T(8,128)(2,1)S(1)}, u32[]{:S(2)}, u32[]{:S(2)}) collective-permute-start(bf16[512,128]{1,0:T(8,128)(2,1)S(1)} %collective-permute-done.refs_7_), channel_id=1, source_target_pairs={{0,6},{2,4},{4,2},{6,0},{8,14},{10,12},{12,10},{14,8},{1,7},{3,5},... | collective-permute-start | bytes 393224 | tf_op jit(solution)/shard_map/ppermute | solution.py:229
  21.1 2.0 %collective-permute-start.8 = (bf16[2048,128]{1,0:T(8,128)(2,1)S(1)}, bf16[2048,128]{1,0:T(8,128)(2,1)S(1)}, u32[]{:S(2)}, u32[]{:S(2)}) collective-permute-start(bf16[2048,128]{1,0:T(8,128)(2,1)S(1)} %get-tuple-element.24.refs_5_), channel_id=1, source_target_pairs={{0,1},{1,0},{2,3},{3,2},{4,5},{5,4},{6,7},{7,6},{8,9},{9,8},{10,11... | collective-permute-start | bytes 1572872 | tf_op jit(solution)/shard_map/ppermute | solution.py:232
  25.8 7.4 %collective-permute-start.14 = (bf16[512,128]{1,0:T(8,128)(2,1)S(1)}, bf16[512,128]{1,0:T(8,128)(2,1)S(1)}, u32[]{:S(2)}, u32[]{:S(2)}) collective-permute-start(bf16[512,128]{1,0:T(8,128)(2,1)S(1)} %get-tuple-element.35), channel_id=1, source_target_pairs={{0,6},{2,4},{4,2},{6,0},{8,14},{10,12},{12,10},{14,8},{1,7},{3,5},... | collective-permute-start | bytes 393224 | tf_op jit(solution)/shard_map/ppermute | solution.py:229
  26.5 10.0 %collective-permute-start.13 = (bf16[512,128]{1,0:T(8,128)(2,1)S(1)}, bf16[512,128]{1,0:T(8,128)(2,1)S(1)}, u32[]{:S(2)}, u32[]{:S(2)}) collective-permute-start(bf16[512,128]{1,0:T(8,128)(2,1)S(1)} %get-tuple-element.34), channel_id=1, source_target_pairs={{0,4},{2,6},{4,0},{6,2},{8,12},{10,14},{12,8},{14,10},{1,5},{3,7},... | collective-permute-start | bytes 393224 | tf_op jit(solution)/shard_map/ppermute | solution.py:229
  26.5 10.0 %collective-permute-start.12 = (bf16[512,128]{1,0:T(8,128)(2,1)S(1)}, bf16[512,128]{1,0:T(8,128)(2,1)S(1)}, u32[]{:S(2)}, u32[]{:S(2)}) collective-permute-start(bf16[512,128]{1,0:T(8,128)(2,1)S(1)} %get-tuple-element.33), channel_id=1, source_target_pairs={{0,2},{2,0},{4,6},{6,4},{8,10},{10,8},{12,14},{14,12},{1,3},{3,1},... | collective-permute-start | bytes 393224 | tf_op jit(solution)/shard_map/ppermute | solution.py:229
  33.0 6.9 %collective-permute-start.9 = (bf16[512,128]{1,0:T(8,128)(2,1)S(1)}, bf16[512,128]{1,0:T(8,128)(2,1)S(1)}, u32[]{:S(2)}, u32[]{:S(2)}) collective-permute-start(bf16[512,128]{1,0:T(8,128)(2,1)S(1)} %get-tuple-element.29), channel_id=1, source_target_pairs={{0,2},{2,0},{4,6},{6,4},{8,10},{10,8},{12,14},{14,12},{1,3},{3,1},... | collective-permute-start | bytes 393224 | tf_op jit(solution)/shard_map/ppermute | solution.py:229
  33.0 6.9 %collective-permute-start.10 = (bf16[512,128]{1,0:T(8,128)(2,1)S(1)}, bf16[512,128]{1,0:T(8,128)(2,1)S(1)}, u32[]{:S(2)}, u32[]{:S(2)}) collective-permute-start(bf16[512,128]{1,0:T(8,128)(2,1)S(1)} %get-tuple-element.30), channel_id=1, source_target_pairs={{0,4},{2,6},{4,0},{6,2},{8,12},{10,14},{12,8},{14,10},{1,5},{3,7},... | collective-permute-start | bytes 393224 | tf_op jit(solution)/shard_map/ppermute | solution.py:229
  33.1 8.7 %collective-permute-start.11 = (bf16[512,128]{1,0:T(8,128)(2,1)S(1)}, bf16[512,128]{1,0:T(8,128)(2,1)S(1)}, u32[]{:S(2)}, u32[]{:S(2)}) collective-permute-start(bf16[512,128]{1,0:T(8,128)(2,1)S(1)} %get-tuple-element.31), channel_id=1, source_target_pairs={{0,6},{2,4},{4,2},{6,0},{8,14},{10,12},{12,10},{14,8},{1,7},{3,5},... | collective-permute-start | bytes 393224 | tf_op jit(solution)/shard_map/ppermute | solution.py:229
  36.6 10.5 %collective-permute-start.15 = (bf16[512,128]{1,0:T(8,128)(2,1)S(1)}, bf16[512,128]{1,0:T(8,128)(2,1)S(1)}, u32[]{:S(2)}, u32[]{:S(2)}) collective-permute-start(bf16[512,128]{1,0:T(8,128)(2,1)S(1)} %add_convert_fusion), channel_id=1, source_target_pairs={{0,8},{2,10},{4,12},{6,14},{8,0},{10,2},{12,4},{14,6},{1,9},{3,11}... | collective-permute-start | bytes 393224 | tf_op jit(solution)/shard_map/ppermute | solution.py:229

commit v7 on v5

--- a/solution.py
+++ b/solution.py
@@ -9,7 +9,7 @@
 
 BLOCK = 128
 UNROLL = 24
-TAIL = 8
+TAILS = (8, 16)
 FIELD = 10
 PLAN_UNROLL = 8
 VMEM_LIMIT = 16 * 1024 * 1024
@@ -93,12 +93,14 @@
         group(i * UNROLL, UNROLL)
         return _
 
-    whole = (live + UNROLL - TAIL - 1) // UNROLL
+    whole = (live + UNROLL - TAILS[-1] - 1) // UNROLL
     lax.fori_loop(0, whole, step, 0)
-
-    @pl.when(whole * UNROLL < live)
-    def _():
-        group(whole * UNROLL, TAIL)
+    rest = live - whole * UNROLL
+    for less, size in zip((0,) + TAILS, TAILS):
+
+        @pl.when((rest > less) & (rest <= size))
+        def _(size=size):
+            group(whole * UNROLL, size)
 
 
 def masked_residual(predicted, tiles, words, slot, live):

time: 48 us -> 48.2 us (level)
  Pallas kernels: 18.8 us -> 7.64 us
  starting transfers between devices: 18.4 us -> 25.3 us
  waiting for transfers between devices: 8.69 us -> 12.8 us
    ppermute x14, starting transfers between devices: 18.3 us -> 25.2 us  [swap_row(): return lax.ppermute(x, 'row', [(i, i ^ k) for i in range(n_row)])]
    pallas_call x3, Pallas kernels: 7.49 us -> 2.79 us  [body(): pl.pallas_call(functools.partial(user_kernel, stage, stages, size, last),...]
    pallas_call x2, Pallas kernels: 7.38 us -> 2.76 us  [body(): pl.pallas_call(functools.partial(item_kernel, tuple(parts), stages, first...]
    ppermute x14, waiting for transfers between devices: 6.79 us -> 10.9 us  [swap_row(): return lax.ppermute(x, 'row', [(i, i ^ k) for i in range(n_row)])]
    pallas_call x1, Pallas kernels: 3.02 us -> 1.21 us  [body(): pl.pallas_call(functools.partial(plan_kernel, shard_tiles, keys, edges),...]
  transfers between devices with their start and end apart: 16 -> 16, of which waited for: 6 -> 8; matrix products, arithmetic and copies ran while one was open for 2% -> 2% of each run, Pallas kernels for 27% -> 10%
where the time goes in v7:
time: 48.2 us; the launch traced here: 48 us
  starting transfers between devices  25.3 us (52%)
  waiting for transfers between devices  12.8 us (27%)
  Pallas kernels  7.64 us (16%)
  between operations  1.46 us (3%)
  local copies, waits for them, and re-layouts  0.74 us (2%)
    ppermute x14, starting transfers between devices, swap_row(): return lax.ppermute(x, 'row', [(i, i ^ k) for i in range(n_row)])  25.2 us
    ppermute x14, waiting for transfers between devices, swap_row(): return lax.ppermute(x, 'row', [(i, i ^ k) for i in range(n_row)])  10.9 us
    pallas_call x3, Pallas kernels, body(): pl.pallas_call(functools.partial(user_kernel, stage, stages, size, last),...  2.79 us
    pallas_call x2, Pallas kernels, body(): pl.pallas_call(functools.partial(item_kernel, tuple(parts), stages, first...  2.76 us
    ppermute x2, waiting for transfers between devices, swap_col(): return lax.ppermute(x, 'col', [(i, i ^ 1) for i in range(n_col)])  1.9 us
    pallas_call x1, Pallas kernels, body(): pl.pallas_call(functools.partial(plan_kernel, shard_tiles, keys, edges),...  1.21 us
  transfers between devices with their start and end apart: 16, of which 8 were waited for; matrix products, arithmetic and copies ran while one was open for 2% of the time, Pallas kernels for 10%

profile of v7, /device:TPU:0, one launch (start us, length us, event | category | flops | bytes accessed | tf_op | source)
XLA Modules:
  0.0 48.0 jit_solution(6872608393344674754)
XLA Ops:
  0.6 0.0 copy-start.2
  0.6 0.0 copy-start.3
  0.7 0.0 copy-start.4
  0.7 0.0 copy-start.5
  0.7 0.0 copy-start
  0.7 0.0 copy-start.1
  0.7 4.1 %collective-permute-start = (bf16[512,128]{1,0:T(8,128)(2,1)}, bf16[512,128]{1,0:T(8,128)(2,1)S(1)}, u32[]{:S(2)}, u32[]{:S(2)}) collective-permute-start(bf16[512,128]{1,0:T(8,128)(2,1)} %items.1), channel_id=1, source_target_pairs={{0,8},{2,10},{4,12},{6,14},{8,0},{10,2},{12,4},{14,6},{1,9},{3,11}... | collective-permute-start | bytes 393224 | tf_op jit(solution)/shard_map/ppermute | solution.py:227
  4.8 1.5 %collective-permute-start.3 = (bf16[512,128]{1,0:T(8,128)(2,1)}, bf16[512,128]{1,0:T(8,128)(2,1)S(1)}, u32[]{:S(2)}, u32[]{:S(2)}) collective-permute-start(bf16[512,128]{1,0:T(8,128)(2,1)} %items.1), channel_id=1, source_target_pairs={{0,2},{2,0},{4,6},{6,4},{8,10},{10,8},{12,14},{14,12},{1,3},{3,1},... | collective-permute-start | bytes 393224 | tf_op jit(solution)/shard_map/ppermute | solution.py:227
  6.3 1.6 %collective-permute-start.4 = (bf16[512,128]{1,0:T(8,128)(2,1)}, bf16[512,128]{1,0:T(8,128)(2,1)S(1)}, u32[]{:S(2)}, u32[]{:S(2)}) collective-permute-start(bf16[512,128]{1,0:T(8,128)(2,1)} %items.1), channel_id=1, source_target_pairs={{0,4},{2,6},{4,0},{6,2},{8,12},{10,14},{12,8},{14,10},{1,5},{3,7},... | collective-permute-start | bytes 393224 | tf_op jit(solution)/shard_map/ppermute | solution.py:227
  7.9 0.4 collective-permute-start.5
  8.3 0.0 collective-permute-start.6
  8.3 0.1 clear.1.total.refs_10_
  9.0 1.2 %plan.1.refs_0_ = s32[651]{0:T(1024)S(4)} custom-call(s32[1,1]{1,0:T(1,128)S(6)} %copy.15.live, s32[192]{0:T(256)S(1)} %bitcast.14, s32[192]{0:T(256)S(1)} %bitcast.15, f32[2048,128]{1,0:T(8,128)S(1)} %clear.1.total.refs_10_), custom_call_target="tpu_custom_call" | custom-call | tf_op jit(solution)/shard_map/plan/pallas_call | solution.py:253
  10.2 1.2 %collective-permute-done.refs_7_ = bf16[512,128]{1,0:T(8,128)(2,1)S(1)} collective-permute-done((bf16[512,128]{1,0:T(8,128)(2,1)}, bf16[512,128]{1,0:T(8,128)(2,1)S(1)}, u32[]{:S(2)}, u32[]{:S(2)}) %collective-permute-start) | collective-permute-done | bytes 131104 | tf_op jit(solution)/shard_map/ppermute | solution.py:227
  11.4 2.1 %collective-permute-start.1 = (bf16[512,128]{1,0:T(8,128)(2,1)S(1)}, bf16[512,128]{1,0:T(8,128)(2,1)S(1)}, u32[]{:S(2)}, u32[]{:S(2)}) collective-permute-start(bf16[512,128]{1,0:T(8,128)(2,1)S(1)} %collective-permute-done.refs_7_), channel_id=1, source_target_pairs={{0,2},{2,0},{4,6},{6,4},{8,10},{10,8},{12,14},{14,12},{1,3},{3,1},... | collective-permute-start | bytes 393224 | tf_op jit(solution)/shard_map/ppermute | solution.py:227
  13.6 0.0 collective-permute-done.3.refs_4_
  13.6 1.7 %collective-permute-start.2 = (bf16[512,128]{1,0:T(8,128)(2,1)S(1)}, bf16[512,128]{1,0:T(8,128)(2,1)S(1)}, u32[]{:S(2)}, u32[]{:S(2)}) collective-permute-start(bf16[512,128]{1,0:T(8,128)(2,1)S(1)} %collective-permute-done.refs_7_), channel_id=1, source_target_pairs={{0,4},{2,6},{4,0},{6,2},{8,12},{10,14},{12,8},{14,10},{1,5},{3,7},... | collective-permute-start | bytes 393224 | tf_op jit(solution)/shard_map/ppermute | solution.py:227
  15.2 0.0 collective-permute-done.4.refs_5_
  15.2 0.0 collective-permute-start.7
  15.2 0.5 %collective-permute-done.5.refs_6_ = bf16[512,128]{1,0:T(8,128)(2,1)S(1)} collective-permute-done((bf16[512,128]{1,0:T(8,128)(2,1)}, bf16[512,128]{1,0:T(8,128)(2,1)S(1)}, u32[]{:S(2)}, u32[]{:S(2)}) %collective-permute-start.5) | collective-permute-done | bytes 131104 | tf_op jit(solution)/shard_map/ppermute | solution.py:227
  15.8 0.0 collective-permute-done.6.refs_9_
  15.8 1.5 %user_terms.3 = (bf16[2560,128]{1,0:T(8,128)(2,1)S(1)}, f32[2048,128]{1,0:T(8,128)S(1)}, bf16[2048,128]{1,0:T(8,128)(2,1)S(1)}) custom-call(s32[651]{0:T(1024)S(4)} %plan.1.refs_0_, bf16[192,128,128]{2,1,0:T(8,128)(2,1)S(1)} %bitcast.4, s32[192,16,128]{2,1,0:T(8,128)S(1)} %bitcast.9, ...), custom_call_target="tpu_custom_call", output_to_operand_aliasing={{1}: (10, {})} | custom-call | flops 2684354560 | bytes 4194304 | tf_op jit(solution)/shard_map/user_terms/pallas_call | solution.py:279
  17.4 1.2 %collective-permute-done.1.refs_3_ = bf16[512,128]{1,0:T(8,128)(2,1)S(1)} collective-permute-done((bf16[512,128]{1,0:T(8,128)(2,1)S(1)}, bf16[512,128]{1,0:T(8,128)(2,1)S(1)}, u32[]{:S(2)}, u32[]{:S(2)}) %collective-permute-start.1) | collective-permute-done | bytes 131104 | tf_op jit(solution)/shard_map/ppermute | solution.py:227
  18.5 1.4 %collective-permute-done.2.refs_4_ = bf16[512,128]{1,0:T(8,128)(2,1)S(1)} collective-permute-done((bf16[512,128]{1,0:T(8,128)(2,1)S(1)}, bf16[512,128]{1,0:T(8,128)(2,1)S(1)}, u32[]{:S(2)}, u32[]{:S(2)}) %collective-permute-start.2) | collective-permute-done | bytes 131104 | tf_op jit(solution)/shard_map/ppermute | solution.py:227
  19.9 0.7 %user_terms.4 = (bf16[1024,128]{1,0:T(8,128)(2,1)S(1)}, f32[2048,128]{1,0:T(8,128)S(1)}) custom-call(s32[651]{0:T(1024)S(4)} %plan.1.refs_0_, bf16[192,128,128]{2,1,0:T(8,128)(2,1)S(1)} %bitcast.5, s32[192,16,128]{2,1,0:T(8,128)S(1)} %bitcast.10, bf16[512,128]{1,0:T(8,128)(2,1)S(1)} %collective-permute-done.1.refs_3_, ...), custom_call_target="tpu_custom_call", output_to_operand_aliasing={{1}: (6, {})} | custom-call | flops 2684354560 | bytes 4194304 | tf_op jit(solution)/shard_map/user_terms/pallas_call | solution.py:279
  20.6 1.3 %collective-permute-done.7.refs_3_ = bf16[512,128]{1,0:T(8,128)(2,1)S(1)} collective-permute-done((bf16[512,128]{1,0:T(8,128)(2,1)S(1)}, bf16[512,128]{1,0:T(8,128)(2,1)S(1)}, u32[]{:S(2)}, u32[]{:S(2)}) %collective-permute-start.7) | collective-permute-done | bytes 131104 | tf_op jit(solution)/shard_map/ppermute | solution.py:227
  21.9 0.5 %user_terms.5 = (bf16[512,128]{1,0:T(8,128)(2,1)S(1)}, f32[2048,128]{1,0:T(8,128)S(1)}, bf16[2048,128]{1,0:T(8,128)(2,1)S(1)}) custom-call(s32[651]{0:T(1024)S(4)} %plan.1.refs_0_, bf16[192,128,128]{2,1,0:T(8,128)(2,1)S(1)} %bitcast.6, s32[192,16,128]{2,1,0:T(8,128)S(1)} %bitcast.11, ...), custom_call_target="tpu_custom_call", output_to_operand_aliasing={{1}: (5, {})} | custom-call | flops 2684354560 | bytes 4194304 | tf_op jit(solution)/shard_map/user_terms/pallas_call | solution.py:279
  22.5 0.1 collective-permute-start.8
  22.5 1.9 %collective-permute-done.8.refs_6_ = bf16[2048,128]{1,0:T(8,128)(2,1)S(1)} collective-permute-done((bf16[2048,128]{1,0:T(8,128)(2,1)S(1)}, bf16[2048,128]{1,0:T(8,128)(2,1)S(1)}, u32[]{:S(2)}, u32[]{:S(2)}) %collective-permute-start.8) | collective-permute-done | bytes 524320 | tf_op jit(solution)/shard_map/ppermute | solution.py:230
  24.4 1.4 %item_terms.2 = (bf16[512,128]{1,0:T(8,128)(2,1)S(1)}, bf16[512,128]{1,0:T(8,128)(2,1)S(1)}, bf16[512,128]{1,0:T(8,128)(2,1)S(1)}, bf16[2048,128]{1,0:T(8,128)(2,1)S(1)}, bf16[2048,128]{1,0:T(8,128)(2,1)S(1)}) custom-call(s32[651]{0:T(1024)S(4)} %plan.1.refs_0_, bf16[192,128,128]{2,1,0:T(8,128)(2,1)S(1)} %bitcast.7, s32[192,16,128]{2,1,0:T(8,128)S(1)} %bitcast.12, ...), custom_call_target="tpu_custom_call" | custom-call | flops 2684354560 | bytes 4194304 | tf_op jit(solution)/shard_map/item_terms/pallas_call | solution.py:313
  25.9 4.7 %collective-permute-start.14 = (bf16[512,128]{1,0:T(8,128)(2,1)S(1)}, bf16[512,128]{1,0:T(8,128)(2,1)S(1)}, u32[]{:S(2)}, u32[]{:S(2)}) collective-permute-start(bf16[512,128]{1,0:T(8,128)(2,1)S(1)} %get-tuple-element.35), channel_id=1, source_target_pairs={{0,6},{2,4},{4,2},{6,0},{8,14},{10,12},{12,10},{14,8},{1,7},{3,5},... | collective-permute-start | bytes 393224 | tf_op jit(solution)/shard_map/ppermute | solution.py:227
  30.5 0.5 %collective-permute-start.13 = (bf16[512,128]{1,0:T(8,128)(2,1)S(1)}, bf16[512,128]{1,0:T(8,128)(2,1)S(1)}, u32[]{:S(2)}, u32[]{:S(2)}) collective-permute-start(bf16[512,128]{1,0:T(8,128)(2,1)S(1)} %get-tuple-element.34), channel_id=1, source_target_pairs={{0,4},{2,6},{4,0},{6,2},{8,12},{10,14},{12,8},{14,10},{1,5},{3,7},... | collective-permute-start | bytes 393224 | tf_op jit(solution)/shard_map/ppermute | solution.py:227
  31.1 0.1 collective-permute-start.12
  31.2 1.3 %item_terms.3 = (f32[512,128]{1,0:T(8,128)S(1)}, bf16[512,128]{1,0:T(8,128)(2,1)S(1)}, bf16[512,128]{1,0:T(8,128)(2,1)S(1)}, bf16[512,128]{1,0:T(8,128)(2,1)S(1)}, f32[512,128]{1,0:T(8,128)S(1)}) custom-call(s32[651]{0:T(1024)S(4)} %plan.1.refs_0_, bf16[192,128,128]{2,1,0:T(8,128)(2,1)S(1)} %bitcast.8, s32[192,16,128]{2,1,0:T(8,128)S(1)} %bitcast.13, ...), custom_call_target="tpu_custom_call" | custom-call | flops 2684354560 | bytes 4194304 | tf_op jit(solution)/shard_map/item_terms/pallas_call | solution.py:313
  32.5 4.4 %collective-permute-start.9 = (bf16[512,128]{1,0:T(8,128)(2,1)S(1)}, bf16[512,128]{1,0:T(8,128)(2,1)S(1)}, u32[]{:S(2)}, u32[]{:S(2)}) collective-permute-start(bf16[512,128]{1,0:T(8,128)(2,1)S(1)} %get-tuple-element.29), channel_id=1, source_target_pairs={{0,2},{2,0},{4,6},{6,4},{8,10},{10,8},{12,14},{14,12},{1,3},{3,1},... | collective-permute-start | bytes 393224 | tf_op jit(solution)/shard_map/ppermute | solution.py:227
  36.9 1.7 %collective-permute-start.10 = (bf16[512,128]{1,0:T(8,128)(2,1)S(1)}, bf16[512,128]{1,0:T(8,128)(2,1)S(1)}, u32[]{:S(2)}, u32[]{:S(2)}) collective-permute-start(bf16[512,128]{1,0:T(8,128)(2,1)S(1)} %get-tuple-element.30), channel_id=1, source_target_pairs={{0,4},{2,6},{4,0},{6,2},{8,12},{10,14},{12,8},{14,10},{1,5},{3,7},... | collective-permute-start | bytes 393224 | tf_op jit(solution)/shard_map/ppermute | solution.py:227
  38.6 0.0 collective-permute-done.14
  38.6 0.0 collective-permute-start.11
  38.6 0.0 collective-permute-done.13
  38.6 0.0 collective-permute-done.12
  38.6 0.1 add_convert_fusion
  38.7 2.5 %collective-permute-start.15 = (bf16[512,128]{1,0:T(8,128)(2,1)S(1)}, bf16[512,128]{1,0:T(8,128)(2,1)S(1)}, u32[]{:S(2)}, u32[]{:S(2)}) collective-permute-start(bf16[512,128]{1,0:T(8,128)(2,1)S(1)} %add_convert_fusion), channel_id=1, source_target_pairs={{0,8},{2,10},{4,12},{6,14},{8,0},{10,2},{12,4},{14,6},{1,9},{3,11}... | collective-permute-start | bytes 393224 | tf_op jit(solution)/shard_map/ppermute | solution.py:227
  41.1 0.7 %constant_dynamic-slice_fusion = bf16[1024,128]{1,0:T(8,128)(2,1)} fusion(bf16[2048,128]{1,0:T(8,128)(2,1)S(1)} %get-tuple-element.25.refs_4_, s32[]{:T(128)S(6)} %select_n.3), kind=kLoop, calls=%fused_computation.1 | loop fusion | bytes 524292 | tf_op jit(solution)/shard_map/dynamic_slice | solution.py:327
  41.8 0.0 collective-permute-done.9.refs_1_
  41.8 4.3 %collective-permute-done.10.refs_2_ = bf16[512,128]{1,0:T(8,128)(2,1)S(1)} collective-permute-done((bf16[512,128]{1,0:T(8,128)(2,1)S(1)}, bf16[512,128]{1,0:T(8,128)(2,1)S(1)}, u32[]{:S(2)}, u32[]{:S(2)}) %collective-permute-start.10) | collective-permute-done | bytes 131104 | tf_op jit(solution)/shard_map/ppermute | solution.py:227
  46.1 1.1 %collective-permute-done.11.refs_3_ = bf16[512,128]{1,0:T(8,128)(2,1)S(1)} collective-permute-done((bf16[512,128]{1,0:T(8,128)(2,1)S(1)}, bf16[512,128]{1,0:T(8,128)(2,1)S(1)}, u32[]{:S(2)}, u32[]{:S(2)}) %collective-permute-start.11) | collective-permute-done | bytes 131104 | tf_op jit(solution)/shard_map/ppermute | solution.py:227
  47.2 0.0 collective-permute-done.15.refs_4_
  47.2 0.8 %finish.1 = bf16[512,128]{1,0:T(8,128)(2,1)} custom-call(bf16[512,128]{1,0:T(8,128)(2,1)S(1)} %copy-done.2, f32[512,128]{1,0:T(8,128)S(1)} %get-tuple-element.28.refs_0_, bf16[512,128]{1,0:T(8,128)(2,1)S(1)} %collective-permute-done.9.refs_1_, bf16[512,128]{1,0:T(8,128)(2,1)S(1)} %collective-permute-done.10.refs_2_, ...), custom_call_target="tpu_custom_call" | custom-call | tf_op jit(solution)/shard_map/finish/pallas_call | solution.py:334
  (6 shorter events, 0.0 us)
Async XLA Ops:
  0.6 15.2 %copy-start.2 = (bf16[512,128]{1,0:T(8,128)(2,1)S(1)}, bf16[512,128]{1,0:T(8,128)(2,1)}, u32[]{:S(2)}) copy-start(bf16[512,128]{1,0:T(8,128)(2,1)} %items.1) | copy-start | bytes 393220
  0.6 15.1 %copy-start.3 = (bf16[1024,128]{1,0:T(8,128)(2,1)S(1)}, bf16[1024,128]{1,0:T(8,128)(2,1)}, u32[]{:S(2)}) copy-start(bf16[1024,128]{1,0:T(8,128)(2,1)} %refs_8_.1) | copy-start | bytes 786436
  0.7 8.4 %copy-start.4 = (s32[1,1,192]{2,1,0:T(1,128)S(1)}, s32[1,1,192]{2,1,0:T(1,128)}, u32[]{:S(2)}) copy-start(s32[1,1,192]{2,1,0:T(1,128)} %param.11) | copy-start | bytes 2308
  0.7 8.4 %copy-start.5 = (s32[1,1,192]{2,1,0:T(1,128)S(1)}, s32[1,1,192]{2,1,0:T(1,128)}, u32[]{:S(2)}) copy-start(s32[1,1,192]{2,1,0:T(1,128)} %param.12) | copy-start | bytes 2308
  0.7 15.1 %copy-start = (bf16[1,1,192,128,128]{4,3,2,1,0:T(8,128)(2,1)S(1)}, bf16[1,1,192,128,128]{4,3,2,1,0:T(8,128)(2,1)}, u32[]{:S(2)}) copy-start(bf16[1,1,192,128,128]{4,3,2,1,0:T(8,128)(2,1)} %param.9) | copy-start | bytes 18874372
  0.7 15.1 %copy-start.1 = (s32[1,1,192,16,128]{4,3,2,1,0:T(8,128)S(1)}, s32[1,1,192,16,128]{4,3,2,1,0:T(8,128)}, u32[]{:S(2)}) copy-start(s32[1,1,192,16,128]{4,3,2,1,0:T(8,128)} %param.10) | copy-start | bytes 4718596
  0.7 10.7 %collective-permute-start = (bf16[512,128]{1,0:T(8,128)(2,1)}, bf16[512,128]{1,0:T(8,128)(2,1)S(1)}, u32[]{:S(2)}, u32[]{:S(2)}) collective-permute-start(bf16[512,128]{1,0:T(8,128)(2,1)} %items.1), channel_id=1, source_target_pairs={{0,8},{2,10},{4,12},{6,14},{8,0},{10,2},{12,4},{14,6},{1,9},{3,11}... | collective-permute-start | bytes 393224 | tf_op jit(solution)/shard_map/ppermute | solution.py:227
  4.8 8.8 %collective-permute-start.3 = (bf16[512,128]{1,0:T(8,128)(2,1)}, bf16[512,128]{1,0:T(8,128)(2,1)S(1)}, u32[]{:S(2)}, u32[]{:S(2)}) collective-permute-start(bf16[512,128]{1,0:T(8,128)(2,1)} %items.1), channel_id=1, source_target_pairs={{0,2},{2,0},{4,6},{6,4},{8,10},{10,8},{12,14},{14,12},{1,3},{3,1},... | collective-permute-start | bytes 393224 | tf_op jit(solution)/shard_map/ppermute | solution.py:227
  6.3 8.9 %collective-permute-start.4 = (bf16[512,128]{1,0:T(8,128)(2,1)}, bf16[512,128]{1,0:T(8,128)(2,1)S(1)}, u32[]{:S(2)}, u32[]{:S(2)}) collective-permute-start(bf16[512,128]{1,0:T(8,128)(2,1)} %items.1), channel_id=1, source_target_pairs={{0,4},{2,6},{4,0},{6,2},{8,12},{10,14},{12,8},{14,10},{1,5},{3,7},... | collective-permute-start | bytes 393224 | tf_op jit(solution)/shard_map/ppermute | solution.py:227
  7.9 7.9 %collective-permute-start.5 = (bf16[512,128]{1,0:T(8,128)(2,1)}, bf16[512,128]{1,0:T(8,128)(2,1)S(1)}, u32[]{:S(2)}, u32[]{:S(2)}) collective-permute-start(bf16[512,128]{1,0:T(8,128)(2,1)} %items.1), channel_id=1, source_target_pairs={{0,6},{2,4},{4,2},{6,0},{8,14},{10,12},{12,10},{14,8},{1,7},{3,5},... | collective-permute-start | bytes 393224 | tf_op jit(solution)/shard_map/ppermute | solution.py:227
  8.3 7.5 %collective-permute-start.6 = (bf16[1024,128]{1,0:T(8,128)(2,1)}, bf16[1024,128]{1,0:T(8,128)(2,1)S(1)}, u32[]{:S(2)}, u32[]{:S(2)}) collective-permute-start(bf16[1024,128]{1,0:T(8,128)(2,1)} %refs_8_.1), channel_id=1, source_target_pairs={{0,1},{1,0},{2,3},{3,2},{4,5},{5,4},{6,7},{7,6},{8,9},{9,8},{10,11... | collective-permute-start | bytes 786440 | tf_op jit(solution)/shard_map/ppermute | solution.py:230
  11.4 7.1 %collective-permute-start.1 = (bf16[512,128]{1,0:T(8,128)(2,1)S(1)}, bf16[512,128]{1,0:T(8,128)(2,1)S(1)}, u32[]{:S(2)}, u32[]{:S(2)}) collective-permute-start(bf16[512,128]{1,0:T(8,128)(2,1)S(1)} %collective-permute-done.refs_7_), channel_id=1, source_target_pairs={{0,2},{2,0},{4,6},{6,4},{8,10},{10,8},{12,14},{14,12},{1,3},{3,1},... | collective-permute-start | bytes 393224 | tf_op jit(solution)/shard_map/ppermute | solution.py:227
  13.6 6.3 %collective-permute-start.2 = (bf16[512,128]{1,0:T(8,128)(2,1)S(1)}, bf16[512,128]{1,0:T(8,128)(2,1)S(1)}, u32[]{:S(2)}, u32[]{:S(2)}) collective-permute-start(bf16[512,128]{1,0:T(8,128)(2,1)S(1)} %collective-permute-done.refs_7_), channel_id=1, source_target_pairs={{0,4},{2,6},{4,0},{6,2},{8,12},{10,14},{12,8},{14,10},{1,5},{3,7},... | collective-permute-start | bytes 393224 | tf_op jit(solution)/shard_map/ppermute | solution.py:227
  15.2 6.7 %collective-permute-start.7 = (bf16[512,128]{1,0:T(8,128)(2,1)S(1)}, bf16[512,128]{1,0:T(8,128)(2,1)S(1)}, u32[]{:S(2)}, u32[]{:S(2)}) collective-permute-start(bf16[512,128]{1,0:T(8,128)(2,1)S(1)} %collective-permute-done.refs_7_), channel_id=1, source_target_pairs={{0,6},{2,4},{4,2},{6,0},{8,14},{10,12},{12,10},{14,8},{1,7},{3,5},... | collective-permute-start | bytes 393224 | tf_op jit(solution)/shard_map/ppermute | solution.py:227
  22.5 2.0 %collective-permute-start.8 = (bf16[2048,128]{1,0:T(8,128)(2,1)S(1)}, bf16[2048,128]{1,0:T(8,128)(2,1)S(1)}, u32[]{:S(2)}, u32[]{:S(2)}) collective-permute-start(bf16[2048,128]{1,0:T(8,128)(2,1)S(1)} %get-tuple-element.24.refs_5_), channel_id=1, source_target_pairs={{0,1},{1,0},{2,3},{3,2},{4,5},{5,4},{6,7},{7,6},{8,9},{9,8},{10,11... | collective-permute-start | bytes 1572872 | tf_op jit(solution)/shard_map/ppermute | solution.py:230
  25.9 12.7 %collective-permute-start.14 = (bf16[512,128]{1,0:T(8,128)(2,1)S(1)}, bf16[512,128]{1,0:T(8,128)(2,1)S(1)}, u32[]{:S(2)}, u32[]{:S(2)}) collective-permute-start(bf16[512,128]{1,0:T(8,128)(2,1)S(1)} %get-tuple-element.35), channel_id=1, source_target_pairs={{0,6},{2,4},{4,2},{6,0},{8,14},{10,12},{12,10},{14,8},{1,7},{3,5},... | collective-permute-start | bytes 393224 | tf_op jit(solution)/shard_map/ppermute | solution.py:227
  30.5 8.0 %collective-permute-start.13 = (bf16[512,128]{1,0:T(8,128)(2,1)S(1)}, bf16[512,128]{1,0:T(8,128)(2,1)S(1)}, u32[]{:S(2)}, u32[]{:S(2)}) collective-permute-start(bf16[512,128]{1,0:T(8,128)(2,1)S(1)} %get-tuple-element.34), channel_id=1, source_target_pairs={{0,4},{2,6},{4,0},{6,2},{8,12},{10,14},{12,8},{14,10},{1,5},{3,7},... | collective-permute-start | bytes 393224 | tf_op jit(solution)/shard_map/ppermute | solution.py:227
  31.1 7.5 %collective-permute-start.12 = (bf16[512,128]{1,0:T(8,128)(2,1)S(1)}, bf16[512,128]{1,0:T(8,128)(2,1)S(1)}, u32[]{:S(2)}, u32[]{:S(2)}) collective-permute-start(bf16[512,128]{1,0:T(8,128)(2,1)S(1)} %get-tuple-element.33), channel_id=1, source_target_pairs={{0,2},{2,0},{4,6},{6,4},{8,10},{10,8},{12,14},{14,12},{1,3},{3,1},... | collective-permute-start | bytes 393224 | tf_op jit(solution)/shard_map/ppermute | solution.py:227
  32.5 9.3 %collective-permute-start.9 = (bf16[512,128]{1,0:T(8,128)(2,1)S(1)}, bf16[512,128]{1,0:T(8,128)(2,1)S(1)}, u32[]{:S(2)}, u32[]{:S(2)}) collective-permute-start(bf16[512,128]{1,0:T(8,128)(2,1)S(1)} %get-tuple-element.29), channel_id=1, source_target_pairs={{0,2},{2,0},{4,6},{6,4},{8,10},{10,8},{12,14},{14,12},{1,3},{3,1},... | collective-permute-start | bytes 393224 | tf_op jit(solution)/shard_map/ppermute | solution.py:227
  36.9 9.2 %collective-permute-start.10 = (bf16[512,128]{1,0:T(8,128)(2,1)S(1)}, bf16[512,128]{1,0:T(8,128)(2,1)S(1)}, u32[]{:S(2)}, u32[]{:S(2)}) collective-permute-start(bf16[512,128]{1,0:T(8,128)(2,1)S(1)} %get-tuple-element.30), channel_id=1, source_target_pairs={{0,4},{2,6},{4,0},{6,2},{8,12},{10,14},{12,8},{14,10},{1,5},{3,7},... | collective-permute-start | bytes 393224 | tf_op jit(solution)/shard_map/ppermute | solution.py:227
  38.6 8.7 %collective-permute-start.11 = (bf16[512,128]{1,0:T(8,128)(2,1)S(1)}, bf16[512,128]{1,0:T(8,128)(2,1)S(1)}, u32[]{:S(2)}, u32[]{:S(2)}) collective-permute-start(bf16[512,128]{1,0:T(8,128)(2,1)S(1)} %get-tuple-element.31), channel_id=1, source_target_pairs={{0,6},{2,4},{4,2},{6,0},{8,14},{10,12},{12,10},{14,8},{1,7},{3,5},... | collective-permute-start | bytes 393224 | tf_op jit(solution)/shard_map/ppermute | solution.py:227
  38.7 8.6 %collective-permute-start.15 = (bf16[512,128]{1,0:T(8,128)(2,1)S(1)}, bf16[512,128]{1,0:T(8,128)(2,1)S(1)}, u32[]{:S(2)}, u32[]{:S(2)}) collective-permute-start(bf16[512,128]{1,0:T(8,128)(2,1)S(1)} %add_convert_fusion), channel_id=1, source_target_pairs={{0,8},{2,10},{4,12},{6,14},{8,0},{10,2},{12,4},{14,6},{1,9},{3,11}... | collective-permute-start | bytes 393224 | tf_op jit(solution)/shard_map/ppermute | solution.py:227
